TPU v7x, 32 devices: a whole 2x2x4 slice. The times are simulated.
32 devices in a mesh: grp: 2 (over y), wide: 4 (over z), lev: 2 (over x), sub: 2 (over core).
Axes of the slice: x: 2, y: 2, z: 4, core: 2. Of those that a mesh axis runs over, the one named last changes fastest.
Arguments:
- air_state: float32 [8, 32, 512], P('lev', ('grp', 'sub'), 'wide'), parts along dimension 1, may hold values from -6 to 6
- diffusivity: float32 [32, 512], P(('grp', 'sub'), 'wide'), parts along dimension 0, may hold values from 0.25 to 2
- absorber: float32 [7, 8, 32, 512], P(None, 'lev', ('grp', 'sub'), 'wide'), parts along dimension 2, may hold values from 0 to 1
- thickness: float32 [8, 32, 512], P('lev', ('grp', 'sub'), 'wide'), parts along dimension 1, may hold values from 0.5 to 1.5
- cos_zenith: float32 [32, 512], P(('grp', 'sub'), 'wide'), parts along dimension 0, may hold values from 0.1 to 1
- sunlit: int32 [32, 512], P(('grp', 'sub'), 'wide'), parts along dimension 0, may hold values from 0 to 1, as said below
- absorb_coef: float32 [7, 224], replicated, may hold values from 0.0005 to 0.2
- solar_weight: float32 [224], replicated, may hold values from 0.2 to 2
Outputs:
- heating_rate: float32 [8, 32, 512], P('lev', ('grp', 'sub'), 'wide'), parts along dimension 1
- new_state: float32 [8, 32, 512], P('lev', ('grp', 'sub'), 'wide'), parts along dimension 1
There are 2 independent parts, one for each index of `grp`. A program takes and returns all parts, laid end to end along the dimension named above; an argument that names none is the same for every part. Nothing has to cross between parts.
Inputs may be any that keep to these rules, and one draw needn't show every extreme that they name: For the columns of one device's block of 8 x 128 grid points and the block at the same y position half of the x devices away, the two blocks together hold at most 1024 sunlit columns; some block is wholly sunlit and some pair reaches 1024.
All inputs are finite; a program needn't handle non-finite values.
Results may differ from a plain program's by a relative error of at most 0.0003.
Values sent between devices are 32-bit elements; how exact they have to be, the bound alone decides.
No kernel may reach another device: no remote copies, remote signals or barrier semaphores. Data moves between devices by JAX's collectives and lax.ppermute only.
A program may use at most 64 MiB of HBM per device.

v0:
```python
import math

import jax
import jax.numpy as jnp
import numpy as np
from jax import lax
from jax.experimental import pallas as pl
from jax.experimental.pallas import tpu as pltpu
from jax.sharding import PartitionSpec as P

time_step = 0.004
points = 4
log2e = 1.4426950408889634
gll_weights = (1.0 / 6.0, 5.0 / 6.0, 5.0 / 6.0, 1.0 / 6.0)
mass_points = (1.0 / 3.0, 5.0 / 6.0, 5.0 / 6.0, 1.0 / 3.0)


def derivative_table():
    root_five = math.sqrt(5.0)
    outer_big = (5.0 + 5.0 * root_five) / 4.0
    outer_small = (5.0 * root_five - 5.0) / 4.0
    inner_big = (1.0 + root_five) / 4.0
    inner_mid = root_five / 2.0
    inner_small = (root_five - 1.0) / 4.0
    return np.array(
        [
            [-3.0, outer_big, -outer_small, 0.5],
            [-inner_big, 0.0, inner_mid, -inner_small],
            [inner_small, -inner_mid, 0.0, inner_big],
            [-0.5, outer_small, -outer_big, 3.0],
        ]
    )


table = derivative_table()


def by_node(node, values):
    out = jnp.full(node.shape, values[3], jnp.float32)
    for i in (2, 1, 0):
        out = jnp.where(node == i, jnp.float32(values[i]), out)
    return out


class Stencil:
    def __init__(self, rows, width):
        self.shape = (rows, width)
        self.row = lax.broadcasted_iota(jnp.int32, (rows, width), 0)
        self.lane = lax.broadcasted_iota(jnp.int32, (rows, width), 1)
        node_y, node_x = self.row % points, self.lane % points
        self.weight_x = by_node(node_x, gll_weights)
        self.weight_y = by_node(node_y, gll_weights)
        self.coefs = {}
        for name, matrix in (("d", table), ("t", table.T)):
            for axis, node in ((0, node_y), (1, node_x)):
                terms = []
                for step in range(-3, 4):
                    values = [
                        matrix[i, i + step] if 0 <= i + step < points else 0.0
                        for i in range(points)
                    ]
                    terms.append(by_node(node, values))
                self.coefs[name, axis] = terms
        self.inv_mass = by_node(node_y, [1.0 / m for m in mass_points]) * by_node(
            node_x, [1.0 / m for m in mass_points]
        )
        self.first_x = (node_x == 0).astype(jnp.float32)
        self.last_x = (node_x == points - 1).astype(jnp.float32)
        self.first_y = (node_y == 0).astype(jnp.float32)
        self.last_y = (node_y == points - 1).astype(jnp.float32)

    def apply(self, name, axis, field):
        size = self.shape[axis]
        out = None
        for step, coef in zip(range(-3, 4), self.coefs[name, axis]):
            if step == 0 and name == "d":
                moved = field
            else:
                moved = pltpu.roll(field, (-step) % size, field.ndim - 2 + axis)
            term = coef * moved
            out = term if out is None else out + term
        return out

    def shifted(self, field, axis, step):
        size = self.shape[axis]
        index = self.row if axis == 0 else self.lane
        moved = pltpu.roll(field, step % size, field.ndim - 2 + axis)
        if axis == 0:
            other = jnp.concatenate([moved[:, 1:], moved[:, :1]], axis=1)
        else:
            other = jnp.concatenate([moved[:, :, 1:], moved[:, :, :1]], axis=2)
        edge = 0 if step == 1 else size - 1
        return jnp.where(index == edge, other, moved)

    def tendency(self, field, kappa):
        flux_x = kappa * self.weight_x * self.apply("d", 1, field)
        flux_y = kappa * self.weight_y * self.apply("d", 0, field)
        r = -self.weight_y * self.apply("t", 1, flux_x) - self.weight_x * self.apply("t", 0, flux_y)
        r = (
            r
            + self.first_x * self.shifted(r, 1, 1)
            + self.last_x * self.shifted(r, 1, -1)
        )
        r = (
            r
            + self.first_y * self.shifted(r, 0, 1)
            + self.last_y * self.shifted(r, 0, -1)
        )
        return r * self.inv_mass


def split(value, pieces):
    out = []
    for _ in range(pieces):
        high = value.astype(jnp.bfloat16)
        out.append(high)
        value = value - high.astype(jnp.float32)
    return out


def fetch_kernel(*refs):
    air, diffusivity, absorber, thickness, zenith, lit, coef, weight = refs[:8]
    amount, state, absorber_out, thickness_out, zenith_out, lit_out, coef_out, weight_out, sems = refs[8:]
    levels = air.shape[0]
    copies = [
        pltpu.make_async_copy(absorber, absorber_out, sems.at[0]),
        pltpu.make_async_copy(air, state.at[pl.ds(0, levels)], sems.at[1]),
        pltpu.make_async_copy(diffusivity, state.at[levels], sems.at[2]),
        pltpu.make_async_copy(zenith, zenith_out, sems.at[3]),
        pltpu.make_async_copy(coef, coef_out, sems.at[4]),
        pltpu.make_async_copy(weight, weight_out, sems.at[5]),
        pltpu.make_async_copy(thickness, thickness_out, sems.at[6]),
        pltpu.make_async_copy(lit, lit_out, sems.at[7]),
    ]
    for copy in copies:
        copy.start()
    for copy in copies:
        copy.wait()
    for s in range(absorber_out.shape[0]):
        total = absorber_out[s, 0]
        for k in range(1, levels):
            total = total + absorber_out[s, k]
        amount[s] = total


def amount_rows(totals, scale, depth, ones):
    value = jnp.concatenate([t * scale for t in totals], axis=0)
    hi, mid, lo = (p.astype(jnp.float32) for p in split(value, 3))
    rest = depth - 4 * value.shape[0]
    index = lax.broadcasted_iota(jnp.int32, (rest, value.shape[1]), 0)
    tail = jnp.where(index < ones, 1.0, 0.0)
    return jnp.concatenate([hi, mid, lo, hi, tail], axis=0).astype(jnp.bfloat16)


def layers_kernel(absorber, zenith, coef, weight, left, drops, spread):
    species, levels, rows, width = absorber.shape
    terms = coef.shape[1]
    group = species * rows
    depth = left.shape[1]
    c_pieces = split(coef[...], 2)
    w_pieces = split(jnp.log2(weight[...]), 3)
    lane = lax.broadcasted_iota(jnp.int32, (rows, depth), 1)
    row = lax.broadcasted_iota(jnp.int32, (rows, depth), 0)
    ones_at = 4 * group
    stack = jnp.concatenate([p.astype(jnp.float32) for p in c_pieces + w_pieces], axis=0)
    count = stack.shape[0]
    pick_row = lax.broadcasted_iota(jnp.int32, (count, depth), 0)
    pick_lane = lax.broadcasted_iota(jnp.int32, (count, depth), 1)
    kind = pick_lane // group
    wanted = jnp.where(kind == 3, species, 0) + (pick_lane % group) // rows
    wanted = jnp.where(kind >= 4, 2 * species + pick_lane - ones_at, wanted)
    pick = (pick_row == wanted).astype(jnp.bfloat16)
    spread[...] = lax.dot_general(
        stack.astype(jnp.bfloat16),
        pick,
        (((0,), (0,)), ((), ())),
        preferred_element_type=jnp.float32,
    )
    mask = ((lane % rows == row) | (lane >= ones_at)).astype(jnp.float32)
    for g in range(0, terms, 2):
        pair = [jnp.broadcast_to(spread[pl.ds(g + i, 1), :], (rows, depth)) * mask for i in (0, 1)]
        left[pl.ds(g * rows, 2 * rows), :] = jnp.concatenate(pair, axis=0).astype(jnp.bfloat16)

    scale = -log2e / zenith[...]
    totals = [jnp.zeros((rows, width), jnp.float32)] * species
    blocks = []
    for k in range(levels + 1):
        if k:
            totals = [totals[s] + absorber[s, k - 1] for s in range(species)]
        blocks.append(amount_rows(totals, scale, depth, 3))
    right = jnp.concatenate(blocks, axis=1)
    chunk = 448
    for start in range(0, terms * rows, chunk):
        out = jnp.exp2(
            jnp.dot(left[pl.ds(start, chunk), :], right, preferred_element_type=jnp.float32)
        )
        for k in range(levels):
            drop = out[:, k * width : (k + 1) * width] - out[:, (k + 1) * width : (k + 2) * width]
            drops[k, pl.ds(start, chunk), :] = drop


def radiate_kernel(left, drops, upper, zenith, lit, thickness, heat):
    levels, rows, width = heat.shape
    depth = left.shape[1]
    species = upper.shape[0]
    zen = zenith[...]
    below = lax.axis_index("lev") > 0
    totals = [jnp.where(below, upper[s], 0.0) for s in range(species)]
    right = amount_rows(totals, -log2e / zen, depth, 0)
    chunk = 448
    sums = [jnp.zeros((rows, width), jnp.float32) for _ in range(levels)]
    for start in range(0, left.shape[0], chunk):
        above = jnp.exp2(
            jnp.dot(left[pl.ds(start, chunk), :], right, preferred_element_type=jnp.float32)
        )
        for k in range(levels):
            absorbed = above * drops[k, pl.ds(start, chunk), :]
            sums[k] = sums[k] + jnp.sum(absorbed.reshape(chunk // rows, rows, width), axis=0)
    lit_zenith = jnp.where(lit[...] == 1, zen, 0.0)
    for k in range(levels):
        heat[k] = lit_zenith * sums[k] / thickness[k]


def strips(levels):
    return [(i, tile) for i in range(2 * levels + 1) for tile in range(2)]


def pack_kernel(own_state, own_heat, other_state, other_heat, even_first, odd_first):
    levels = own_heat.shape[0]
    rows, width = own_heat.shape[1:]
    edge = 2 * points
    slots = width // edge
    lane = lax.broadcasted_iota(jnp.int32, (rows, width), 1)
    tiles = [(jnp.zeros((rows, width), jnp.float32), jnp.zeros((rows, width), jnp.float32)) for _ in range(own_first_tiles(levels, slots))]
    for j, (i, tile) in enumerate(strips(levels)):
        state, heat = (own_state, own_heat) if tile == 0 else (other_state, other_heat)
        value = state[i] if i <= levels else heat[i - levels - 1]
        n, slot = divmod(j, slots)
        here = lane // edge == slot
        low = pltpu.roll(value, (slot * edge) % width, 1)
        high = pltpu.roll(value, (slot * edge + edge) % width, 1)
        tiles[n] = (jnp.where(here, low, tiles[n][0]), jnp.where(here, high, tiles[n][1]))
    even = lax.axis_index("wide") % 2 == 0
    for n, (low, high) in enumerate(tiles):
        odd_first[n] = jnp.where(even, low, high)
        even_first[n] = jnp.where(even, high, low)


def own_first_tiles(levels, slots):
    return -(-(2 * (2 * levels + 1)) // slots)


def step_kernel(own_state, own_heat, other_state, other_heat, got_two, got_one, heat_out, out):
    levels = own_heat.shape[0]
    rows, width = own_heat.shape[1:]
    edge = 2 * points
    slots = width // edge
    stencil = Stencil(rows, width)
    even = lax.axis_index("wide") % 2 == 0
    lane = stencil.lane
    halo = {}
    for j, (i, tile) in enumerate(strips(levels)):
        n, slot = divmod(j, slots)
        from_left = jnp.where(even, got_one[n], got_two[n])
        from_right = jnp.where(even, got_two[n], got_one[n])
        after = pltpu.roll(from_right, (-slot * edge) % width, 1)
        before = pltpu.roll(from_left, (-slot * edge - edge) % width, 1)
        value = jnp.where(lane < edge, after, jnp.where(lane >= width - edge, before, 0.0))
        halo[i, tile] = value

    def ring(i):
        parts = []
        for tile in range(2):
            state, heat = (own_state, own_heat) if tile == 0 else (other_state, other_heat)
            main = state[i] if i <= levels else heat[i - levels - 1]
            parts.append(jnp.stack([main, halo[i, tile]], axis=0))
        return jnp.stack(parts, axis=0)

    air = jnp.stack([ring(i) for i in range(levels)], axis=0)
    kappa = ring(levels)[None]
    heat = jnp.stack([ring(levels + 1 + i) for i in range(levels)], axis=0)
    first = air + time_step * (stencil.tendency(air, kappa) + heat)
    new = 0.5 * (air + first + time_step * (stencil.tendency(first, kappa) + heat))
    for k in range(levels):
        out[k] = new[k, 0, 0]
        heat_out[k] = own_heat[k]


def swap(value, axis, pairs):
    route = [(a, b) for a, b in pairs] + [(b, a) for a, b in pairs]
    return lax.ppermute(value, axis, route)


def shards(
    air_state, diffusivity, absorber, thickness, cos_zenith, sunlit, absorb_coef, solar_weight
):
    levels, rows, width = air_state.shape
    terms = absorb_coef.shape[1]
    tile = lambda n: jax.ShapeDtypeStruct((n, rows, width), jnp.float32)
    big = pltpu.CompilerParams(vmem_limit_bytes=32 * 1024 * 1024)
    weight = solar_weight[None]
    args = (air_state, diffusivity, absorber, thickness, cos_zenith, sunlit, absorb_coef, weight)
    args = tuple(pltpu.with_memory_space_constraint(x, pltpu.HBM) for x in args)
    same = lambda x: jax.ShapeDtypeStruct(x.shape, x.dtype)
    amount, own_state, absorber, thickness, cos_zenith, sunlit, absorb_coef, weight = pl.pallas_call(
        fetch_kernel,
        out_shape=(tile(absorber.shape[0]), tile(levels + 1)) + tuple(same(x) for x in args[2:]),
        in_specs=[pl.BlockSpec(memory_space=pltpu.HBM)] * len(args),
        scratch_shapes=[pltpu.SemaphoreType.DMA((len(args),))],
        compiler_params=pltpu.CompilerParams(vmem_limit_bytes=32 * 1024 * 1024),
        name="fetch",
    )(*args)
    size = lax.axis_size("lev")
    lev = lax.axis_index("lev")
    upper = None
    for step in range(1, size):
        moved = lax.ppermute(amount, "lev", [(i, (i + step) % size) for i in range(size)])
        if size > 2:
            moved = jnp.where(lev >= step, moved, 0.0)
        upper = moved if upper is None else upper + moved
    if upper is None:
        upper = jnp.zeros_like(amount)
    other_state = swap(own_state, "sub", [(0, 1)])
    left, drops = pl.pallas_call(
        layers_kernel,
        out_shape=(
            jax.ShapeDtypeStruct((terms * rows, 256), jnp.bfloat16),
            jax.ShapeDtypeStruct((levels, terms * rows, width), jnp.float32),
        ),
        scratch_shapes=[pltpu.VMEM((terms, 256), jnp.float32)],
        compiler_params=big,
        name="layers",
    )(absorber, cos_zenith, absorb_coef, weight)
    own_heat = pl.pallas_call(
        radiate_kernel, out_shape=tile(levels), compiler_params=big, name="radiate"
    )(left, drops, upper, cos_zenith, sunlit, thickness)
    other_heat = swap(own_heat, "sub", [(0, 1)])
    tiles = own_first_tiles(levels, width // (2 * points))
    even_first, odd_first = pl.pallas_call(
        pack_kernel, out_shape=(tile(tiles), tile(tiles)), compiler_params=big, name="pack"
    )(own_state, own_heat, other_state, other_heat)
    wide = lax.axis_size("wide")
    got_two = swap(even_first, "wide", [(i, i + 1) for i in range(0, wide, 2)])
    got_one = swap(odd_first, "wide", [(i, (i + 1) % wide) for i in range(1, wide, 2)])
    heat, new_state = pl.pallas_call(
        step_kernel, out_shape=(tile(levels), tile(levels)), compiler_params=big, name="step"
    )(own_state, own_heat, other_state, other_heat, got_two, got_one)
    return (heat, new_state)


def solution(mesh):
    in_specs = (
        P("lev", ("grp", "sub"), "wide"),
        P(("grp", "sub"), "wide"),
        P(None, "lev", ("grp", "sub"), "wide"),
        P("lev", ("grp", "sub"), "wide"),
        P(("grp", "sub"), "wide"),
        P(("grp", "sub"), "wide"),
        P(),
        P(),
    )
    out_specs = (P("lev", ("grp", "sub"), "wide"), P("lev", ("grp", "sub"), "wide"))
    return jax.shard_map(shards, mesh=mesh, in_specs=in_specs, out_specs=out_specs, check_vma=False)
```

profile of v0, /device:TPU:0, one launch (start us, length us, event | category | flops | bytes accessed | tf_op | source)
XLA Modules:
  0.0 17.5 jit_solution(17647925427983764821)
XLA Ops:
  0.6 1.0 %fetch.1 = (f32[7,8,128]{2,1,0:T(8,128)S(1)}, f32[5,8,128]{2,1,0:T(8,128)S(1)}, f32[7,4,8,128]{3,2,1,0:T(8,128)S(1)}, f32[4,8,128]{2,1,0:T(8,128)S(1)}, f32[8,12...) custom-call(f32[4,8,128]{2,1,0:T(8,128)} %refs_0_.1, f32[8,128]{1,0:T(8,128)} %refs_1_.1, ...), custom_call_target="tpu_custom_call" | custom-call | tf_op jit(solution)/shard_map/fetch/pallas_call | solution.py:305
  1.6 3.0 %collective-permute-start = (f32[7,8,128]{2,1,0:T(8,128)S(1)}, f32[7,8,128]{2,1,0:T(8,128)S(1)}, u32[]{:S(2)}, u32[]{:S(2)}) collective-permute-start(f32[7,8,128]{2,1,0:T(8,128)S(1)} %get-tuple-element.21), channel_id=1, source_target_pairs={{0,2},{2,0},{1,3},{3,1},{4,6},{6,4},{5,7},{7,5},{8,10},{10,8},{9,1... | collective-permute-start | bytes 86024 | tf_op jit(solution)/shard_map/ppermute | solution.py:317
  4.6 0.0 collective-permute-start.1
  4.6 1.1 %layers.1 = (bf16[1792,256]{1,0:T(8,128)(2,1)S(1)}, f32[4,1792,128]{2,1,0:T(8,128)S(1)}) custom-call(f32[7,4,8,128]{3,2,1,0:T(8,128)S(1)} %get-tuple-element.15.absorber, f32[8,128]{1,0:T(8,128)S(1)} %get-tuple-element.16.zenith, f32[7,224]{1,0:T(8,128)S(1)} %get-tuple-element.17.coef, f32[1,224]{1,0:T(1,128)S(1)} %get-tuple-element.18.weight), custom_call_target="tpu_custom_call" | custom-call | tf_op jit(solution)/shard_map/layers/pallas_call | solution.py:324
  5.7 0.7 %collective-permute-done.upper = f32[7,8,128]{2,1,0:T(8,128)S(1)} collective-permute-done((f32[7,8,128]{2,1,0:T(8,128)S(1)}, f32[7,8,128]{2,1,0:T(8,128)S(1)}, u32[]{:S(2)}, u32[]{:S(2)}) %collective-permute-start) | collective-permute-done | bytes 28704 | tf_op jit(solution)/shard_map/ppermute | solution.py:317
  6.5 0.5 %radiate.1.own_heat = f32[4,8,128]{2,1,0:T(8,128)S(1)} custom-call(bf16[1792,256]{1,0:T(8,128)(2,1)S(1)} %get-tuple-element.19.left, f32[4,1792,128]{2,1,0:T(8,128)S(1)} %get-tuple-element.20.drops, f32[7,8,128]{2,1,0:T(8,128)S(1)} %collective-permute-done.upper, f32[8,128]{1,0:T(8,128)S(1)} %get-tuple-element.16.zenith, ...), custom_call_target="tpu_custom_call" | custom-call | tf_op jit(solution)/shard_map/radiate/pallas_call | solution.py:334
  7.0 0.1 collective-permute-start.2
  7.1 0.0 collective-permute-done.1.other_state
  7.1 1.2 %collective-permute-done.2.other_heat = f32[4,8,128]{2,1,0:T(8,128)S(1)} collective-permute-done((f32[4,8,128]{2,1,0:T(8,128)S(1)}, f32[4,8,128]{2,1,0:T(8,128)S(1)}, u32[]{:S(2)}, u32[]{:S(2)}) %collective-permute-start.2) | collective-permute-done | bytes 16416 | tf_op jit(solution)/shard_map/ppermute | solution.py:291
  8.3 0.1 pack.1
  8.4 2.2 %collective-permute-start.3 = (f32[2,8,128]{2,1,0:T(8,128)S(1)}, f32[2,8,128]{2,1,0:T(8,128)S(1)}, u32[]{:S(2)}, u32[]{:S(2)}) collective-permute-start(f32[2,8,128]{2,1,0:T(8,128)S(1)} %get-tuple-element.24), channel_id=1, source_target_pairs={{0,4},{8,12},{4,0},{12,8},{1,5},{9,13},{5,1},{13,9},{2,6},{10,14},... | collective-permute-start | bytes 24584 | tf_op jit(solution)/shard_map/ppermute | solution.py:291
  10.6 2.5 %collective-permute-start.4 = (f32[2,8,128]{2,1,0:T(8,128)S(1)}, f32[2,8,128]{2,1,0:T(8,128)S(1)}, u32[]{:S(2)}, u32[]{:S(2)}) collective-permute-start(f32[2,8,128]{2,1,0:T(8,128)S(1)} %get-tuple-element.25), channel_id=1, source_target_pairs={{4,8},{12,0},{8,4},{0,12},{5,9},{13,1},{9,5},{1,13},{6,10},{14,2},... | collective-permute-start | bytes 24584 | tf_op jit(solution)/shard_map/ppermute | solution.py:291
  13.0 0.0 collective-permute-done.3.got_two
  13.0 3.0 %collective-permute-done.4.got_one = f32[2,8,128]{2,1,0:T(8,128)S(1)} collective-permute-done((f32[2,8,128]{2,1,0:T(8,128)S(1)}, f32[2,8,128]{2,1,0:T(8,128)S(1)}, u32[]{:S(2)}, u32[]{:S(2)}) %collective-permute-start.4) | collective-permute-done | bytes 8224 | tf_op jit(solution)/shard_map/ppermute | solution.py:291
  16.0 1.5 %step.1 = (f32[4,8,128]{2,1,0:T(8,128)}, f32[4,8,128]{2,1,0:T(8,128)}) custom-call(f32[5,8,128]{2,1,0:T(8,128)S(1)} %get-tuple-element.14.own_state, f32[4,8,128]{2,1,0:T(8,128)S(1)} %radiate.1.own_heat, f32[5,8,128]{2,1,0:T(8,128)S(1)} %collective-permute-done.1.other_state, f32[4,8,128]{2,1,0:T(8,128)S(1)} %collective-permute-done.2.other_heat, ...), custom_call_target="tpu_custom_call" | custom-call | tf_op jit(solution)/shard_map/step/pallas_call | solution.py:345
Async XLA Ops:
  1.6 4.9 %collective-permute-start = (f32[7,8,128]{2,1,0:T(8,128)S(1)}, f32[7,8,128]{2,1,0:T(8,128)S(1)}, u32[]{:S(2)}, u32[]{:S(2)}) collective-permute-start(f32[7,8,128]{2,1,0:T(8,128)S(1)} %get-tuple-element.21), channel_id=1, source_target_pairs={{0,2},{2,0},{1,3},{3,1},{4,6},{6,4},{5,7},{7,5},{8,10},{10,8},{9,1... | collective-permute-start | bytes 86024 | tf_op jit(solution)/shard_map/ppermute | solution.py:317
  4.6 2.5 %collective-permute-start.1 = (f32[5,8,128]{2,1,0:T(8,128)S(1)}, f32[5,8,128]{2,1,0:T(8,128)S(1)}, u32[]{:S(2)}, u32[]{:S(2)}) collective-permute-start(f32[5,8,128]{2,1,0:T(8,128)S(1)} %get-tuple-element.14.own_state), channel_id=1, source_target_pairs={{0,1},{1,0},{2,3},{3,2},{4,5},{5,4},{6,7},{7,6},{8,9},{9,8},{10,11... | collective-permute-start | bytes 61448 | tf_op jit(solution)/shard_map/ppermute | solution.py:291
  7.0 1.2 %collective-permute-start.2 = (f32[4,8,128]{2,1,0:T(8,128)S(1)}, f32[4,8,128]{2,1,0:T(8,128)S(1)}, u32[]{:S(2)}, u32[]{:S(2)}) collective-permute-start(f32[4,8,128]{2,1,0:T(8,128)S(1)} %radiate.1.own_heat), channel_id=1, source_target_pairs={{0,1},{1,0},{2,3},{3,2},{4,5},{5,4},{6,7},{7,6},{8,9},{9,8},{10,11... | collective-permute-start | bytes 49160 | tf_op jit(solution)/shard_map/ppermute | solution.py:291
  8.4 4.6 %collective-permute-start.3 = (f32[2,8,128]{2,1,0:T(8,128)S(1)}, f32[2,8,128]{2,1,0:T(8,128)S(1)}, u32[]{:S(2)}, u32[]{:S(2)}) collective-permute-start(f32[2,8,128]{2,1,0:T(8,128)S(1)} %get-tuple-element.24), channel_id=1, source_target_pairs={{0,4},{8,12},{4,0},{12,8},{1,5},{9,13},{5,1},{13,9},{2,6},{10,14},... | collective-permute-start | bytes 24584 | tf_op jit(solution)/shard_map/ppermute | solution.py:291
  10.6 5.4 %collective-permute-start.4 = (f32[2,8,128]{2,1,0:T(8,128)S(1)}, f32[2,8,128]{2,1,0:T(8,128)S(1)}, u32[]{:S(2)}, u32[]{:S(2)}) collective-permute-start(f32[2,8,128]{2,1,0:T(8,128)S(1)} %get-tuple-element.25), channel_id=1, source_target_pairs={{4,8},{12,0},{8,4},{0,12},{5,9},{13,1},{9,5},{1,13},{6,10},{14,2},... | collective-permute-start | bytes 24584 | tf_op jit(solution)/shard_map/ppermute | solution.py:291
where the time goes:
time: 17.7 us; the launch traced here: 17.5 us
  starting transfers between devices  7.72 us (44%)
  waiting for transfers between devices  4.88 us (28%)
  Pallas kernels  4.26 us (24%)
  between operations  0.68 us (4%)
    ppermute x4, starting transfers between devices, swap(): return lax.ppermute(value, axis, route)  4.71 us
    ppermute x4, waiting for transfers between devices, swap(): return lax.ppermute(value, axis, route)  4.14 us
    ppermute x1, starting transfers between devices, shards(): lax.ppermute(amount, 'lev', [(i, (i + step) % size) for i in range(size)])  3 us
    pallas_call x1, Pallas kernels, shards(): pl.pallas_call(step_kernel, out_shape=(tile(levels), tile(levels)), compi...  1.53 us
    pallas_call x1, Pallas kernels, shards(): pl.pallas_call(layers_kernel, out_shape=(jax.ShapeDtypeStruct((terms * ro...  1.1 us
    pallas_call x1, Pallas kernels, shards(): pl.pallas_call(fetch_kernel, out_shape=(tile(absorber.shape[0]), tile(lev...  0.99 us
    ppermute x1, waiting for transfers between devices, shards(): lax.ppermute(amount, 'lev', [(i, (i + step) % size) for i in range(size)])  0.74 us
    pallas_call x1, Pallas kernels, shards(): pl.pallas_call(radiate_kernel, out_shape=tile(levels), compiler_params=bi...  0.54 us
  transfers between devices with their start and end apart: 5, of which 3 were waited for; matrix products, arithmetic and copies ran while one was open for 0% of the time, Pallas kernels for 9%

commit v1 on v0

--- a/solution.py
+++ b/solution.py
@@ -225,7 +225,7 @@
     return [(i, tile) for i in range(2 * levels + 1) for tile in range(2)]
 
 
-def pack_kernel(own_state, own_heat, other_state, other_heat, even_first, odd_first):
+def pack_kernel(own_state, own_heat, other_state, other_heat, packed):
     levels = own_heat.shape[0]
     rows, width = own_heat.shape[1:]
     edge = 2 * points
@@ -240,29 +240,34 @@
         low = pltpu.roll(value, (slot * edge) % width, 1)
         high = pltpu.roll(value, (slot * edge + edge) % width, 1)
         tiles[n] = (jnp.where(here, low, tiles[n][0]), jnp.where(here, high, tiles[n][1]))
-    even = lax.axis_index("wide") % 2 == 0
+    wide = packed.shape[0]
+    me = lax.axis_index("wide")
+    packed[...] = jnp.zeros(packed.shape, jnp.float32)
+    before, after = lax.rem(me + wide - 1, wide), lax.rem(me + 1, wide)
     for n, (low, high) in enumerate(tiles):
-        odd_first[n] = jnp.where(even, low, high)
-        even_first[n] = jnp.where(even, high, low)
+        packed[before, n] = low
+        packed[after, n] = high
 
 
 def own_first_tiles(levels, slots):
     return -(-(2 * (2 * levels + 1)) // slots)
 
 
-def step_kernel(own_state, own_heat, other_state, other_heat, got_two, got_one, heat_out, out):
+def step_kernel(own_state, own_heat, other_state, other_heat, got, heat_out, out):
     levels = own_heat.shape[0]
     rows, width = own_heat.shape[1:]
     edge = 2 * points
     slots = width // edge
     stencil = Stencil(rows, width)
-    even = lax.axis_index("wide") % 2 == 0
+    wide = got.shape[0]
+    me = lax.axis_index("wide")
+    left_mate, right_mate = lax.rem(me + wide - 1, wide), lax.rem(me + 1, wide)
     lane = stencil.lane
     halo = {}
     for j, (i, tile) in enumerate(strips(levels)):
         n, slot = divmod(j, slots)
-        from_left = jnp.where(even, got_one[n], got_two[n])
-        from_right = jnp.where(even, got_two[n], got_one[n])
+        from_left = got[left_mate, n]
+        from_right = got[right_mate, n]
         after = pltpu.roll(from_right, (-slot * edge) % width, 1)
         before = pltpu.roll(from_left, (-slot * edge - edge) % width, 1)
         value = jnp.where(lane < edge, after, jnp.where(lane >= width - edge, before, 0.0))
@@ -336,15 +341,17 @@
     )(left, drops, upper, cos_zenith, sunlit, thickness)
     other_heat = swap(own_heat, "sub", [(0, 1)])
     tiles = own_first_tiles(levels, width // (2 * points))
-    even_first, odd_first = pl.pallas_call(
-        pack_kernel, out_shape=(tile(tiles), tile(tiles)), compiler_params=big, name="pack"
+    wide = lax.axis_size("wide")
+    packed = pl.pallas_call(
+        pack_kernel,
+        out_shape=jax.ShapeDtypeStruct((wide, tiles, rows, width), jnp.float32),
+        compiler_params=big,
+        name="pack",
     )(own_state, own_heat, other_state, other_heat)
-    wide = lax.axis_size("wide")
-    got_two = swap(even_first, "wide", [(i, i + 1) for i in range(0, wide, 2)])
-    got_one = swap(odd_first, "wide", [(i, (i + 1) % wide) for i in range(1, wide, 2)])
+    got = lax.all_to_all(packed, "wide", 0, 0)
     heat, new_state = pl.pallas_call(
         step_kernel, out_shape=(tile(levels), tile(levels)), compiler_params=big, name="step"
-    )(own_state, own_heat, other_state, other_heat, got_two, got_one)
+    )(own_state, own_heat, other_state, other_heat, got)
     return (heat, new_state)
 
 

time: 17.7 us -> 21 us (1.19)
  blocking collectives: 0 us -> 10.9 us
  starting transfers between devices: 7.72 us -> 3.08 us
  waiting for transfers between devices: 4.88 us -> 1.91 us
    all_to_all x0 -> x1, blocking collectives: none -> 10.9 us  [shards(): got = lax.all_to_all(packed, 'wide', 0, 0)]
    ppermute x4 -> x2, starting transfers between devices: 4.71 us -> 0.07 us  [swap(): return lax.ppermute(value, axis, route)]
    ppermute x4 -> x2, waiting for transfers between devices: 4.14 us -> 1.16 us  [swap(): return lax.ppermute(value, axis, route)]
  transfers between devices with their start and end apart: 5 -> 3, of which waited for: 3 -> 2; matrix products, arithmetic and copies ran while one was open for 0% -> 0% of each run, Pallas kernels for 9% -> 8%
where the time goes in v1:
time: 21 us; the launch traced here: 20.8 us
  blocking collectives  10.9 us (52%)
  Pallas kernels  4.26 us (20%)
  starting transfers between devices  3.08 us (15%)
  waiting for transfers between devices  1.91 us (9%)
  between operations  0.68 us (3%)
    all_to_all x1, blocking collectives, shards(): got = lax.all_to_all(packed, 'wide', 0, 0)  10.9 us
    ppermute x1, starting transfers between devices, shards(): lax.ppermute(amount, 'lev', [(i, (i + step) % size) for i in range(size)])  3 us
    pallas_call x1, Pallas kernels, shards(): pl.pallas_call(step_kernel, out_shape=(tile(levels), tile(levels)), compi...  1.53 us
    ppermute x2, waiting for transfers between devices, swap(): return lax.ppermute(value, axis, route)  1.16 us
    pallas_call x1, Pallas kernels, shards(): pl.pallas_call(layers_kernel, out_shape=(jax.ShapeDtypeStruct((terms * ro...  1.1 us
    pallas_call x1, Pallas kernels, shards(): pl.pallas_call(fetch_kernel, out_shape=(tile(absorber.shape[0]), tile(lev...  0.99 us
    ppermute x1, waiting for transfers between devices, shards(): lax.ppermute(amount, 'lev', [(i, (i + step) % size) for i in range(size)])  0.74 us
    pallas_call x1, Pallas kernels, shards(): pl.pallas_call(radiate_kernel, out_shape=tile(levels), compiler_params=bi...  0.54 us
  transfers between devices with their start and end apart: 3, of which 2 were waited for; matrix products, arithmetic and copies ran while one was open for 0% of the time, Pallas kernels for 8%

profile of v1, /device:TPU:0, one launch (start us, length us, event | category | flops | bytes accessed | tf_op | source)
XLA Modules:
  0.0 20.8 jit_solution(15953646397086517044)
XLA Ops:
  0.6 1.0 %fetch.1 = (f32[7,8,128]{2,1,0:T(8,128)S(1)}, f32[5,8,128]{2,1,0:T(8,128)S(1)}, f32[7,4,8,128]{3,2,1,0:T(8,128)S(1)}, f32[4,8,128]{2,1,0:T(8,128)S(1)}, f32[8,12...) custom-call(f32[4,8,128]{2,1,0:T(8,128)} %refs_0_.1, f32[8,128]{1,0:T(8,128)} %refs_1_.1, ...), custom_call_target="tpu_custom_call" | custom-call | tf_op jit(solution)/shard_map/fetch/pallas_call | solution.py:310
  1.6 3.0 %collective-permute-start = (f32[7,8,128]{2,1,0:T(8,128)S(1)}, f32[7,8,128]{2,1,0:T(8,128)S(1)}, u32[]{:S(2)}, u32[]{:S(2)}) collective-permute-start(f32[7,8,128]{2,1,0:T(8,128)S(1)} %get-tuple-element.19), channel_id=1, source_target_pairs={{0,2},{2,0},{1,3},{3,1},{4,6},{6,4},{5,7},{7,5},{8,10},{10,8},{9,1... | collective-permute-start | bytes 86024 | tf_op jit(solution)/shard_map/ppermute | solution.py:322
  4.6 0.0 collective-permute-start.1
  4.6 1.1 %layers.1 = (bf16[1792,256]{1,0:T(8,128)(2,1)S(1)}, f32[4,1792,128]{2,1,0:T(8,128)S(1)}) custom-call(f32[7,4,8,128]{3,2,1,0:T(8,128)S(1)} %get-tuple-element.13.absorber, f32[8,128]{1,0:T(8,128)S(1)} %get-tuple-element.14.zenith, f32[7,224]{1,0:T(8,128)S(1)} %get-tuple-element.15.coef, f32[1,224]{1,0:T(1,128)S(1)} %get-tuple-element.16.weight), custom_call_target="tpu_custom_call" | custom-call | tf_op jit(solution)/shard_map/layers/pallas_call | solution.py:329
  5.7 0.7 %collective-permute-done.upper = f32[7,8,128]{2,1,0:T(8,128)S(1)} collective-permute-done((f32[7,8,128]{2,1,0:T(8,128)S(1)}, f32[7,8,128]{2,1,0:T(8,128)S(1)}, u32[]{:S(2)}, u32[]{:S(2)}) %collective-permute-start) | collective-permute-done | bytes 28704 | tf_op jit(solution)/shard_map/ppermute | solution.py:322
  6.5 0.5 %radiate.1.own_heat = f32[4,8,128]{2,1,0:T(8,128)S(1)} custom-call(bf16[1792,256]{1,0:T(8,128)(2,1)S(1)} %get-tuple-element.17.left, f32[4,1792,128]{2,1,0:T(8,128)S(1)} %get-tuple-element.18.drops, f32[7,8,128]{2,1,0:T(8,128)S(1)} %collective-permute-done.upper, f32[8,128]{1,0:T(8,128)S(1)} %get-tuple-element.14.zenith, ...), custom_call_target="tpu_custom_call" | custom-call | tf_op jit(solution)/shard_map/radiate/pallas_call | solution.py:339
  7.0 0.1 collective-permute-start.2
  7.1 0.0 collective-permute-done.1.other_state
  7.1 1.2 %collective-permute-done.2.other_heat = f32[4,8,128]{2,1,0:T(8,128)S(1)} collective-permute-done((f32[4,8,128]{2,1,0:T(8,128)S(1)}, f32[4,8,128]{2,1,0:T(8,128)S(1)}, u32[]{:S(2)}, u32[]{:S(2)}) %collective-permute-start.2) | collective-permute-done | bytes 16416 | tf_op jit(solution)/shard_map/ppermute | solution.py:296
  8.3 0.1 pack.1
  8.4 10.9 %all_to_all.5.got = f32[4,2,8,128]{3,2,1,0:T(8,128)S(1)} all-to-all(f32[4,2,8,128]{3,2,1,0:T(8,128)S(1)} %pack.1), channel_id=1, replica_groups=mesh['grp'=2,'wide'=4,'lev'=2,'sub'=2] {'wide'}, dimensions={0} | all-to-all | bytes 65536 | tf_op jit(solution)/shard_map/all_to_all | solution.py:351
  19.2 1.5 %step.1 = (f32[4,8,128]{2,1,0:T(8,128)}, f32[4,8,128]{2,1,0:T(8,128)}) custom-call(f32[5,8,128]{2,1,0:T(8,128)S(1)} %get-tuple-element.12.own_state, f32[4,8,128]{2,1,0:T(8,128)S(1)} %radiate.1.own_heat, f32[5,8,128]{2,1,0:T(8,128)S(1)} %collective-permute-done.1.other_state, f32[4,8,128]{2,1,0:T(8,128)S(1)} %collective-permute-done.2.other_heat, ...), custom_call_target="tpu_custom_call" | custom-call | tf_op jit(solution)/shard_map/step/pallas_call | solution.py:352
Async XLA Ops:
  1.6 4.9 %collective-permute-start = (f32[7,8,128]{2,1,0:T(8,128)S(1)}, f32[7,8,128]{2,1,0:T(8,128)S(1)}, u32[]{:S(2)}, u32[]{:S(2)}) collective-permute-start(f32[7,8,128]{2,1,0:T(8,128)S(1)} %get-tuple-element.19), channel_id=1, source_target_pairs={{0,2},{2,0},{1,3},{3,1},{4,6},{6,4},{5,7},{7,5},{8,10},{10,8},{9,1... | collective-permute-start | bytes 86024 | tf_op jit(solution)/shard_map/ppermute | solution.py:322
  4.6 2.5 %collective-permute-start.1 = (f32[5,8,128]{2,1,0:T(8,128)S(1)}, f32[5,8,128]{2,1,0:T(8,128)S(1)}, u32[]{:S(2)}, u32[]{:S(2)}) collective-permute-start(f32[5,8,128]{2,1,0:T(8,128)S(1)} %get-tuple-element.12.own_state), channel_id=1, source_target_pairs={{0,1},{1,0},{2,3},{3,2},{4,5},{5,4},{6,7},{7,6},{8,9},{9,8},{10,11... | collective-permute-start | bytes 61448 | tf_op jit(solution)/shard_map/ppermute | solution.py:296
  7.0 1.2 %collective-permute-start.2 = (f32[4,8,128]{2,1,0:T(8,128)S(1)}, f32[4,8,128]{2,1,0:T(8,128)S(1)}, u32[]{:S(2)}, u32[]{:S(2)}) collective-permute-start(f32[4,8,128]{2,1,0:T(8,128)S(1)} %radiate.1.own_heat), channel_id=1, source_target_pairs={{0,1},{1,0},{2,3},{3,2},{4,5},{5,4},{6,7},{7,6},{8,9},{9,8},{10,11... | collective-permute-start | bytes 49160 | tf_op jit(solution)/shard_map/ppermute | solution.py:296

commit v2 on v0

--- a/solution.py
+++ b/solution.py
@@ -48,65 +48,61 @@
         self.row = lax.broadcasted_iota(jnp.int32, (rows, width), 0)
         self.lane = lax.broadcasted_iota(jnp.int32, (rows, width), 1)
         node_y, node_x = self.row % points, self.lane % points
+        self.nodes = (node_y, node_x)
         self.weight_x = by_node(node_x, gll_weights)
         self.weight_y = by_node(node_y, gll_weights)
-        self.coefs = {}
-        for name, matrix in (("d", table), ("t", table.T)):
-            for axis, node in ((0, node_y), (1, node_x)):
-                terms = []
-                for step in range(-3, 4):
-                    values = [
-                        matrix[i, i + step] if 0 <= i + step < points else 0.0
-                        for i in range(points)
-                    ]
-                    terms.append(by_node(node, values))
-                self.coefs[name, axis] = terms
-        self.inv_mass = by_node(node_y, [1.0 / m for m in mass_points]) * by_node(
-            node_x, [1.0 / m for m in mass_points]
-        )
-        self.first_x = (node_x == 0).astype(jnp.float32)
-        self.last_x = (node_x == points - 1).astype(jnp.float32)
+        self.inv_mass_y = by_node(node_y, [1.0 / m for m in mass_points])
+        self.inv_mass = self.inv_mass_y * by_node(node_x, [1.0 / m for m in mass_points])
+        inner_first = (node_x == 0) & (self.lane > 0)
+        inner_last = (node_x == points - 1) & (self.lane < width - 1)
+        self.first_x = inner_first.astype(jnp.float32)
+        self.last_x = inner_last.astype(jnp.float32)
         self.first_y = (node_y == 0).astype(jnp.float32)
         self.last_y = (node_y == points - 1).astype(jnp.float32)
+        self.coefs = {}
+
+    def coef(self, name, axis):
+        if (name, axis) not in self.coefs:
+            matrix = table if name == "d" else table.T
+            self.coefs[name, axis] = [
+                by_node(
+                    self.nodes[axis],
+                    [matrix[i, i + step] if 0 <= i + step < points else 0.0 for i in range(points)],
+                )
+                for step in range(-3, 4)
+            ]
+        return self.coefs[name, axis]
 
     def apply(self, name, axis, field):
         size = self.shape[axis]
         out = None
-        for step, coef in zip(range(-3, 4), self.coefs[name, axis]):
-            if step == 0 and name == "d":
-                moved = field
-            else:
-                moved = pltpu.roll(field, (-step) % size, field.ndim - 2 + axis)
+        for step, coef in zip(range(-3, 4), self.coef(name, axis)):
+            moved = field if step == 0 else pltpu.roll(field, (-step) % size, field.ndim - 2 + axis)
             term = coef * moved
             out = term if out is None else out + term
         return out
 
-    def shifted(self, field, axis, step):
-        size = self.shape[axis]
-        index = self.row if axis == 0 else self.lane
-        moved = pltpu.roll(field, step % size, field.ndim - 2 + axis)
-        if axis == 0:
-            other = jnp.concatenate([moved[:, 1:], moved[:, :1]], axis=1)
-        else:
-            other = jnp.concatenate([moved[:, :, 1:], moved[:, :, :1]], axis=2)
-        edge = 0 if step == 1 else size - 1
-        return jnp.where(index == edge, other, moved)
-
-    def tendency(self, field, kappa):
+    def residual(self, field, kappa):
         flux_x = kappa * self.weight_x * self.apply("d", 1, field)
         flux_y = kappa * self.weight_y * self.apply("d", 0, field)
-        r = -self.weight_y * self.apply("t", 1, flux_x) - self.weight_x * self.apply("t", 0, flux_y)
-        r = (
-            r
-            + self.first_x * self.shifted(r, 1, 1)
-            + self.last_x * self.shifted(r, 1, -1)
+        part_x = self.weight_y * self.apply("t", 1, flux_x)
+        return -part_x - self.weight_x * self.apply("t", 0, flux_y)
+
+    def rows_joined(self, own, other):
+        rows = self.shape[0]
+        axis = own.ndim - 2
+        before = jnp.where(self.row == 0, pltpu.roll(other, 1, axis), pltpu.roll(own, 1, axis))
+        after = jnp.where(
+            self.row == rows - 1, pltpu.roll(other, rows - 1, axis), pltpu.roll(own, rows - 1, axis)
         )
-        r = (
-            r
-            + self.first_y * self.shifted(r, 0, 1)
-            + self.last_y * self.shifted(r, 0, -1)
-        )
-        return r * self.inv_mass
+        return own + self.first_y * before + self.last_y * after
+
+    def columns_joined(self, field):
+        width = self.shape[1]
+        axis = field.ndim - 1
+        before = pltpu.roll(field, 1, axis)
+        after = pltpu.roll(field, width - 1, axis)
+        return field + self.first_x * before + self.last_x * after
 
 
 def split(value, pieces):
@@ -221,69 +217,118 @@
         heat[k] = lit_zenith * sums[k] / thickness[k]
 
 
-def strips(levels):
-    return [(i, tile) for i in range(2 * levels + 1) for tile in range(2)]
-
-
-def pack_kernel(own_state, own_heat, other_state, other_heat, even_first, odd_first):
-    levels = own_heat.shape[0]
-    rows, width = own_heat.shape[1:]
-    edge = 2 * points
-    slots = width // edge
-    lane = lax.broadcasted_iota(jnp.int32, (rows, width), 1)
-    tiles = [(jnp.zeros((rows, width), jnp.float32), jnp.zeros((rows, width), jnp.float32)) for _ in range(own_first_tiles(levels, slots))]
-    for j, (i, tile) in enumerate(strips(levels)):
-        state, heat = (own_state, own_heat) if tile == 0 else (other_state, other_heat)
-        value = state[i] if i <= levels else heat[i - levels - 1]
-        n, slot = divmod(j, slots)
-        here = lane // edge == slot
-        low = pltpu.roll(value, (slot * edge) % width, 1)
-        high = pltpu.roll(value, (slot * edge + edge) % width, 1)
-        tiles[n] = (jnp.where(here, low, tiles[n][0]), jnp.where(here, high, tiles[n][1]))
-    even = lax.axis_index("wide") % 2 == 0
-    for n, (low, high) in enumerate(tiles):
-        odd_first[n] = jnp.where(even, low, high)
-        even_first[n] = jnp.where(even, high, low)
-
-
-def own_first_tiles(levels, slots):
-    return -(-(2 * (2 * levels + 1)) // slots)
-
-
-def step_kernel(own_state, own_heat, other_state, other_heat, got_two, got_one, heat_out, out):
-    levels = own_heat.shape[0]
-    rows, width = own_heat.shape[1:]
-    edge = 2 * points
-    slots = width // edge
+def to_edge_tile(stencil, edge, kind, columns):
+    width = stencil.shape[1]
+    half = width // 2
+    count = len(columns)
+    for j, value in enumerate(columns):
+        at = kind * count + j
+        low = pltpu.roll(value, at, 1) if at else value
+        high = pltpu.roll(value, (half + at + 1) % width, 1)
+        edge = jnp.where(stencil.lane == at, low, edge)
+        edge = jnp.where(stencil.lane == half + at, high, edge)
+    return edge
+
+
+def tiles_of(field):
+    return [field[l, t] for t in range(2) for l in range(field.shape[0])]
+
+
+def state_kernel(own_state, other_state, first_tend, second, edge_out, span_out):
+    levels = own_state.shape[0] - 1
+    rows, width = own_state.shape[1:]
     stencil = Stencil(rows, width)
-    even = lax.axis_index("wide") % 2 == 0
-    lane = stencil.lane
-    halo = {}
-    for j, (i, tile) in enumerate(strips(levels)):
-        n, slot = divmod(j, slots)
-        from_left = jnp.where(even, got_one[n], got_two[n])
-        from_right = jnp.where(even, got_two[n], got_one[n])
-        after = pltpu.roll(from_right, (-slot * edge) % width, 1)
-        before = pltpu.roll(from_left, (-slot * edge - edge) % width, 1)
-        value = jnp.where(lane < edge, after, jnp.where(lane >= width - edge, before, 0.0))
-        halo[i, tile] = value
-
-    def ring(i):
-        parts = []
-        for tile in range(2):
-            state, heat = (own_state, own_heat) if tile == 0 else (other_state, other_heat)
-            main = state[i] if i <= levels else heat[i - levels - 1]
-            parts.append(jnp.stack([main, halo[i, tile]], axis=0))
-        return jnp.stack(parts, axis=0)
-
-    air = jnp.stack([ring(i) for i in range(levels)], axis=0)
-    kappa = ring(levels)[None]
-    heat = jnp.stack([ring(levels + 1 + i) for i in range(levels)], axis=0)
-    first = air + time_step * (stencil.tendency(air, kappa) + heat)
-    new = 0.5 * (air + first + time_step * (stencil.tendency(first, kappa) + heat))
-    for k in range(levels):
-        out[k] = new[k, 0, 0]
-        heat_out[k] = own_heat[k]
+    air = jnp.stack([own_state[:levels], other_state[:levels]], axis=1)
+    kappa = jnp.stack([own_state[levels], other_state[levels]], axis=0)
+    r = stencil.residual(air, kappa)
+    joined = stencil.rows_joined(r, jnp.concatenate([r[:, 1:], r[:, :1]], axis=1))
+    tend = stencil.inv_mass * stencil.columns_joined(joined)
+    first_tend[...] = tend[:, 0]
+    second[...] = stencil.residual(tend, kappa)
+    left_side = stencil.lane < width // 2
+    node_x = stencil.nodes[1]
+    to_edge = jnp.where(left_side, by_node(node_x, table[:, 0]), by_node(node_x, table[:, 3]))
+    span = stencil.apply("t", 1, kappa * stencil.weight_x * to_edge)
+    in_edge = (stencil.lane < points) | (stencil.lane >= width - points)
+    span = jnp.where(in_edge, span, 0.0)
+    span_out[...] = span
+    edge = jnp.zeros((rows, width), jnp.float32)
+    edge = to_edge_tile(stencil, edge, 0, tiles_of(joined))
+    edge = to_edge_tile(stencil, edge, 2, [span[t] for t in range(2) for _ in range(levels)])
+    edge_out[...] = to_edge_tile(stencil, edge, 3, [kappa[t] for t in range(2) for _ in range(levels)])
+
+
+def edge_kernel(own_state, other_state, own_heat, other_heat, second, edge_in, joined_out, edge_out):
+    levels, rows, width = own_heat.shape
+    stencil = Stencil(rows, width)
+    heat = jnp.stack([own_heat[...], other_heat[...]], axis=1)
+    kappa = jnp.stack([own_state[levels], other_state[levels]], axis=0)
+    r = second[...] + stencil.residual(heat, kappa)
+    joined = stencil.rows_joined(r, jnp.concatenate([r[:, 1:], r[:, :1]], axis=1))
+    joined_out[...] = joined[:, 0]
+    edge_out[...] = to_edge_tile(stencil, edge_in[...], 1, tiles_of(joined))
+
+
+def base_kernel(own_state, own_heat, first_tend, joined, heat_out, base):
+    levels, rows, width = own_heat.shape
+    stencil = Stencil(rows, width)
+    heat = own_heat[...]
+    heat_out[...] = heat
+    second = stencil.inv_mass * stencil.columns_joined(joined[...])
+    base[...] = (
+        own_state[:levels]
+        + time_step * (first_tend[...] + heat)
+        + (0.5 * time_step * time_step) * second
+    )
+
+
+def step_kernel(base, span, own_edge, from_before, from_after, out):
+    levels, rows, width = base.shape
+    half = width // 2
+    count = 2 * levels
+    stencil = Stencil(rows, width)
+    row, lane = stencil.row, stencil.lane
+    own = own_edge[...]
+    mates = pltpu.roll(jnp.where(lane >= half, from_before[...], from_after[...]), half, 1)
+
+    def kind(tile, n):
+        return pltpu.roll(tile, (-n * count) % width, 1)
+
+    def along_y(kappa, value):
+        flux = stencil.weight_y * kappa * stencil.apply("d", 0, value)
+        return -gll_weights[0] * stencil.apply("t", 0, flux)
+
+    def joined(value):
+        other = jnp.where(
+            lane % count < levels,
+            pltpu.roll(value, width - levels, 1),
+            pltpu.roll(value, levels, 1),
+        )
+        return stencil.rows_joined(value, other)
+
+    edge_mass = stencil.inv_mass_y * (1.0 / mass_points[0])
+    change = edge_mass * mates
+    mates_change = edge_mass * own
+    in_mates = along_y(kind(mates, 3), mates_change) - stencil.weight_y * kind(mates, 2) * mates_change
+    add = kind(mates, 1) + joined(along_y(kind(own, 3), change) + in_mates)
+    at_left, at_right = lane == 0, lane == width - 1
+
+    def spread(tile, j):
+        low = jnp.broadcast_to(tile[:, j : j + 1], (rows, width))
+        high = jnp.broadcast_to(tile[:, half + j : half + j + 1], (rows, width))
+        return jnp.where(lane < half, low, high)
+
+    for l in range(levels):
+        changes = [spread(change, t * levels + l) for t in range(2)]
+        r = [-stencil.weight_y * span[t] * changes[t] for t in range(2)]
+        moved = stencil.columns_joined(stencil.rows_joined(r[0], r[1]))
+        edges = at_left | at_right
+        moved = moved + jnp.where(edges, spread(add, l), 0.0)
+        out[l] = (
+            base[l]
+            + time_step * jnp.where(edges, changes[0], 0.0)
+            + (0.5 * time_step * time_step) * stencil.inv_mass * moved
+        )
 
 
 def swap(value, axis, pairs):
@@ -335,16 +380,26 @@
         radiate_kernel, out_shape=tile(levels), compiler_params=big, name="radiate"
     )(left, drops, upper, cos_zenith, sunlit, thickness)
     other_heat = swap(own_heat, "sub", [(0, 1)])
-    tiles = own_first_tiles(levels, width // (2 * points))
-    even_first, odd_first = pl.pallas_call(
-        pack_kernel, out_shape=(tile(tiles), tile(tiles)), compiler_params=big, name="pack"
-    )(own_state, own_heat, other_state, other_heat)
+    pair = jax.ShapeDtypeStruct((levels, 2, rows, width), jnp.float32)
+    plane = jax.ShapeDtypeStruct((rows, width), jnp.float32)
+    first_tend, second, edge, span = pl.pallas_call(
+        state_kernel,
+        out_shape=(tile(levels), pair, plane, tile(2)),
+        compiler_params=big,
+        name="state",
+    )(own_state, other_state)
+    joined, edge = pl.pallas_call(
+        edge_kernel, out_shape=(tile(levels), plane), compiler_params=big, name="edges"
+    )(own_state, other_state, own_heat, other_heat, second, edge)
     wide = lax.axis_size("wide")
-    got_two = swap(even_first, "wide", [(i, i + 1) for i in range(0, wide, 2)])
-    got_one = swap(odd_first, "wide", [(i, (i + 1) % wide) for i in range(1, wide, 2)])
-    heat, new_state = pl.pallas_call(
-        step_kernel, out_shape=(tile(levels), tile(levels)), compiler_params=big, name="step"
-    )(own_state, own_heat, other_state, other_heat, got_two, got_one)
+    from_before = lax.ppermute(edge, "wide", [(i, (i + 1) % wide) for i in range(wide)])
+    from_after = lax.ppermute(edge, "wide", [((i + 1) % wide, i) for i in range(wide)])
+    heat, base = pl.pallas_call(
+        base_kernel, out_shape=(tile(levels), tile(levels)), compiler_params=big, name="base"
+    )(own_state, own_heat, first_tend, joined)
+    new_state = pl.pallas_call(
+        step_kernel, out_shape=tile(levels), compiler_params=big, name="step"
+    )(base, span, edge, from_before, from_after)
     return (heat, new_state)
 
 

time: 17.7 us -> 15.5 us (0.88)
  waiting for transfers between devices: 4.88 us -> 2.28 us
  Pallas kernels: 4.26 us -> 5.03 us
  starting transfers between devices: 7.72 us -> 7.32 us
    ppermute x4 -> x2, starting transfers between devices: 4.71 us -> 0.07 us  [swap(): return lax.ppermute(value, axis, route)]
    ppermute x0 -> x2, starting transfers between devices: none -> 4.24 us  [the longest x1 2.15 us: shards(): lax.ppermute(edge, 'wide', [(i, (i + 1) % wide) for i in range(wide)])]
    ppermute x4 -> x2, waiting for transfers between devices: 4.14 us -> 0.58 us  [swap(): return lax.ppermute(value, axis, route)]
    ppermute x0 -> x2, waiting for transfers between devices: none -> 0.95 us  [the longest x1 0.95 us: shards(): lax.ppermute(edge, 'wide', [(i, (i + 1) % wide) for i in range(wide)])]
    pallas_call x2 -> x4, Pallas kernels: 1.64 us -> 2.41 us  [the longest x1 0.92 us: shards(): pl.pallas_call(step_kernel, out_shape=tile(levels), compiler_params=big,...]
  transfers between devices with their start and end apart: 5 -> 5, of which waited for: 3 -> 3; matrix products, arithmetic and copies ran while one was open for 0% -> 0% of each run, Pallas kernels for 9% -> 18%
where the time goes in v2:
time: 15.5 us; the launch traced here: 15.3 us
  starting transfers between devices  7.32 us (47%)
  Pallas kernels  5.03 us (32%)
  waiting for transfers between devices  2.28 us (15%)
  between operations  0.69 us (4%)
    ppermute x1, starting transfers between devices, shards(): lax.ppermute(amount, 'lev', [(i, (i + step) % size) for i in range(size)])  3 us
    ppermute x1, starting transfers between devices, shards(): lax.ppermute(edge, 'wide', [(i, (i + 1) % wide) for i in range(wide)])  2.15 us
    ppermute x1, starting transfers between devices, shards(): lax.ppermute(edge, 'wide', [((i + 1) % wide, i) for i in range(wide)])  2.09 us
    pallas_call x1, Pallas kernels, shards(): pl.pallas_call(layers_kernel, out_shape=(jax.ShapeDtypeStruct((terms * ro...  1.1 us
    pallas_call x1, Pallas kernels, shards(): pl.pallas_call(fetch_kernel, out_shape=(tile(absorber.shape[0]), tile(lev...  0.99 us
    ppermute x1, waiting for transfers between devices, shards(): lax.ppermute(edge, 'wide', [(i, (i + 1) % wide) for i in range(wide)])  0.95 us
    pallas_call x1, Pallas kernels, shards(): pl.pallas_call(step_kernel, out_shape=tile(levels), compiler_params=big,...  0.92 us
    ppermute x1, waiting for transfers between devices, shards(): lax.ppermute(amount, 'lev', [(i, (i + step) % size) for i in range(size)])  0.74 us
  transfers between devices with their start and end apart: 5, of which 3 were waited for; matrix products, arithmetic and copies ran while one was open for 0% of the time, Pallas kernels for 18%

profile of v2, /device:TPU:0, one launch (start us, length us, event | category | flops | bytes accessed | tf_op | source)
XLA Modules:
  0.0 15.3 jit_solution(702667684710770221)
XLA Ops:
  0.6 1.0 %fetch.1 = (f32[7,8,128]{2,1,0:T(8,128)S(1)}, f32[5,8,128]{2,1,0:T(8,128)S(1)}, f32[7,4,8,128]{3,2,1,0:T(8,128)S(1)}, f32[4,8,128]{2,1,0:T(8,128)S(1)}, f32[8,12...) custom-call(f32[4,8,128]{2,1,0:T(8,128)} %refs_0_.1, f32[8,128]{1,0:T(8,128)} %refs_1_.1, ...), custom_call_target="tpu_custom_call" | custom-call | tf_op jit(solution)/shard_map/fetch/pallas_call | solution.py:350
  1.6 3.0 %collective-permute-start = (f32[7,8,128]{2,1,0:T(8,128)S(1)}, f32[7,8,128]{2,1,0:T(8,128)S(1)}, u32[]{:S(2)}, u32[]{:S(2)}) collective-permute-start(f32[7,8,128]{2,1,0:T(8,128)S(1)} %get-tuple-element.27), channel_id=1, source_target_pairs={{0,2},{2,0},{1,3},{3,1},{4,6},{6,4},{5,7},{7,5},{8,10},{10,8},{9,1... | collective-permute-start | bytes 86024 | tf_op jit(solution)/shard_map/ppermute | solution.py:362
  4.6 0.0 collective-permute-start.1
  4.6 1.1 %layers.1 = (bf16[1792,256]{1,0:T(8,128)(2,1)S(1)}, f32[4,1792,128]{2,1,0:T(8,128)S(1)}) custom-call(f32[7,4,8,128]{3,2,1,0:T(8,128)S(1)} %get-tuple-element.21.absorber, f32[8,128]{1,0:T(8,128)S(1)} %get-tuple-element.22.zenith, f32[7,224]{1,0:T(8,128)S(1)} %get-tuple-element.23.coef, f32[1,224]{1,0:T(1,128)S(1)} %get-tuple-element.24.weight), custom_call_target="tpu_custom_call" | custom-call | tf_op jit(solution)/shard_map/layers/pallas_call | solution.py:369
  5.7 0.7 %collective-permute-done.upper = f32[7,8,128]{2,1,0:T(8,128)S(1)} collective-permute-done((f32[7,8,128]{2,1,0:T(8,128)S(1)}, f32[7,8,128]{2,1,0:T(8,128)S(1)}, u32[]{:S(2)}, u32[]{:S(2)}) %collective-permute-start) | collective-permute-done | bytes 28704 | tf_op jit(solution)/shard_map/ppermute | solution.py:362
  6.5 0.5 %radiate.1.own_heat = f32[4,8,128]{2,1,0:T(8,128)S(1)} custom-call(bf16[1792,256]{1,0:T(8,128)(2,1)S(1)} %get-tuple-element.25.left, f32[4,1792,128]{2,1,0:T(8,128)S(1)} %get-tuple-element.26.drops, f32[7,8,128]{2,1,0:T(8,128)S(1)} %collective-permute-done.upper, f32[8,128]{1,0:T(8,128)S(1)} %get-tuple-element.22.zenith, ...), custom_call_target="tpu_custom_call" | custom-call | tf_op jit(solution)/shard_map/radiate/pallas_call | solution.py:379
  7.0 0.1 collective-permute-start.2
  7.1 0.0 collective-permute-done.1.other_state
  7.1 0.6 %state.1 = (f32[4,8,128]{2,1,0:T(8,128)S(1)}, f32[4,2,8,128]{3,2,1,0:T(8,128)S(1)}, f32[8,128]{1,0:T(8,128)S(1)}, f32[2,8,128]{2,1,0:T(8,128)S(1)}) custom-call(f32[5,8,128]{2,1,0:T(8,128)S(1)} %get-tuple-element.20.own_state, f32[5,8,128]{2,1,0:T(8,128)S(1)} %collective-permute-done.1.other_state), custom_call_target="tpu_custom_call" | custom-call | tf_op jit(solution)/shard_map/state/pallas_call | solution.py:385
  7.7 0.6 %collective-permute-done.2.other_heat = f32[4,8,128]{2,1,0:T(8,128)S(1)} collective-permute-done((f32[4,8,128]{2,1,0:T(8,128)S(1)}, f32[4,8,128]{2,1,0:T(8,128)S(1)}, u32[]{:S(2)}, u32[]{:S(2)}) %collective-permute-start.2) | collective-permute-done | bytes 16416 | tf_op jit(solution)/shard_map/ppermute | solution.py:336
  8.3 0.3 %edges.1 = (f32[4,8,128]{2,1,0:T(8,128)S(1)}, f32[8,128]{1,0:T(8,128)S(1)}) custom-call(f32[5,8,128]{2,1,0:T(8,128)S(1)} %get-tuple-element.20.own_state, f32[5,8,128]{2,1,0:T(8,128)S(1)} %collective-permute-done.1.other_state, f32[4,8,128]{2,1,0:T(8,128)S(1)} %radiate.1.own_heat, f32[4,8,128]{2,1,0:T(8,128)S(1)} %collective-permute-done.2.other_heat, ...), custom_call_target="tpu_custom_call" | custom-call | tf_op jit(solution)/shard_map/edges/pallas_call | solution.py:391
  8.6 2.2 %collective-permute-start.3 = (f32[8,128]{1,0:T(8,128)S(1)}, f32[8,128]{1,0:T(8,128)S(1)}, u32[]{:S(2)}, u32[]{:S(2)}) collective-permute-start(f32[8,128]{1,0:T(8,128)S(1)} %get-tuple-element.37.own_edge), channel_id=1, source_target_pairs={{0,4},{4,8},{8,12},{12,0},{1,5},{5,9},{9,13},{13,1},{2,6},{6,10},{... | collective-permute-start | bytes 12296 | tf_op jit(solution)/shard_map/ppermute | solution.py:395
  10.7 2.1 %collective-permute-start.4 = (f32[8,128]{1,0:T(8,128)S(1)}, f32[8,128]{1,0:T(8,128)S(1)}, u32[]{:S(2)}, u32[]{:S(2)}) collective-permute-start(f32[8,128]{1,0:T(8,128)S(1)} %get-tuple-element.37.own_edge), channel_id=1, source_target_pairs={{4,0},{8,4},{12,8},{0,12},{5,1},{9,5},{13,9},{1,13},{6,2},{10,6},{... | collective-permute-start | bytes 12296 | tf_op jit(solution)/shard_map/ppermute | solution.py:396
  12.8 0.6 %base.1 = (f32[4,8,128]{2,1,0:T(8,128)}, f32[4,8,128]{2,1,0:T(8,128)S(1)}) custom-call(f32[5,8,128]{2,1,0:T(8,128)S(1)} %get-tuple-element.20.own_state, f32[4,8,128]{2,1,0:T(8,128)S(1)} %radiate.1.own_heat, f32[4,8,128]{2,1,0:T(8,128)S(1)} %get-tuple-element.30.first_tend, f32[4,8,128]{2,1,0:T(8,128)S(1)} %get-tuple-element.33.joined), custom_call_target="tpu_custom_call" | custom-call | tf_op jit(solution)/shard_map/base/pallas_call | solution.py:397
  13.4 1.0 %collective-permute-done.3.from_before = f32[8,128]{1,0:T(8,128)S(1)} collective-permute-done((f32[8,128]{1,0:T(8,128)S(1)}, f32[8,128]{1,0:T(8,128)S(1)}, u32[]{:S(2)}, u32[]{:S(2)}) %collective-permute-start.3) | collective-permute-done | bytes 4128 | tf_op jit(solution)/shard_map/ppermute | solution.py:395
  14.4 0.0 collective-permute-done.4.from_after
  14.4 0.9 %step.1 = f32[4,8,128]{2,1,0:T(8,128)} custom-call(f32[4,8,128]{2,1,0:T(8,128)S(1)} %get-tuple-element.35.base, f32[2,8,128]{2,1,0:T(8,128)S(1)} %get-tuple-element.36.span, f32[8,128]{1,0:T(8,128)S(1)} %get-tuple-element.37.own_edge, f32[8,128]{1,0:T(8,128)S(1)} %collective-permute-done.3.from_before, f32[8,128]{1,0:T(8,128)S(1)} %collective-permute-done.4.from_after), custom_call_target="tpu_custom_call" | custom-call | tf_op jit(solution)/shard_map/step/pallas_call | solution.py:400
Async XLA Ops:
  1.6 4.9 %collective-permute-start = (f32[7,8,128]{2,1,0:T(8,128)S(1)}, f32[7,8,128]{2,1,0:T(8,128)S(1)}, u32[]{:S(2)}, u32[]{:S(2)}) collective-permute-start(f32[7,8,128]{2,1,0:T(8,128)S(1)} %get-tuple-element.27), channel_id=1, source_target_pairs={{0,2},{2,0},{1,3},{3,1},{4,6},{6,4},{5,7},{7,5},{8,10},{10,8},{9,1... | collective-permute-start | bytes 86024 | tf_op jit(solution)/shard_map/ppermute | solution.py:362
  4.6 2.5 %collective-permute-start.1 = (f32[5,8,128]{2,1,0:T(8,128)S(1)}, f32[5,8,128]{2,1,0:T(8,128)S(1)}, u32[]{:S(2)}, u32[]{:S(2)}) collective-permute-start(f32[5,8,128]{2,1,0:T(8,128)S(1)} %get-tuple-element.20.own_state), channel_id=1, source_target_pairs={{0,1},{1,0},{2,3},{3,2},{4,5},{5,4},{6,7},{7,6},{8,9},{9,8},{10,11... | collective-permute-start | bytes 61448 | tf_op jit(solution)/shard_map/ppermute | solution.py:336
  7.0 1.2 %collective-permute-start.2 = (f32[4,8,128]{2,1,0:T(8,128)S(1)}, f32[4,8,128]{2,1,0:T(8,128)S(1)}, u32[]{:S(2)}, u32[]{:S(2)}) collective-permute-start(f32[4,8,128]{2,1,0:T(8,128)S(1)} %radiate.1.own_heat), channel_id=1, source_target_pairs={{0,1},{1,0},{2,3},{3,2},{4,5},{5,4},{6,7},{7,6},{8,9},{9,8},{10,11... | collective-permute-start | bytes 49160 | tf_op jit(solution)/shard_map/ppermute | solution.py:336
  8.6 5.8 %collective-permute-start.3 = (f32[8,128]{1,0:T(8,128)S(1)}, f32[8,128]{1,0:T(8,128)S(1)}, u32[]{:S(2)}, u32[]{:S(2)}) collective-permute-start(f32[8,128]{1,0:T(8,128)S(1)} %get-tuple-element.37.own_edge), channel_id=1, source_target_pairs={{0,4},{4,8},{8,12},{12,0},{1,5},{5,9},{9,13},{13,1},{2,6},{6,10},{... | collective-permute-start | bytes 12296 | tf_op jit(solution)/shard_map/ppermute | solution.py:395
  10.7 3.7 %collective-permute-start.4 = (f32[8,128]{1,0:T(8,128)S(1)}, f32[8,128]{1,0:T(8,128)S(1)}, u32[]{:S(2)}, u32[]{:S(2)}) collective-permute-start(f32[8,128]{1,0:T(8,128)S(1)} %get-tuple-element.37.own_edge), channel_id=1, source_target_pairs={{4,0},{8,4},{12,8},{0,12},{5,1},{9,5},{13,9},{1,13},{6,2},{10,6},{... | collective-permute-start | bytes 12296 | tf_op jit(solution)/shard_map/ppermute | solution.py:396

commit v3 on v2

--- a/solution.py
+++ b/solution.py
@@ -10,6 +10,7 @@
 
 time_step = 0.004
 points = 4
+strip = 2 * points
 log2e = 1.4426950408889634
 gll_weights = (1.0 / 6.0, 5.0 / 6.0, 5.0 / 6.0, 1.0 / 6.0)
 mass_points = (1.0 / 3.0, 5.0 / 6.0, 5.0 / 6.0, 1.0 / 3.0)
@@ -103,6 +104,15 @@
         before = pltpu.roll(field, 1, axis)
         after = pltpu.roll(field, width - 1, axis)
         return field + self.first_x * before + self.last_x * after
+
+
+def to_strips(lane, start, values):
+    width = lane.shape[1]
+    for n, value in enumerate(values):
+        if value is not None:
+            moved = pltpu.roll(value, strip * n + points, 1)
+            start = jnp.where(lane // strip == n, moved, start)
+    return start
 
 
 def split(value, pieces):
@@ -195,135 +205,177 @@
             drops[k, pl.ds(start, chunk), :] = drop
 
 
-def radiate_kernel(left, drops, upper, zenith, lit, thickness, heat):
+def radiate_kernel(
+    left, drops, upper, upper_strips, packet, zenith, lit, thickness, second, kappa, fixed, heat, edge
+):
     levels, rows, width = heat.shape
     depth = left.shape[1]
     species = upper.shape[0]
+    stencil = Stencil(rows, width)
     zen = zenith[...]
     below = lax.axis_index("lev") > 0
     totals = [jnp.where(below, upper[s], 0.0) for s in range(species)]
-    right = amount_rows(totals, -log2e / zen, depth, 0)
+    raw = levels + 1
+    strip_totals = []
+    for s in range(species):
+        layer = packet[raw + s]
+        total = jnp.where(below, upper_strips[s], 0.0)
+        for k in range(levels):
+            total = total + pltpu.roll(layer, strip * (k + 1), 1)
+        strip_totals.append(total)
+    right = jnp.concatenate(
+        [
+            amount_rows(totals, -log2e / zen, depth, 0),
+            amount_rows(strip_totals, -log2e / packet[raw + species], depth, 3),
+        ],
+        axis=1,
+    )
     chunk = 448
-    sums = [jnp.zeros((rows, width), jnp.float32) for _ in range(levels)]
+    lanes = 4
+    zero = jnp.zeros((rows, width), jnp.float32)
+    sums = [[zero] * lanes for _ in range(levels)]
+    strip_sums = [zero] * lanes
     for start in range(0, left.shape[0], chunk):
         above = jnp.exp2(
             jnp.dot(left[pl.ds(start, chunk), :], right, preferred_element_type=jnp.float32)
         )
-        for k in range(levels):
-            absorbed = above * drops[k, pl.ds(start, chunk), :]
-            sums[k] = sums[k] + jnp.sum(absorbed.reshape(chunk // rows, rows, width), axis=0)
+        for i in range(chunk // rows):
+            at, n = i * rows, i % lanes
+            main = above[at : at + rows, :width]
+            strip_sums[n] = strip_sums[n] + above[at : at + rows, width:]
+            for k in range(levels):
+                sums[k][n] = sums[k][n] + main * drops[k, pl.ds(start + at, rows), :]
+
+    def total_of(parts):
+        return (parts[0] + parts[1]) + (parts[2] + parts[3])
+
     lit_zenith = jnp.where(lit[...] == 1, zen, 0.0)
+    heats = [lit_zenith * total_of(sums[k]) / thickness[k] for k in range(levels)]
     for k in range(levels):
-        heat[k] = lit_zenith * sums[k] / thickness[k]
-
-
-def to_edge_tile(stencil, edge, kind, columns):
-    width = stencil.shape[1]
-    half = width // 2
-    count = len(columns)
-    for j, value in enumerate(columns):
-        at = kind * count + j
-        low = pltpu.roll(value, at, 1) if at else value
-        high = pltpu.roll(value, (half + at + 1) % width, 1)
-        edge = jnp.where(stencil.lane == at, low, edge)
-        edge = jnp.where(stencil.lane == half + at, high, edge)
-    return edge
+        heat[k] = heats[k]
+    passed = total_of(strip_sums)
+    other = packet[raw + species + 1] * (passed - pltpu.roll(passed, width - strip, 1))
+    strips = to_strips(stencil.lane, zero, heats) + pltpu.roll(other, width // 2, 1)
+    r = second[...] + stencil.residual(strips, kappa[...])
+    joined = stencil.rows_joined(r, pltpu.roll(r, width // 2, 1))
+    node = stencil.lane % strip
+    edge[...] = jnp.where((node == points - 1) | (node == points), joined, fixed[...])
 
 
 def tiles_of(field):
-    return [field[l, t] for t in range(2) for l in range(field.shape[0])]
-
-
-def state_kernel(own_state, other_state, first_tend, second, edge_out, span_out):
+    gap = [None] * (8 - field.shape[0])
+    return [t for n in range(2) for t in [field[l, n] for l in range(field.shape[0])] + gap]
+
+
+def strips_kernel(own_state, absorber, zenith, lit, thickness, amount, packet, upper_strips):
+    species, levels, rows, width = absorber.shape
+    lane = lax.broadcasted_iota(jnp.int32, (rows, width), 1)
+    zero = jnp.zeros((rows, width), jnp.float32)
+    raw = levels + 1
+
+    def everywhere(value, count):
+        out = to_strips(lane, zero, [value])
+        step = strip
+        while step < strip * count:
+            out = out + pltpu.roll(out, step, 1)
+            step *= 2
+        return out
+
+    for s in range(species):
+        upper_strips[s] = everywhere(amount[s], 8)
+        packet[raw + s] = to_strips(lane, zero, [absorber[s, k] for k in range(levels)])
+    for i in range(raw):
+        packet[i] = own_state[i]
+    zen = zenith[...]
+    packet[raw + species] = everywhere(zen, 16)
+    lit_zenith = jnp.where(lit[...] == 1, zen, 0.0)
+    packet[raw + species + 1] = to_strips(
+        lane, zero, [lit_zenith / thickness[k] for k in range(levels)]
+    )
+
+
+def state_kernel(own_state, packet, first_tend, second, span_out, second_strips, kappa_strips, fixed, mine):
     levels = own_state.shape[0] - 1
     rows, width = own_state.shape[1:]
     stencil = Stencil(rows, width)
-    air = jnp.stack([own_state[:levels], other_state[:levels]], axis=1)
-    kappa = jnp.stack([own_state[levels], other_state[levels]], axis=0)
+    lane = stencil.lane
+    zero = jnp.zeros((rows, width), jnp.float32)
+    air = jnp.stack([own_state[:levels], packet[:levels]], axis=1)
+    kappa = jnp.stack([own_state[levels], packet[levels]], axis=0)
     r = stencil.residual(air, kappa)
     joined = stencil.rows_joined(r, jnp.concatenate([r[:, 1:], r[:, :1]], axis=1))
     tend = stencil.inv_mass * stencil.columns_joined(joined)
     first_tend[...] = tend[:, 0]
-    second[...] = stencil.residual(tend, kappa)
-    left_side = stencil.lane < width // 2
+    r = stencil.residual(tend, kappa)
+    second[...] = r
+    second_strips[...] = to_strips(lane, zero, tiles_of(r))
+    left_side = lane < width // 2
     node_x = stencil.nodes[1]
     to_edge = jnp.where(left_side, by_node(node_x, table[:, 0]), by_node(node_x, table[:, 3]))
     span = stencil.apply("t", 1, kappa * stencil.weight_x * to_edge)
-    in_edge = (stencil.lane < points) | (stencil.lane >= width - points)
+    in_edge = (lane < points) | (lane >= width - points)
     span = jnp.where(in_edge, span, 0.0)
     span_out[...] = span
-    edge = jnp.zeros((rows, width), jnp.float32)
-    edge = to_edge_tile(stencil, edge, 0, tiles_of(joined))
-    edge = to_edge_tile(stencil, edge, 2, [span[t] for t in range(2) for _ in range(levels)])
-    edge_out[...] = to_edge_tile(stencil, edge, 3, [kappa[t] for t in range(2) for _ in range(levels)])
-
-
-def edge_kernel(own_state, other_state, own_heat, other_heat, second, edge_in, joined_out, edge_out):
+    own = to_strips(lane, zero, tiles_of(joined))
+    by_level = lambda field: to_strips(
+        lane, zero, tiles_of(jnp.broadcast_to(field[None], (levels,) + field.shape))
+    )
+    kappa_edge = by_level(kappa)
+    kappa_strips[...] = kappa_edge
+    out = zero
+    node = lane % strip
+    for step, value in ((1, own), (2, by_level(span)), (3, kappa_edge)):
+        out = jnp.where(node == points - 1 - step, pltpu.roll(value, width - step, 1), out)
+        out = jnp.where(node == points + step, pltpu.roll(value, step, 1), out)
+    fixed[...] = out
+    change = stencil.inv_mass_y * (1.0 / mass_points[0]) * own
+    mine[0] = change
+    mine[1] = stencil.weight_y * stencil.apply("d", 0, change)
+
+
+def base_kernel(own_state, packet, own_heat, other_heat, first_tend, second, heat_out, base):
     levels, rows, width = own_heat.shape
     stencil = Stencil(rows, width)
-    heat = jnp.stack([own_heat[...], other_heat[...]], axis=1)
-    kappa = jnp.stack([own_state[levels], other_state[levels]], axis=0)
+    own = own_heat[...]
+    heat_out[...] = own
+    heat = jnp.stack([own, other_heat[...]], axis=1)
+    kappa = jnp.stack([own_state[levels], packet[levels]], axis=0)
     r = second[...] + stencil.residual(heat, kappa)
-    joined = stencil.rows_joined(r, jnp.concatenate([r[:, 1:], r[:, :1]], axis=1))
-    joined_out[...] = joined[:, 0]
-    edge_out[...] = to_edge_tile(stencil, edge_in[...], 1, tiles_of(joined))
-
-
-def base_kernel(own_state, own_heat, first_tend, joined, heat_out, base):
-    levels, rows, width = own_heat.shape
-    stencil = Stencil(rows, width)
-    heat = own_heat[...]
-    heat_out[...] = heat
-    second = stencil.inv_mass * stencil.columns_joined(joined[...])
+    joined = stencil.rows_joined(r[:, 0], r[:, 1])
     base[...] = (
         own_state[:levels]
-        + time_step * (first_tend[...] + heat)
-        + (0.5 * time_step * time_step) * second
-    )
-
-
-def step_kernel(base, span, own_edge, from_before, from_after, out):
+        + time_step * (first_tend[...] + own)
+        + (0.5 * time_step * time_step) * (stencil.inv_mass * stencil.columns_joined(joined))
+    )
+
+
+def step_kernel(base, span, kappa, mine, from_before, from_after, out):
     levels, rows, width = base.shape
     half = width // 2
-    count = 2 * levels
     stencil = Stencil(rows, width)
-    row, lane = stencil.row, stencil.lane
-    own = own_edge[...]
-    mates = pltpu.roll(jnp.where(lane >= half, from_before[...], from_after[...]), half, 1)
-
-    def kind(tile, n):
-        return pltpu.roll(tile, (-n * count) % width, 1)
-
-    def along_y(kappa, value):
-        flux = stencil.weight_y * kappa * stencil.apply("d", 0, value)
-        return -gll_weights[0] * stencil.apply("t", 0, flux)
-
-    def joined(value):
-        other = jnp.where(
-            lane % count < levels,
-            pltpu.roll(value, width - levels, 1),
-            pltpu.roll(value, levels, 1),
-        )
-        return stencil.rows_joined(value, other)
-
-    edge_mass = stencil.inv_mass_y * (1.0 / mass_points[0])
-    change = edge_mass * mates
-    mates_change = edge_mass * own
-    in_mates = along_y(kind(mates, 3), mates_change) - stencil.weight_y * kind(mates, 2) * mates_change
-    add = kind(mates, 1) + joined(along_y(kind(own, 3), change) + in_mates)
-    at_left, at_right = lane == 0, lane == width - 1
-
-    def spread(tile, j):
-        low = jnp.broadcast_to(tile[:, j : j + 1], (rows, width))
-        high = jnp.broadcast_to(tile[:, half + j : half + j + 1], (rows, width))
+    lane = stencil.lane
+    before, after = from_before[...], from_after[...]
+    at_first = lane % strip == points
+
+    def of_mates(step):
+        return jnp.where(at_first, pltpu.roll(before, step, 1), pltpu.roll(after, width - step, 1))
+
+    change = stencil.inv_mass_y * (1.0 / mass_points[0]) * of_mates(2)
+    flux = of_mates(4) * mine[1] + stencil.weight_y * kappa[...] * stencil.apply("d", 0, change)
+    r = -gll_weights[0] * stencil.apply("t", 0, flux) - stencil.weight_y * of_mates(3) * mine[0]
+    add = of_mates(1) + stencil.rows_joined(r, pltpu.roll(r, half, 1))
+    edges = (lane == 0) | (lane == width - 1)
+
+    def spread(tile, at):
+        low = jnp.broadcast_to(tile[:, at + points : at + points + 1], (rows, width))
+        high = jnp.broadcast_to(tile[:, at + points - 1 : at + points], (rows, width))
         return jnp.where(lane < half, low, high)
 
     for l in range(levels):
-        changes = [spread(change, t * levels + l) for t in range(2)]
+        changes = [spread(change, t * half + strip * l) for t in range(2)]
         r = [-stencil.weight_y * span[t] * changes[t] for t in range(2)]
         moved = stencil.columns_joined(stencil.rows_joined(r[0], r[1]))
-        edges = at_left | at_right
-        moved = moved + jnp.where(edges, spread(add, l), 0.0)
+        moved = moved + jnp.where(edges, spread(add, strip * l), 0.0)
         out[l] = (
             base[l]
             + time_step * jnp.where(edges, changes[0], 0.0)
@@ -355,17 +407,29 @@
         compiler_params=pltpu.CompilerParams(vmem_limit_bytes=32 * 1024 * 1024),
         name="fetch",
     )(*args)
+    species = absorber.shape[0]
+    packet, strip_amount = pl.pallas_call(
+        strips_kernel,
+        out_shape=(tile(levels + 1 + species + 2), tile(species)),
+        compiler_params=big,
+        name="strips",
+    )(own_state, absorber, cos_zenith, sunlit, thickness, amount)
     size = lax.axis_size("lev")
     lev = lax.axis_index("lev")
-    upper = None
+    upper = upper_strips = None
     for step in range(1, size):
-        moved = lax.ppermute(amount, "lev", [(i, (i + step) % size) for i in range(size)])
+        straight = [(i, (i + step) % size) for i in range(size)]
+        crossed = [(2 * i + c, 2 * j + 1 - c) for i, j in straight for c in range(2)]
+        moved = lax.ppermute(amount, "lev", straight)
+        moved_strips = lax.ppermute(strip_amount, ("lev", "sub"), crossed)
         if size > 2:
             moved = jnp.where(lev >= step, moved, 0.0)
+            moved_strips = jnp.where(lev >= step, moved_strips, 0.0)
         upper = moved if upper is None else upper + moved
+        upper_strips = moved_strips if upper_strips is None else upper_strips + moved_strips
     if upper is None:
-        upper = jnp.zeros_like(amount)
-    other_state = swap(own_state, "sub", [(0, 1)])
+        upper, upper_strips = jnp.zeros_like(amount), jnp.zeros_like(amount)
+    other_packet = swap(packet, "sub", [(0, 1)])
     left, drops = pl.pallas_call(
         layers_kernel,
         out_shape=(
@@ -376,30 +440,39 @@
         compiler_params=big,
         name="layers",
     )(absorber, cos_zenith, absorb_coef, weight)
-    own_heat = pl.pallas_call(
-        radiate_kernel, out_shape=tile(levels), compiler_params=big, name="radiate"
-    )(left, drops, upper, cos_zenith, sunlit, thickness)
-    other_heat = swap(own_heat, "sub", [(0, 1)])
     pair = jax.ShapeDtypeStruct((levels, 2, rows, width), jnp.float32)
     plane = jax.ShapeDtypeStruct((rows, width), jnp.float32)
-    first_tend, second, edge, span = pl.pallas_call(
+    first_tend, second, span, second_strips, kappa_strips, fixed, mine = pl.pallas_call(
         state_kernel,
-        out_shape=(tile(levels), pair, plane, tile(2)),
+        out_shape=(tile(levels), pair, tile(2), plane, plane, plane, tile(2)),
         compiler_params=big,
         name="state",
-    )(own_state, other_state)
-    joined, edge = pl.pallas_call(
-        edge_kernel, out_shape=(tile(levels), plane), compiler_params=big, name="edges"
-    )(own_state, other_state, own_heat, other_heat, second, edge)
+    )(own_state, other_packet)
+    own_heat, edge = pl.pallas_call(
+        radiate_kernel, out_shape=(tile(levels), plane), compiler_params=big, name="radiate"
+    )(
+        left,
+        drops,
+        upper,
+        upper_strips,
+        other_packet,
+        cos_zenith,
+        sunlit,
+        thickness,
+        second_strips,
+        kappa_strips,
+        fixed,
+    )
     wide = lax.axis_size("wide")
     from_before = lax.ppermute(edge, "wide", [(i, (i + 1) % wide) for i in range(wide)])
     from_after = lax.ppermute(edge, "wide", [((i + 1) % wide, i) for i in range(wide)])
+    other_heat = swap(own_heat, "sub", [(0, 1)])
     heat, base = pl.pallas_call(
         base_kernel, out_shape=(tile(levels), tile(levels)), compiler_params=big, name="base"
-    )(own_state, own_heat, first_tend, joined)
+    )(own_state, other_packet, own_heat, other_heat, first_tend, second)
     new_state = pl.pallas_call(
         step_kernel, out_shape=tile(levels), compiler_params=big, name="step"
-    )(base, span, edge, from_before, from_after)
+    )(base, span, kappa_strips, mine, from_before, from_after)
     return (heat, new_state)
 
 

time: 15.5 us -> 16.1 us (1.039)
  Pallas kernels: 5.03 us -> 5.9 us
  starting transfers between devices: 7.32 us -> 7.12 us
    ppermute x1 -> x2, waiting for transfers between devices: 0.74 us -> 1.47 us  [the longest x1 1.4 us: shards(): moved_strips = lax.ppermute(strip_amount, ('lev', 'sub'), crossed)]
    pallas_call x3, Pallas kernels: 1.42 us -> 2.11 us  [the longest x1 1.13 us: shards(): pl.pallas_call(radiate_kernel, out_shape=(tile(levels), plane), compiler_...]
    ppermute x2, starting transfers between devices: 0.07 us -> 0.67 us  [swap(): return lax.ppermute(value, axis, route)]
    ppermute x2, waiting for transfers between devices: 0.58 us -> 0.01 us  [swap(): return lax.ppermute(value, axis, route)]
    ppermute x1, starting transfers between devices: 2.15 us -> 1.58 us  [shards(): lax.ppermute(edge, 'wide', [(i, (i + 1) % wide) for i in range(wide)])]
    ppermute x1 -> x2, starting transfers between devices: 3 us -> 2.63 us  [the longest x1 2.56 us: shards(): moved = lax.ppermute(amount, 'lev', straight)]
    pallas_call x1, Pallas kernels: 0.61 us -> 0.84 us  [shards(): pl.pallas_call(base_kernel, out_shape=(tile(levels), tile(levels)), compi...]
    ppermute x1, waiting for transfers between devices: 0.95 us -> 0.74 us  [shards(): lax.ppermute(edge, 'wide', [(i, (i + 1) % wide) for i in range(wide)])]
  transfers between devices with their start and end apart: 5 -> 6, of which waited for: 3 -> 3; matrix products, arithmetic and copies ran while one was open for 0% -> 0% of each run, Pallas kernels for 18% -> 16%
where the time goes in v3:
time: 16.1 us; the launch traced here: 15.9 us
  starting transfers between devices  7.12 us (44%)
  Pallas kernels  5.9 us (37%)
  waiting for transfers between devices  2.22 us (14%)
  between operations  0.67 us (4%)
    ppermute x1, starting transfers between devices, shards(): moved = lax.ppermute(amount, 'lev', straight)  2.56 us
    ppermute x1, starting transfers between devices, shards(): lax.ppermute(edge, 'wide', [((i + 1) % wide, i) for i in range(wide)])  2.25 us
    ppermute x1, starting transfers between devices, shards(): lax.ppermute(edge, 'wide', [(i, (i + 1) % wide) for i in range(wide)])  1.58 us
    ppermute x1, waiting for transfers between devices, shards(): moved_strips = lax.ppermute(strip_amount, ('lev', 'sub'), crossed)  1.4 us
    pallas_call x1, Pallas kernels, shards(): pl.pallas_call(radiate_kernel, out_shape=(tile(levels), plane), compiler_...  1.13 us
    pallas_call x1, Pallas kernels, shards(): pl.pallas_call(layers_kernel, out_shape=(jax.ShapeDtypeStruct((terms * ro...  1.1 us
    pallas_call x1, Pallas kernels, shards(): pl.pallas_call(fetch_kernel, out_shape=(tile(absorber.shape[0]), tile(lev...  0.99 us
    pallas_call x1, Pallas kernels, shards(): pl.pallas_call(step_kernel, out_shape=tile(levels), compiler_params=big,...  0.86 us
  transfers between devices with their start and end apart: 6, of which 3 were waited for; matrix products, arithmetic and copies ran while one was open for 0% of the time, Pallas kernels for 16%

profile of v3, /device:TPU:0, one launch (start us, length us, event | category | flops | bytes accessed | tf_op | source)
XLA Modules:
  0.0 15.9 jit_solution(16396954759242078538)
XLA Ops:
  0.6 1.0 %fetch.1 = (f32[7,8,128]{2,1,0:T(8,128)S(1)}, f32[5,8,128]{2,1,0:T(8,128)S(1)}, f32[7,4,8,128]{3,2,1,0:T(8,128)S(1)}, f32[4,8,128]{2,1,0:T(8,128)S(1)}, f32[8,12...) custom-call(f32[4,8,128]{2,1,0:T(8,128)} %refs_0_.1, f32[8,128]{1,0:T(8,128)} %refs_1_.1, ...), custom_call_target="tpu_custom_call" | custom-call | tf_op jit(solution)/shard_map/fetch/pallas_call | solution.py:402
  1.6 0.3 %strips.1 = (f32[14,8,128]{2,1,0:T(8,128)S(1)}, f32[7,8,128]{2,1,0:T(8,128)S(1)}) custom-call(f32[5,8,128]{2,1,0:T(8,128)S(1)} %get-tuple-element.25.own_state, f32[7,4,8,128]{3,2,1,0:T(8,128)S(1)} %get-tuple-element.26.absorber, f32[8,128]{1,0:T(8,128)S(1)} %get-tuple-element.27.zenith, s32[8,128]{1,0:T(8,128)S(1)} %get-tuple-element.28.lit, ...), custom_call_target="tpu_custom_call" | custom-call | tf_op jit(solution)/shard_map/strips/pallas_call | solution.py:411
  2.0 0.5 %collective-permute-start = (f32[14,8,128]{2,1,0:T(8,128)S(1)}, f32[14,8,128]{2,1,0:T(8,128)S(1)}, u32[]{:S(2)}, u32[]{:S(2)}) collective-permute-start(f32[14,8,128]{2,1,0:T(8,128)S(1)} %get-tuple-element.31), channel_id=1, source_target_pairs={{0,1},{1,0},{2,3},{3,2},{4,5},{5,4},{6,7},{7,6},{8,9},{9,8},{10,11... | collective-permute-start | bytes 172040 | tf_op jit(solution)/shard_map/ppermute | solution.py:388
  2.5 2.6 %collective-permute-start.1 = (f32[7,8,128]{2,1,0:T(8,128)S(1)}, f32[7,8,128]{2,1,0:T(8,128)S(1)}, u32[]{:S(2)}, u32[]{:S(2)}) collective-permute-start(f32[7,8,128]{2,1,0:T(8,128)S(1)} %get-tuple-element.30.amount), channel_id=1, source_target_pairs={{0,2},{2,0},{1,3},{3,1},{4,6},{6,4},{5,7},{7,5},{8,10},{10,8},{9,1... | collective-permute-start | bytes 86024 | tf_op jit(solution)/shard_map/ppermute | solution.py:423
  5.0 0.1 collective-permute-start.2
  5.1 1.1 %layers.1 = (bf16[1792,256]{1,0:T(8,128)(2,1)S(1)}, f32[4,1792,128]{2,1,0:T(8,128)S(1)}) custom-call(f32[7,4,8,128]{3,2,1,0:T(8,128)S(1)} %get-tuple-element.26.absorber, f32[8,128]{1,0:T(8,128)S(1)} %get-tuple-element.27.zenith, f32[7,224]{1,0:T(8,128)S(1)} %get-tuple-element.32.coef, f32[1,224]{1,0:T(1,128)S(1)} %get-tuple-element.33.weight), custom_call_target="tpu_custom_call" | custom-call | tf_op jit(solution)/shard_map/layers/pallas_call | solution.py:433
  6.2 0.0 collective-permute-done.packet
  6.2 0.6 %state.1 = (f32[4,8,128]{2,1,0:T(8,128)S(1)}, f32[4,2,8,128]{3,2,1,0:T(8,128)S(1)}, f32[2,8,128]{2,1,0:T(8,128)S(1)}, f32[8,128]{1,0:T(8,128)S(1)}, f32[8,128]{1...) custom-call(f32[5,8,128]{2,1,0:T(8,128)S(1)} %get-tuple-element.25.own_state, ...), custom_call_target="tpu_custom_call" | custom-call | tf_op jit(solution)/shard_map/state/pallas_call | solution.py:445
  6.9 0.1 collective-permute-done.1.upper
  6.9 1.4 %collective-permute-done.2.upper_strips = f32[7,8,128]{2,1,0:T(8,128)S(1)} collective-permute-done((f32[7,8,128]{2,1,0:T(8,128)S(1)}, f32[7,8,128]{2,1,0:T(8,128)S(1)}, u32[]{:S(2)}, u32[]{:S(2)}) %collective-permute-start.2) | collective-permute-done | bytes 28704 | tf_op jit(solution)/shard_map/ppermute | solution.py:424
  8.3 1.1 %radiate.1 = (f32[4,8,128]{2,1,0:T(8,128)S(1)}, f32[8,128]{1,0:T(8,128)S(1)}) custom-call(bf16[1792,256]{1,0:T(8,128)(2,1)S(1)} %get-tuple-element.34.left, f32[4,1792,128]{2,1,0:T(8,128)S(1)} %get-tuple-element.35.drops, f32[7,8,128]{2,1,0:T(8,128)S(1)} %collective-permute-done.1.upper, f32[7,8,128]{2,1,0:T(8,128)S(1)} %collective-permute-done.2.upper_strips, ...), custom_call_target="tpu_custom_call" | custom-call | tf_op jit(solution)/shard_map/radiate/pallas_call | solution.py:451
  9.5 0.2 %collective-permute-start.3 = (f32[4,8,128]{2,1,0:T(8,128)S(1)}, f32[4,8,128]{2,1,0:T(8,128)S(1)}, u32[]{:S(2)}, u32[]{:S(2)}) collective-permute-start(f32[4,8,128]{2,1,0:T(8,128)S(1)} %get-tuple-element.40.own_heat), channel_id=1, source_target_pairs={{0,1},{1,0},{2,3},{3,2},{4,5},{5,4},{6,7},{7,6},{8,9},{9,8},{10,11... | collective-permute-start | bytes 49160 | tf_op jit(solution)/shard_map/ppermute | solution.py:388
  9.6 1.6 %collective-permute-start.4 = (f32[8,128]{1,0:T(8,128)S(1)}, f32[8,128]{1,0:T(8,128)S(1)}, u32[]{:S(2)}, u32[]{:S(2)}) collective-permute-start(f32[8,128]{1,0:T(8,128)S(1)} %get-tuple-element.47), channel_id=1, source_target_pairs={{0,4},{4,8},{8,12},{12,0},{1,5},{5,9},{9,13},{13,1},{2,6},{6,10},{... | collective-permute-start | bytes 12296 | tf_op jit(solution)/shard_map/ppermute | solution.py:467
  11.2 2.2 %collective-permute-start.5 = (f32[8,128]{1,0:T(8,128)S(1)}, f32[8,128]{1,0:T(8,128)S(1)}, u32[]{:S(2)}, u32[]{:S(2)}) collective-permute-start(f32[8,128]{1,0:T(8,128)S(1)} %get-tuple-element.47), channel_id=1, source_target_pairs={{4,0},{8,4},{12,8},{0,12},{5,1},{9,5},{13,9},{1,13},{6,2},{10,6},{... | collective-permute-start | bytes 12296 | tf_op jit(solution)/shard_map/ppermute | solution.py:468
  13.5 0.0 collective-permute-done.3.other_heat
  13.5 0.8 %base.1 = (f32[4,8,128]{2,1,0:T(8,128)}, f32[4,8,128]{2,1,0:T(8,128)S(1)}) custom-call(f32[5,8,128]{2,1,0:T(8,128)S(1)} %get-tuple-element.25.own_state, f32[14,8,128]{2,1,0:T(8,128)S(1)} %collective-permute-done.packet, f32[4,8,128]{2,1,0:T(8,128)S(1)} %get-tuple-element.40.own_heat, f32[4,8,128]{2,1,0:T(8,128)S(1)} %collective-permute-done.3.other_heat, ...), custom_call_target="tpu_custom_call" | custom-call | tf_op jit(solution)/shard_map/base/pallas_call | solution.py:470
  14.3 0.7 %collective-permute-done.4.from_before = f32[8,128]{1,0:T(8,128)S(1)} collective-permute-done((f32[8,128]{1,0:T(8,128)S(1)}, f32[8,128]{1,0:T(8,128)S(1)}, u32[]{:S(2)}, u32[]{:S(2)}) %collective-permute-start.4) | collective-permute-done | bytes 4128 | tf_op jit(solution)/shard_map/ppermute | solution.py:467
  15.0 0.0 collective-permute-done.5.from_after
  15.0 0.9 %step.1 = f32[4,8,128]{2,1,0:T(8,128)} custom-call(f32[4,8,128]{2,1,0:T(8,128)S(1)} %get-tuple-element.44.base, f32[2,8,128]{2,1,0:T(8,128)S(1)} %get-tuple-element.45.span, f32[8,128]{1,0:T(8,128)S(1)} %get-tuple-element.38.kappa, f32[2,8,128]{2,1,0:T(8,128)S(1)} %get-tuple-element.46.mine, f32[8,128]{1,0:T(8,128)S(1)} %collective-permute-done.4.from_before, ...), custom_call_target="tpu_custom_call" | custom-call | tf_op jit(solution)/shard_map/step/pallas_call | solution.py:473
Async XLA Ops:
  2.0 4.2 %collective-permute-start = (f32[14,8,128]{2,1,0:T(8,128)S(1)}, f32[14,8,128]{2,1,0:T(8,128)S(1)}, u32[]{:S(2)}, u32[]{:S(2)}) collective-permute-start(f32[14,8,128]{2,1,0:T(8,128)S(1)} %get-tuple-element.31), channel_id=1, source_target_pairs={{0,1},{1,0},{2,3},{3,2},{4,5},{5,4},{6,7},{7,6},{8,9},{9,8},{10,11... | collective-permute-start | bytes 172040 | tf_op jit(solution)/shard_map/ppermute | solution.py:388
  2.5 4.5 %collective-permute-start.1 = (f32[7,8,128]{2,1,0:T(8,128)S(1)}, f32[7,8,128]{2,1,0:T(8,128)S(1)}, u32[]{:S(2)}, u32[]{:S(2)}) collective-permute-start(f32[7,8,128]{2,1,0:T(8,128)S(1)} %get-tuple-element.30.amount), channel_id=1, source_target_pairs={{0,2},{2,0},{1,3},{3,1},{4,6},{6,4},{5,7},{7,5},{8,10},{10,8},{9,1... | collective-permute-start | bytes 86024 | tf_op jit(solution)/shard_map/ppermute | solution.py:423
  5.0 3.3 %collective-permute-start.2 = (f32[7,8,128]{2,1,0:T(8,128)S(1)}, f32[7,8,128]{2,1,0:T(8,128)S(1)}, u32[]{:S(2)}, u32[]{:S(2)}) collective-permute-start(f32[7,8,128]{2,1,0:T(8,128)S(1)} %get-tuple-element.36), channel_id=1, source_target_pairs={{0,3},{1,2},{2,1},{3,0},{4,7},{5,6},{6,5},{7,4},{8,11},{9,10},{10,... | collective-permute-start | bytes 86024 | tf_op jit(solution)/shard_map/ppermute | solution.py:424
  9.5 4.0 %collective-permute-start.3 = (f32[4,8,128]{2,1,0:T(8,128)S(1)}, f32[4,8,128]{2,1,0:T(8,128)S(1)}, u32[]{:S(2)}, u32[]{:S(2)}) collective-permute-start(f32[4,8,128]{2,1,0:T(8,128)S(1)} %get-tuple-element.40.own_heat), channel_id=1, source_target_pairs={{0,1},{1,0},{2,3},{3,2},{4,5},{5,4},{6,7},{7,6},{8,9},{9,8},{10,11... | collective-permute-start | bytes 49160 | tf_op jit(solution)/shard_map/ppermute | solution.py:388
  9.6 5.4 %collective-permute-start.4 = (f32[8,128]{1,0:T(8,128)S(1)}, f32[8,128]{1,0:T(8,128)S(1)}, u32[]{:S(2)}, u32[]{:S(2)}) collective-permute-start(f32[8,128]{1,0:T(8,128)S(1)} %get-tuple-element.47), channel_id=1, source_target_pairs={{0,4},{4,8},{8,12},{12,0},{1,5},{5,9},{9,13},{13,1},{2,6},{6,10},{... | collective-permute-start | bytes 12296 | tf_op jit(solution)/shard_map/ppermute | solution.py:467
  11.2 3.8 %collective-permute-start.5 = (f32[8,128]{1,0:T(8,128)S(1)}, f32[8,128]{1,0:T(8,128)S(1)}, u32[]{:S(2)}, u32[]{:S(2)}) collective-permute-start(f32[8,128]{1,0:T(8,128)S(1)} %get-tuple-element.47), channel_id=1, source_target_pairs={{4,0},{8,4},{12,8},{0,12},{5,1},{9,5},{13,9},{1,13},{6,2},{10,6},{... | collective-permute-start | bytes 12296 | tf_op jit(solution)/shard_map/ppermute | solution.py:468

commit v4 on v3

--- a/solution.py
+++ b/solution.py
@@ -1,3 +1,4 @@
+import functools
 import math
 
 import jax
@@ -158,7 +159,9 @@
     return jnp.concatenate([hi, mid, lo, hi, tail], axis=0).astype(jnp.bfloat16)
 
 
-def layers_kernel(absorber, zenith, coef, weight, left, drops, spread):
+def layers_kernel(
+    own_state, absorber, zenith, lit, thickness, coef, weight, left, drops, strips, factor, kappa, spread
+):
     species, levels, rows, width = absorber.shape
     terms = coef.shape[1]
     group = species * rows
@@ -204,62 +207,80 @@
             drop = out[:, k * width : (k + 1) * width] - out[:, (k + 1) * width : (k + 2) * width]
             drops[k, pl.ds(start, chunk), :] = drop
 
-
-def radiate_kernel(
-    left, drops, upper, upper_strips, packet, zenith, lit, thickness, second, kappa, fixed, heat, edge
-):
+    place = lax.broadcasted_iota(jnp.int32, (rows, width), 1)
+    zero = jnp.zeros((rows, width), jnp.float32)
+    for s in range(species):
+        total, sums = zero, [None]
+        for k in range(levels):
+            total = total + absorber[s, k]
+            sums.append(total)
+        strips[s] = to_strips(place, zero, sums)
+    strips[species] = to_strips(place, zero - 1.0, [scale] * (levels + 1))
+    lit_zenith = jnp.where(lit[...] == 1, zenith[...], 0.0)
+    factor[...] = to_strips(place, zero, [lit_zenith / thickness[k] for k in range(levels)])
+    kappa[...] = to_strips(place, zero, [own_state[levels]] * levels)
+
+
+def radiate_kernel(left, drops, upper, zenith, lit, thickness, after, heat):
     levels, rows, width = heat.shape
     depth = left.shape[1]
     species = upper.shape[0]
-    stencil = Stencil(rows, width)
     zen = zenith[...]
     below = lax.axis_index("lev") > 0
     totals = [jnp.where(below, upper[s], 0.0) for s in range(species)]
-    raw = levels + 1
-    strip_totals = []
-    for s in range(species):
-        layer = packet[raw + s]
-        total = jnp.where(below, upper_strips[s], 0.0)
-        for k in range(levels):
-            total = total + pltpu.roll(layer, strip * (k + 1), 1)
-        strip_totals.append(total)
-    right = jnp.concatenate(
-        [
-            amount_rows(totals, -log2e / zen, depth, 0),
-            amount_rows(strip_totals, -log2e / packet[raw + species], depth, 3),
-        ],
-        axis=1,
-    )
+    right = amount_rows(totals, -log2e / zen, depth, 0)
     chunk = 448
-    lanes = 4
-    zero = jnp.zeros((rows, width), jnp.float32)
-    sums = [[zero] * lanes for _ in range(levels)]
-    strip_sums = [zero] * lanes
+    sums = [jnp.zeros((rows, width), jnp.float32) for _ in range(levels)]
     for start in range(0, left.shape[0], chunk):
         above = jnp.exp2(
             jnp.dot(left[pl.ds(start, chunk), :], right, preferred_element_type=jnp.float32)
         )
-        for i in range(chunk // rows):
-            at, n = i * rows, i % lanes
-            main = above[at : at + rows, :width]
-            strip_sums[n] = strip_sums[n] + above[at : at + rows, width:]
-            for k in range(levels):
-                sums[k][n] = sums[k][n] + main * drops[k, pl.ds(start + at, rows), :]
-
-    def total_of(parts):
-        return (parts[0] + parts[1]) + (parts[2] + parts[3])
-
+        for k in range(levels):
+            absorbed = above * drops[k, pl.ds(start, chunk), :]
+            sums[k] = sums[k] + jnp.sum(absorbed.reshape(chunk // rows, rows, width), axis=0)
     lit_zenith = jnp.where(lit[...] == 1, zen, 0.0)
-    heats = [lit_zenith * total_of(sums[k]) / thickness[k] for k in range(levels)]
     for k in range(levels):
-        heat[k] = heats[k]
-    passed = total_of(strip_sums)
-    other = packet[raw + species + 1] * (passed - pltpu.roll(passed, width - strip, 1))
-    strips = to_strips(stencil.lane, zero, heats) + pltpu.roll(other, width // 2, 1)
-    r = second[...] + stencil.residual(strips, kappa[...])
+        heat[k] = lit_zenith * sums[k] / thickness[k]
+
+
+def edge_heat_kernel(levels, left, upper, layers, factor, kappa, second, out):
+    species = upper.shape[0]
+    rows, width = factor.shape
+    stencil = Stencil(rows, width)
+    lane = stencil.lane
+    below = lax.axis_index("lev") > 0
+    totals = []
+    for s in range(species):
+        above = jnp.where(below & (lane < strip), pltpu.roll(upper[s], points, 1), 0.0)
+        total = layers[s] + above
+        for k in range(1, levels + 1):
+            total = total + pltpu.roll(above, strip * k, 1)
+        totals.append(total)
+    right = amount_rows(totals, layers[species], left.shape[1], 3)
+    passed = jnp.exp2(jnp.dot(left[...], right, preferred_element_type=jnp.float32))
+    passed = sum_rows(passed, rows)
+    heat = factor[...] * (passed - pltpu.roll(passed, width - strip, 1))
+    out[...] = stencil.residual(heat, kappa[...]) + jnp.where(lane < width // 2, second[...], 0.0)
+
+
+def sum_rows(value, rows):
+    parts = [value[i : i + rows] for i in range(0, value.shape[0], rows)]
+    sums = parts[:8]
+    for i in range(8, len(parts)):
+        sums[i % 8] = sums[i % 8] + parts[i]
+    while len(sums) > 1:
+        sums = [sum(sums[i : i + 2]) for i in range(0, len(sums), 2)]
+    return sums[0]
+
+
+def join_kernel(own, other, fixed, heat, edge, heat_out):
+    rows, width = own.shape
+    stencil = Stencil(rows, width)
+    r = own[...] + pltpu.roll(other[...], width // 2, 1)
     joined = stencil.rows_joined(r, pltpu.roll(r, width // 2, 1))
     node = stencil.lane % strip
     edge[...] = jnp.where((node == points - 1) | (node == points), joined, fixed[...])
+    heat_out[...] = heat[...]
 
 
 def tiles_of(field):
@@ -267,41 +288,14 @@
     return [t for n in range(2) for t in [field[l, n] for l in range(field.shape[0])] + gap]
 
 
-def strips_kernel(own_state, absorber, zenith, lit, thickness, amount, packet, upper_strips):
-    species, levels, rows, width = absorber.shape
-    lane = lax.broadcasted_iota(jnp.int32, (rows, width), 1)
-    zero = jnp.zeros((rows, width), jnp.float32)
-    raw = levels + 1
-
-    def everywhere(value, count):
-        out = to_strips(lane, zero, [value])
-        step = strip
-        while step < strip * count:
-            out = out + pltpu.roll(out, step, 1)
-            step *= 2
-        return out
-
-    for s in range(species):
-        upper_strips[s] = everywhere(amount[s], 8)
-        packet[raw + s] = to_strips(lane, zero, [absorber[s, k] for k in range(levels)])
-    for i in range(raw):
-        packet[i] = own_state[i]
-    zen = zenith[...]
-    packet[raw + species] = everywhere(zen, 16)
-    lit_zenith = jnp.where(lit[...] == 1, zen, 0.0)
-    packet[raw + species + 1] = to_strips(
-        lane, zero, [lit_zenith / thickness[k] for k in range(levels)]
-    )
-
-
-def state_kernel(own_state, packet, first_tend, second, span_out, second_strips, kappa_strips, fixed, mine):
+def state_kernel(own_state, other_state, first_tend, second, span_out, second_strips, kappa_strips, fixed, mine):
     levels = own_state.shape[0] - 1
     rows, width = own_state.shape[1:]
     stencil = Stencil(rows, width)
     lane = stencil.lane
     zero = jnp.zeros((rows, width), jnp.float32)
-    air = jnp.stack([own_state[:levels], packet[:levels]], axis=1)
-    kappa = jnp.stack([own_state[levels], packet[levels]], axis=0)
+    air = jnp.stack([own_state[:levels], other_state[:levels]], axis=1)
+    kappa = jnp.stack([own_state[levels], other_state[levels]], axis=0)
     r = stencil.residual(air, kappa)
     joined = stencil.rows_joined(r, jnp.concatenate([r[:, 1:], r[:, :1]], axis=1))
     tend = stencil.inv_mass * stencil.columns_joined(joined)
@@ -333,13 +327,13 @@
     mine[1] = stencil.weight_y * stencil.apply("d", 0, change)
 
 
-def base_kernel(own_state, packet, own_heat, other_heat, first_tend, second, heat_out, base):
+def base_kernel(own_state, other_state, own_heat, other_heat, first_tend, second, heat_out, base):
     levels, rows, width = own_heat.shape
     stencil = Stencil(rows, width)
     own = own_heat[...]
     heat_out[...] = own
     heat = jnp.stack([own, other_heat[...]], axis=1)
-    kappa = jnp.stack([own_state[levels], packet[levels]], axis=0)
+    kappa = jnp.stack([own_state[levels], other_state[levels]], axis=0)
     r = second[...] + stencil.residual(heat, kappa)
     joined = stencil.rows_joined(r[:, 0], r[:, 1])
     base[...] = (
@@ -408,68 +402,58 @@
         name="fetch",
     )(*args)
     species = absorber.shape[0]
-    packet, strip_amount = pl.pallas_call(
-        strips_kernel,
-        out_shape=(tile(levels + 1 + species + 2), tile(species)),
-        compiler_params=big,
-        name="strips",
-    )(own_state, absorber, cos_zenith, sunlit, thickness, amount)
     size = lax.axis_size("lev")
     lev = lax.axis_index("lev")
-    upper = upper_strips = None
+    upper = None
     for step in range(1, size):
-        straight = [(i, (i + step) % size) for i in range(size)]
-        crossed = [(2 * i + c, 2 * j + 1 - c) for i, j in straight for c in range(2)]
-        moved = lax.ppermute(amount, "lev", straight)
-        moved_strips = lax.ppermute(strip_amount, ("lev", "sub"), crossed)
+        moved = lax.ppermute(amount, "lev", [(i, (i + step) % size) for i in range(size)])
         if size > 2:
             moved = jnp.where(lev >= step, moved, 0.0)
-            moved_strips = jnp.where(lev >= step, moved_strips, 0.0)
         upper = moved if upper is None else upper + moved
-        upper_strips = moved_strips if upper_strips is None else upper_strips + moved_strips
     if upper is None:
-        upper, upper_strips = jnp.zeros_like(amount), jnp.zeros_like(amount)
-    other_packet = swap(packet, "sub", [(0, 1)])
-    left, drops = pl.pallas_call(
+        upper = jnp.zeros_like(amount)
+    other_state = swap(own_state, "sub", [(0, 1)])
+    plane = jax.ShapeDtypeStruct((rows, width), jnp.float32)
+    left, drops, strips, factor, kappa = pl.pallas_call(
         layers_kernel,
         out_shape=(
             jax.ShapeDtypeStruct((terms * rows, 256), jnp.bfloat16),
             jax.ShapeDtypeStruct((levels, terms * rows, width), jnp.float32),
+            tile(species + 1),
+            plane,
+            plane,
         ),
         scratch_shapes=[pltpu.VMEM((terms, 256), jnp.float32)],
         compiler_params=big,
         name="layers",
-    )(absorber, cos_zenith, absorb_coef, weight)
+    )(own_state, absorber, cos_zenith, sunlit, thickness, absorb_coef, weight)
     pair = jax.ShapeDtypeStruct((levels, 2, rows, width), jnp.float32)
-    plane = jax.ShapeDtypeStruct((rows, width), jnp.float32)
     first_tend, second, span, second_strips, kappa_strips, fixed, mine = pl.pallas_call(
         state_kernel,
         out_shape=(tile(levels), pair, tile(2), plane, plane, plane, tile(2)),
         compiler_params=big,
         name="state",
-    )(own_state, other_packet)
-    own_heat, edge = pl.pallas_call(
-        radiate_kernel, out_shape=(tile(levels), plane), compiler_params=big, name="radiate"
-    )(
-        left,
-        drops,
-        upper,
-        upper_strips,
-        other_packet,
-        cos_zenith,
-        sunlit,
-        thickness,
-        second_strips,
-        kappa_strips,
-        fixed,
-    )
+    )(own_state, other_state)
+    own_r = pl.pallas_call(
+        functools.partial(edge_heat_kernel, levels),
+        out_shape=plane,
+        compiler_params=big,
+        name="edge_heat",
+    )(left, upper, strips, factor, kappa, second_strips)
+    other_r = swap(own_r, "sub", [(0, 1)])
+    own_heat = pl.pallas_call(
+        radiate_kernel, out_shape=tile(levels), compiler_params=big, name="radiate"
+    )(left, drops, upper, cos_zenith, sunlit, thickness, own_r)
+    edge, own_heat = pl.pallas_call(
+        join_kernel, out_shape=(plane, tile(levels)), compiler_params=big, name="join"
+    )(own_r, other_r, fixed, own_heat)
     wide = lax.axis_size("wide")
     from_before = lax.ppermute(edge, "wide", [(i, (i + 1) % wide) for i in range(wide)])
     from_after = lax.ppermute(edge, "wide", [((i + 1) % wide, i) for i in range(wide)])
     other_heat = swap(own_heat, "sub", [(0, 1)])
     heat, base = pl.pallas_call(
         base_kernel, out_shape=(tile(levels), tile(levels)), compiler_params=big, name="base"
-    )(own_state, other_packet, own_heat, other_heat, first_tend, second)
+    )(own_state, other_state, own_heat, other_heat, first_tend, second)
     new_state = pl.pallas_call(
         step_kernel, out_shape=tile(levels), compiler_params=big, name="step"
     )(base, span, kappa_strips, mine, from_before, from_after)

time: 16.1 us -> 15.6 us (0.969)
  waiting for transfers between devices: 2.22 us -> 1.19 us
  starting transfers between devices: 7.12 us -> 7.67 us
    ppermute x2 -> x1, waiting for transfers between devices: 1.47 us -> 0.03 us  [shards(): lax.ppermute(amount, 'lev', [(i, (i + step) % size) for i in range(size)])]
    ppermute x2 -> x3, waiting for transfers between devices: 0.01 us -> 0.38 us  [swap(): return lax.ppermute(value, axis, route)]
    ppermute x2 -> x1, starting transfers between devices: 2.63 us -> 3 us  [shards(): lax.ppermute(amount, 'lev', [(i, (i + step) % size) for i in range(size)])]
    ppermute x1, starting transfers between devices: 1.58 us -> 1.84 us  [shards(): lax.ppermute(edge, 'wide', [(i, (i + 1) % wide) for i in range(wide)])]
    ppermute x1, starting transfers between devices: 2.25 us -> 2.03 us  [shards(): lax.ppermute(edge, 'wide', [((i + 1) % wide, i) for i in range(wide)])]
    ppermute x2 -> x3, starting transfers between devices: 0.67 us -> 0.8 us  [swap(): return lax.ppermute(value, axis, route)]
    pallas_call x2 -> x3, Pallas kernels: 1.48 us -> 1.48 us  [the longest x1 0.81 us: shards(): pl.pallas_call(functools.partial(edge_heat_kernel, levels), out_shape=pla...]
  transfers between devices with their start and end apart: 6 -> 6, of which waited for: 3 -> 3; matrix products, arithmetic and copies ran while one was open for 0% -> 0% of each run, Pallas kernels for 16% -> 20%
where the time goes in v4:
time: 15.6 us; the launch traced here: 15.4 us
  starting transfers between devices  7.67 us (49%)
  Pallas kernels  5.89 us (38%)
  waiting for transfers between devices  1.19 us (8%)
  between operations  0.67 us (4%)
    ppermute x1, starting transfers between devices, shards(): lax.ppermute(amount, 'lev', [(i, (i + step) % size) for i in range(size)])  3 us
    ppermute x1, starting transfers between devices, shards(): lax.ppermute(edge, 'wide', [((i + 1) % wide, i) for i in range(wide)])  2.03 us
    ppermute x1, starting transfers between devices, shards(): lax.ppermute(edge, 'wide', [(i, (i + 1) % wide) for i in range(wide)])  1.84 us
    pallas_call x1, Pallas kernels, shards(): pl.pallas_call(layers_kernel, out_shape=(jax.ShapeDtypeStruct((terms * ro...  1.09 us
    pallas_call x1, Pallas kernels, shards(): pl.pallas_call(fetch_kernel, out_shape=(tile(absorber.shape[0]), tile(lev...  0.99 us
    pallas_call x1, Pallas kernels, shards(): pl.pallas_call(step_kernel, out_shape=tile(levels), compiler_params=big,...  0.86 us
    pallas_call x1, Pallas kernels, shards(): pl.pallas_call(base_kernel, out_shape=(tile(levels), tile(levels)), compi...  0.84 us
    pallas_call x1, Pallas kernels, shards(): pl.pallas_call(functools.partial(edge_heat_kernel, levels), out_shape=pla...  0.81 us
  transfers between devices with their start and end apart: 6, of which 3 were waited for; matrix products, arithmetic and copies ran while one was open for 0% of the time, Pallas kernels for 20%

profile of v4, /device:TPU:0, one launch (start us, length us, event | category | flops | bytes accessed | tf_op | source)
XLA Modules:
  0.0 15.4 jit_solution(15701418044348288987)
XLA Ops:
  0.6 1.0 %fetch.1 = (f32[7,8,128]{2,1,0:T(8,128)S(1)}, f32[5,8,128]{2,1,0:T(8,128)S(1)}, f32[7,4,8,128]{3,2,1,0:T(8,128)S(1)}, f32[4,8,128]{2,1,0:T(8,128)S(1)}, f32[8,12...) custom-call(f32[4,8,128]{2,1,0:T(8,128)} %refs_0_.1, f32[8,128]{1,0:T(8,128)} %refs_1_.1, ...), custom_call_target="tpu_custom_call" | custom-call | tf_op jit(solution)/shard_map/fetch/pallas_call | solution.py:396
  1.6 3.0 %collective-permute-start.1 = (f32[7,8,128]{2,1,0:T(8,128)S(1)}, f32[7,8,128]{2,1,0:T(8,128)S(1)}, u32[]{:S(2)}, u32[]{:S(2)}) collective-permute-start(f32[7,8,128]{2,1,0:T(8,128)S(1)} %get-tuple-element.34), channel_id=1, source_target_pairs={{0,2},{2,0},{1,3},{3,1},{4,6},{6,4},{5,7},{7,5},{8,10},{10,8},{9,1... | collective-permute-start | bytes 86024 | tf_op jit(solution)/shard_map/ppermute | solution.py:409
  4.6 0.0 collective-permute-start
  4.6 1.1 %layers.1 = (bf16[1792,256]{1,0:T(8,128)(2,1)S(1)}, f32[4,1792,128]{2,1,0:T(8,128)S(1)}, f32[8,8,128]{2,1,0:T(8,128)S(1)}, f32[8,128]{1,0:T(8,128)S(1)}, f32[8,128]{1,0:T(8,128)S(1)}) custom-call(f32[5,8,128]{2,1,0:T(8,128)S(1)} %get-tuple-element.26.own_state, f32[7,4,8,128]{3,2,1,0:T(8,128)S(1)} %get-tuple-element.27.absorber, ...), custom_call_target="tpu_custom_call" | custom-call | tf_op jit(solution)/shard_map/layers/pallas_call | solution.py:417
  5.7 0.1 collective-permute-done.other_state
  5.8 0.6 %state.1 = (f32[4,8,128]{2,1,0:T(8,128)S(1)}, f32[4,2,8,128]{3,2,1,0:T(8,128)S(1)}, f32[2,8,128]{2,1,0:T(8,128)S(1)}, f32[8,128]{1,0:T(8,128)S(1)}, f32[8,128]{1...) custom-call(f32[5,8,128]{2,1,0:T(8,128)S(1)} %get-tuple-element.26.own_state, ...), custom_call_target="tpu_custom_call" | custom-call | tf_op jit(solution)/shard_map/state/pallas_call | solution.py:431
  6.5 0.0 collective-permute-done.1.upper
  6.5 0.8 %edge_heat.1.after.own = f32[8,128]{1,0:T(8,128)S(1)} custom-call(bf16[1792,256]{1,0:T(8,128)(2,1)S(1)} %get-tuple-element.33.left, f32[7,8,128]{2,1,0:T(8,128)S(1)} %collective-permute-done.1.upper, f32[8,8,128]{2,1,0:T(8,128)S(1)} %get-tuple-element.35.layers, f32[8,128]{1,0:T(8,128)S(1)} %get-tuple-element.36.factor, ...), custom_call_target="tpu_custom_call" | custom-call | tf_op jit(solution)/shard_map/edge_heat/pallas_call | solution.py:437
  7.3 0.5 %collective-permute-start.2 = (f32[8,128]{1,0:T(8,128)S(1)}, f32[8,128]{1,0:T(8,128)S(1)}, u32[]{:S(2)}, u32[]{:S(2)}) collective-permute-start(f32[8,128]{1,0:T(8,128)S(1)} %edge_heat.1.after.own), channel_id=1, source_target_pairs={{0,1},{1,0},{2,3},{3,2},{4,5},{5,4},{6,7},{7,6},{8,9},{9,8},{10,11... | collective-permute-start | bytes 12296 | tf_op jit(solution)/shard_map/ppermute | solution.py:382
  7.7 0.5 %radiate.1.heat = f32[4,8,128]{2,1,0:T(8,128)S(1)} custom-call(bf16[1792,256]{1,0:T(8,128)(2,1)S(1)} %get-tuple-element.33.left, f32[4,1792,128]{2,1,0:T(8,128)S(1)} %get-tuple-element.40.drops, f32[7,8,128]{2,1,0:T(8,128)S(1)} %collective-permute-done.1.upper, f32[8,128]{1,0:T(8,128)S(1)} %get-tuple-element.28.zenith, s32[8,128]{1,0:T(8,128)S(1)} %get-tuple-element.29.lit, ...), custom_call_target="tpu_custom_call" | custom-call | tf_op jit(solution)/shard_map/radiate/pallas_call | solution.py:444
  8.3 0.3 %collective-permute-done.2.other = f32[8,128]{1,0:T(8,128)S(1)} collective-permute-done((f32[8,128]{1,0:T(8,128)S(1)}, f32[8,128]{1,0:T(8,128)S(1)}, u32[]{:S(2)}, u32[]{:S(2)}) %collective-permute-start.2) | collective-permute-done | bytes 4128 | tf_op jit(solution)/shard_map/ppermute | solution.py:382
  8.6 0.1 join.1
  8.7 0.3 %collective-permute-start.3 = (f32[4,8,128]{2,1,0:T(8,128)S(1)}, f32[4,8,128]{2,1,0:T(8,128)S(1)}, u32[]{:S(2)}, u32[]{:S(2)}) collective-permute-start(f32[4,8,128]{2,1,0:T(8,128)S(1)} %get-tuple-element.41.own_heat), channel_id=1, source_target_pairs={{0,1},{1,0},{2,3},{3,2},{4,5},{5,4},{6,7},{7,6},{8,9},{9,8},{10,11... | collective-permute-start | bytes 49160 | tf_op jit(solution)/shard_map/ppermute | solution.py:382
  9.1 1.8 %collective-permute-start.4 = (f32[8,128]{1,0:T(8,128)S(1)}, f32[8,128]{1,0:T(8,128)S(1)}, u32[]{:S(2)}, u32[]{:S(2)}) collective-permute-start(f32[8,128]{1,0:T(8,128)S(1)} %get-tuple-element.49), channel_id=1, source_target_pairs={{0,4},{4,8},{8,12},{12,0},{1,5},{5,9},{9,13},{13,1},{2,6},{6,10},{... | collective-permute-start | bytes 12296 | tf_op jit(solution)/shard_map/ppermute | solution.py:451
  10.9 2.0 %collective-permute-start.5 = (f32[8,128]{1,0:T(8,128)S(1)}, f32[8,128]{1,0:T(8,128)S(1)}, u32[]{:S(2)}, u32[]{:S(2)}) collective-permute-start(f32[8,128]{1,0:T(8,128)S(1)} %get-tuple-element.49), channel_id=1, source_target_pairs={{4,0},{8,4},{12,8},{0,12},{5,1},{9,5},{13,9},{1,13},{6,2},{10,6},{... | collective-permute-start | bytes 12296 | tf_op jit(solution)/shard_map/ppermute | solution.py:452
  12.9 0.0 collective-permute-done.3.other_heat
  12.9 0.8 %base.1 = (f32[4,8,128]{2,1,0:T(8,128)}, f32[4,8,128]{2,1,0:T(8,128)S(1)}) custom-call(f32[5,8,128]{2,1,0:T(8,128)S(1)} %get-tuple-element.26.own_state, f32[5,8,128]{2,1,0:T(8,128)S(1)} %collective-permute-done.other_state, f32[4,8,128]{2,1,0:T(8,128)S(1)} %get-tuple-element.41.own_heat, f32[4,8,128]{2,1,0:T(8,128)S(1)} %collective-permute-done.3.other_heat, ...), custom_call_target="tpu_custom_call" | custom-call | tf_op jit(solution)/shard_map/base/pallas_call | solution.py:454
  13.8 0.8 %collective-permute-done.4.from_before = f32[8,128]{1,0:T(8,128)S(1)} collective-permute-done((f32[8,128]{1,0:T(8,128)S(1)}, f32[8,128]{1,0:T(8,128)S(1)}, u32[]{:S(2)}, u32[]{:S(2)}) %collective-permute-start.4) | collective-permute-done | bytes 4128 | tf_op jit(solution)/shard_map/ppermute | solution.py:451
  14.6 0.0 collective-permute-done.5.from_after
  14.6 0.9 %step.1 = f32[4,8,128]{2,1,0:T(8,128)} custom-call(f32[4,8,128]{2,1,0:T(8,128)S(1)} %get-tuple-element.45.base, f32[2,8,128]{2,1,0:T(8,128)S(1)} %get-tuple-element.46.span, f32[8,128]{1,0:T(8,128)S(1)} %get-tuple-element.47.kappa, f32[2,8,128]{2,1,0:T(8,128)S(1)} %get-tuple-element.48.mine, f32[8,128]{1,0:T(8,128)S(1)} %collective-permute-done.4.from_before, ...), custom_call_target="tpu_custom_call" | custom-call | tf_op jit(solution)/shard_map/step/pallas_call | solution.py:457
Async XLA Ops:
  1.6 4.9 %collective-permute-start.1 = (f32[7,8,128]{2,1,0:T(8,128)S(1)}, f32[7,8,128]{2,1,0:T(8,128)S(1)}, u32[]{:S(2)}, u32[]{:S(2)}) collective-permute-start(f32[7,8,128]{2,1,0:T(8,128)S(1)} %get-tuple-element.34), channel_id=1, source_target_pairs={{0,2},{2,0},{1,3},{3,1},{4,6},{6,4},{5,7},{7,5},{8,10},{10,8},{9,1... | collective-permute-start | bytes 86024 | tf_op jit(solution)/shard_map/ppermute | solution.py:409
  4.6 1.2 %collective-permute-start = (f32[5,8,128]{2,1,0:T(8,128)S(1)}, f32[5,8,128]{2,1,0:T(8,128)S(1)}, u32[]{:S(2)}, u32[]{:S(2)}) collective-permute-start(f32[5,8,128]{2,1,0:T(8,128)S(1)} %get-tuple-element.26.own_state), channel_id=1, source_target_pairs={{0,1},{1,0},{2,3},{3,2},{4,5},{5,4},{6,7},{7,6},{8,9},{9,8},{10,11... | collective-permute-start | bytes 61448 | tf_op jit(solution)/shard_map/ppermute | solution.py:382
  7.3 1.3 %collective-permute-start.2 = (f32[8,128]{1,0:T(8,128)S(1)}, f32[8,128]{1,0:T(8,128)S(1)}, u32[]{:S(2)}, u32[]{:S(2)}) collective-permute-start(f32[8,128]{1,0:T(8,128)S(1)} %edge_heat.1.after.own), channel_id=1, source_target_pairs={{0,1},{1,0},{2,3},{3,2},{4,5},{5,4},{6,7},{7,6},{8,9},{9,8},{10,11... | collective-permute-start | bytes 12296 | tf_op jit(solution)/shard_map/ppermute | solution.py:382
  8.7 4.2 %collective-permute-start.3 = (f32[4,8,128]{2,1,0:T(8,128)S(1)}, f32[4,8,128]{2,1,0:T(8,128)S(1)}, u32[]{:S(2)}, u32[]{:S(2)}) collective-permute-start(f32[4,8,128]{2,1,0:T(8,128)S(1)} %get-tuple-element.41.own_heat), channel_id=1, source_target_pairs={{0,1},{1,0},{2,3},{3,2},{4,5},{5,4},{6,7},{7,6},{8,9},{9,8},{10,11... | collective-permute-start | bytes 49160 | tf_op jit(solution)/shard_map/ppermute | solution.py:382
  9.1 5.5 %collective-permute-start.4 = (f32[8,128]{1,0:T(8,128)S(1)}, f32[8,128]{1,0:T(8,128)S(1)}, u32[]{:S(2)}, u32[]{:S(2)}) collective-permute-start(f32[8,128]{1,0:T(8,128)S(1)} %get-tuple-element.49), channel_id=1, source_target_pairs={{0,4},{4,8},{8,12},{12,0},{1,5},{5,9},{9,13},{13,1},{2,6},{6,10},{... | collective-permute-start | bytes 12296 | tf_op jit(solution)/shard_map/ppermute | solution.py:451
  10.9 3.7 %collective-permute-start.5 = (f32[8,128]{1,0:T(8,128)S(1)}, f32[8,128]{1,0:T(8,128)S(1)}, u32[]{:S(2)}, u32[]{:S(2)}) collective-permute-start(f32[8,128]{1,0:T(8,128)S(1)} %get-tuple-element.49), channel_id=1, source_target_pairs={{4,0},{8,4},{12,8},{0,12},{5,1},{9,5},{13,9},{1,13},{6,2},{10,6},{... | collective-permute-start | bytes 12296 | tf_op jit(solution)/shard_map/ppermute | solution.py:452

commit v5 on v4

--- a/solution.py
+++ b/solution.py
@@ -1,4 +1,3 @@
-import functools
 import math
 
 import jax
@@ -159,9 +158,7 @@
     return jnp.concatenate([hi, mid, lo, hi, tail], axis=0).astype(jnp.bfloat16)
 
 
-def layers_kernel(
-    own_state, absorber, zenith, lit, thickness, coef, weight, left, drops, strips, factor, kappa, spread
-):
+def layers_kernel(absorber, zenith, coef, weight, left, drops, spread):
     species, levels, rows, width = absorber.shape
     terms = coef.shape[1]
     group = species * rows
@@ -207,21 +204,8 @@
             drop = out[:, k * width : (k + 1) * width] - out[:, (k + 1) * width : (k + 2) * width]
             drops[k, pl.ds(start, chunk), :] = drop
 
-    place = lax.broadcasted_iota(jnp.int32, (rows, width), 1)
-    zero = jnp.zeros((rows, width), jnp.float32)
-    for s in range(species):
-        total, sums = zero, [None]
-        for k in range(levels):
-            total = total + absorber[s, k]
-            sums.append(total)
-        strips[s] = to_strips(place, zero, sums)
-    strips[species] = to_strips(place, zero - 1.0, [scale] * (levels + 1))
-    lit_zenith = jnp.where(lit[...] == 1, zenith[...], 0.0)
-    factor[...] = to_strips(place, zero, [lit_zenith / thickness[k] for k in range(levels)])
-    kappa[...] = to_strips(place, zero, [own_state[levels]] * levels)
-
-
-def radiate_kernel(left, drops, upper, zenith, lit, thickness, after, heat):
+
+def radiate_kernel(left, drops, upper, zenith, lit, thickness, heat):
     levels, rows, width = heat.shape
     depth = left.shape[1]
     species = upper.shape[0]
@@ -229,58 +213,34 @@
     below = lax.axis_index("lev") > 0
     totals = [jnp.where(below, upper[s], 0.0) for s in range(species)]
     right = amount_rows(totals, -log2e / zen, depth, 0)
+    lit_zenith = jnp.where(lit[...] == 1, zen, 0.0)
+    factors = [lit_zenith / thickness[k] for k in range(levels)]
     chunk = 448
-    sums = [jnp.zeros((rows, width), jnp.float32) for _ in range(levels)]
+    zero = jnp.zeros((rows, width), jnp.float32)
+    sums = [[zero, zero] for _ in range(levels)]
     for start in range(0, left.shape[0], chunk):
         above = jnp.exp2(
             jnp.dot(left[pl.ds(start, chunk), :], right, preferred_element_type=jnp.float32)
         )
-        for k in range(levels):
-            absorbed = above * drops[k, pl.ds(start, chunk), :]
-            sums[k] = sums[k] + jnp.sum(absorbed.reshape(chunk // rows, rows, width), axis=0)
-    lit_zenith = jnp.where(lit[...] == 1, zen, 0.0)
+        for n, at in enumerate(range(0, chunk, rows)):
+            part = above[at : at + rows]
+            for k in range(levels):
+                drop = drops[k, pl.ds(start + at, rows), :]
+                sums[k][n % 2] = sums[k][n % 2] + part * drop
     for k in range(levels):
-        heat[k] = lit_zenith * sums[k] / thickness[k]
-
-
-def edge_heat_kernel(levels, left, upper, layers, factor, kappa, second, out):
-    species = upper.shape[0]
-    rows, width = factor.shape
+        heat[k] = factors[k] * (sums[k][0] + sums[k][1])
+
+
+def edge_kernel(own_heat, other_heat, second, kappa, fixed, edge):
+    levels, rows, width = own_heat.shape
     stencil = Stencil(rows, width)
-    lane = stencil.lane
-    below = lax.axis_index("lev") > 0
-    totals = []
-    for s in range(species):
-        above = jnp.where(below & (lane < strip), pltpu.roll(upper[s], points, 1), 0.0)
-        total = layers[s] + above
-        for k in range(1, levels + 1):
-            total = total + pltpu.roll(above, strip * k, 1)
-        totals.append(total)
-    right = amount_rows(totals, layers[species], left.shape[1], 3)
-    passed = jnp.exp2(jnp.dot(left[...], right, preferred_element_type=jnp.float32))
-    passed = sum_rows(passed, rows)
-    heat = factor[...] * (passed - pltpu.roll(passed, width - strip, 1))
-    out[...] = stencil.residual(heat, kappa[...]) + jnp.where(lane < width // 2, second[...], 0.0)
-
-
-def sum_rows(value, rows):
-    parts = [value[i : i + rows] for i in range(0, value.shape[0], rows)]
-    sums = parts[:8]
-    for i in range(8, len(parts)):
-        sums[i % 8] = sums[i % 8] + parts[i]
-    while len(sums) > 1:
-        sums = [sum(sums[i : i + 2]) for i in range(0, len(sums), 2)]
-    return sums[0]
-
-
-def join_kernel(own, other, fixed, heat, edge, heat_out):
-    rows, width = own.shape
-    stencil = Stencil(rows, width)
-    r = own[...] + pltpu.roll(other[...], width // 2, 1)
+    heats = [own_heat[k] for k in range(levels)] + [None] * (8 - levels)
+    heats = heats + [other_heat[k] for k in range(levels)]
+    strips = to_strips(stencil.lane, jnp.zeros((rows, width), jnp.float32), heats)
+    r = second[...] + stencil.residual(strips, kappa[...])
     joined = stencil.rows_joined(r, pltpu.roll(r, width // 2, 1))
     node = stencil.lane % strip
     edge[...] = jnp.where((node == points - 1) | (node == points), joined, fixed[...])
-    heat_out[...] = heat[...]
 
 
 def tiles_of(field):
@@ -401,7 +361,6 @@
         compiler_params=pltpu.CompilerParams(vmem_limit_bytes=32 * 1024 * 1024),
         name="fetch",
     )(*args)
-    species = absorber.shape[0]
     size = lax.axis_size("lev")
     lev = lax.axis_index("lev")
     upper = None
@@ -414,19 +373,20 @@
         upper = jnp.zeros_like(amount)
     other_state = swap(own_state, "sub", [(0, 1)])
     plane = jax.ShapeDtypeStruct((rows, width), jnp.float32)
-    left, drops, strips, factor, kappa = pl.pallas_call(
+    left, drops = pl.pallas_call(
         layers_kernel,
         out_shape=(
             jax.ShapeDtypeStruct((terms * rows, 256), jnp.bfloat16),
             jax.ShapeDtypeStruct((levels, terms * rows, width), jnp.float32),
-            tile(species + 1),
-            plane,
-            plane,
         ),
         scratch_shapes=[pltpu.VMEM((terms, 256), jnp.float32)],
         compiler_params=big,
         name="layers",
-    )(own_state, absorber, cos_zenith, sunlit, thickness, absorb_coef, weight)
+    )(absorber, cos_zenith, absorb_coef, weight)
+    own_heat = pl.pallas_call(
+        radiate_kernel, out_shape=tile(levels), compiler_params=big, name="radiate"
+    )(left, drops, upper, cos_zenith, sunlit, thickness)
+    other_heat = swap(own_heat, "sub", [(0, 1)])
     pair = jax.ShapeDtypeStruct((levels, 2, rows, width), jnp.float32)
     first_tend, second, span, second_strips, kappa_strips, fixed, mine = pl.pallas_call(
         state_kernel,
@@ -434,23 +394,12 @@
         compiler_params=big,
         name="state",
     )(own_state, other_state)
-    own_r = pl.pallas_call(
-        functools.partial(edge_heat_kernel, levels),
-        out_shape=plane,
-        compiler_params=big,
-        name="edge_heat",
-    )(left, upper, strips, factor, kappa, second_strips)
-    other_r = swap(own_r, "sub", [(0, 1)])
-    own_heat = pl.pallas_call(
-        radiate_kernel, out_shape=tile(levels), compiler_params=big, name="radiate"
-    )(left, drops, upper, cos_zenith, sunlit, thickness, own_r)
-    edge, own_heat = pl.pallas_call(
-        join_kernel, out_shape=(plane, tile(levels)), compiler_params=big, name="join"
-    )(own_r, other_r, fixed, own_heat)
+    edge = pl.pallas_call(edge_kernel, out_shape=plane, compiler_params=big, name="edges")(
+        own_heat, other_heat, second_strips, kappa_strips, fixed
+    )
     wide = lax.axis_size("wide")
     from_before = lax.ppermute(edge, "wide", [(i, (i + 1) % wide) for i in range(wide)])
     from_after = lax.ppermute(edge, "wide", [((i + 1) % wide, i) for i in range(wide)])
-    other_heat = swap(own_heat, "sub", [(0, 1)])
     heat, base = pl.pallas_call(
         base_kernel, out_shape=(tile(levels), tile(levels)), compiler_params=big, name="base"
     )(own_state, other_state, own_heat, other_heat, first_tend, second)

time: 15.6 us -> 15.4 us (0.987)
  waiting for transfers between devices: 1.19 us -> 2.01 us
  Pallas kernels: 5.89 us -> 5.3 us
  starting transfers between devices: 7.67 us -> 7.26 us
    ppermute x3 -> x2, starting transfers between devices: 0.8 us -> 0.07 us  [swap(): return lax.ppermute(value, axis, route)]
    ppermute x1, waiting for transfers between devices: 0.03 us -> 0.74 us  [shards(): lax.ppermute(amount, 'lev', [(i, (i + step) % size) for i in range(size)])]
    pallas_call x2 -> x1, Pallas kernels: 0.95 us -> 0.3 us  [shards(): pl.pallas_call(edge_kernel, out_shape=plane, compiler_params=big, name='e...]
    ppermute x1, starting transfers between devices: 1.84 us -> 2.1 us  [shards(): lax.ppermute(edge, 'wide', [(i, (i + 1) % wide) for i in range(wide)])]
    ppermute x3 -> x2, waiting for transfers between devices: 0.38 us -> 0.53 us  [swap(): return lax.ppermute(value, axis, route)]
  transfers between devices with their start and end apart: 6 -> 5, of which waited for: 3 -> 3; matrix products, arithmetic and copies ran while one was open for 0% -> 0% of each run, Pallas kernels for 20% -> 21%
where the time goes in v5:
time: 15.4 us; the launch traced here: 15.2 us
  starting transfers between devices  7.26 us (47%)
  Pallas kernels  5.3 us (34%)
  waiting for transfers between devices  2.01 us (13%)
  between operations  0.68 us (4%)
    ppermute x1, starting transfers between devices, shards(): lax.ppermute(amount, 'lev', [(i, (i + step) % size) for i in range(size)])  3 us
    ppermute x1, starting transfers between devices, shards(): lax.ppermute(edge, 'wide', [(i, (i + 1) % wide) for i in range(wide)])  2.1 us
    ppermute x1, starting transfers between devices, shards(): lax.ppermute(edge, 'wide', [((i + 1) % wide, i) for i in range(wide)])  2.07 us
    pallas_call x1, Pallas kernels, shards(): pl.pallas_call(layers_kernel, out_shape=(jax.ShapeDtypeStruct((terms * ro...  1.1 us
    pallas_call x1, Pallas kernels, shards(): pl.pallas_call(fetch_kernel, out_shape=(tile(absorber.shape[0]), tile(lev...  0.99 us
    pallas_call x1, Pallas kernels, shards(): pl.pallas_call(step_kernel, out_shape=tile(levels), compiler_params=big,...  0.86 us
    pallas_call x1, Pallas kernels, shards(): pl.pallas_call(base_kernel, out_shape=(tile(levels), tile(levels)), compi...  0.84 us
    ppermute x1, waiting for transfers between devices, shards(): lax.ppermute(amount, 'lev', [(i, (i + step) % size) for i in range(size)])  0.74 us
  transfers between devices with their start and end apart: 5, of which 3 were waited for; matrix products, arithmetic and copies ran while one was open for 0% of the time, Pallas kernels for 21%

profile of v5, /device:TPU:0, one launch (start us, length us, event | category | flops | bytes accessed | tf_op | source)
XLA Modules:
  0.0 15.2 jit_solution(2104768272051069948)
XLA Ops:
  0.6 1.0 %fetch.1 = (f32[7,8,128]{2,1,0:T(8,128)S(1)}, f32[5,8,128]{2,1,0:T(8,128)S(1)}, f32[7,4,8,128]{3,2,1,0:T(8,128)S(1)}, f32[4,8,128]{2,1,0:T(8,128)S(1)}, f32[8,12...) custom-call(f32[4,8,128]{2,1,0:T(8,128)} %refs_0_.1, f32[8,128]{1,0:T(8,128)} %refs_1_.1, ...), custom_call_target="tpu_custom_call" | custom-call | tf_op jit(solution)/shard_map/fetch/pallas_call | solution.py:356
  1.6 3.0 %collective-permute-start.1 = (f32[7,8,128]{2,1,0:T(8,128)S(1)}, f32[7,8,128]{2,1,0:T(8,128)S(1)}, u32[]{:S(2)}, u32[]{:S(2)}) collective-permute-start(f32[7,8,128]{2,1,0:T(8,128)S(1)} %get-tuple-element.28), channel_id=1, source_target_pairs={{0,2},{2,0},{1,3},{3,1},{4,6},{6,4},{5,7},{7,5},{8,10},{10,8},{9,1... | collective-permute-start | bytes 86024 | tf_op jit(solution)/shard_map/ppermute | solution.py:368
  4.6 0.0 collective-permute-start
  4.6 1.1 %layers.1 = (bf16[1792,256]{1,0:T(8,128)(2,1)S(1)}, f32[4,1792,128]{2,1,0:T(8,128)S(1)}) custom-call(f32[7,4,8,128]{3,2,1,0:T(8,128)S(1)} %get-tuple-element.22.absorber, f32[8,128]{1,0:T(8,128)S(1)} %get-tuple-element.23.zenith, f32[7,224]{1,0:T(8,128)S(1)} %get-tuple-element.24.coef, f32[1,224]{1,0:T(1,128)S(1)} %get-tuple-element.25.weight), custom_call_target="tpu_custom_call" | custom-call | tf_op jit(solution)/shard_map/layers/pallas_call | solution.py:376
  5.7 0.7 %collective-permute-done.1.upper = f32[7,8,128]{2,1,0:T(8,128)S(1)} collective-permute-done((f32[7,8,128]{2,1,0:T(8,128)S(1)}, f32[7,8,128]{2,1,0:T(8,128)S(1)}, u32[]{:S(2)}, u32[]{:S(2)}) %collective-permute-start.1) | collective-permute-done | bytes 28704 | tf_op jit(solution)/shard_map/ppermute | solution.py:368
  6.5 0.6 %radiate.1.own_heat = f32[4,8,128]{2,1,0:T(8,128)S(1)} custom-call(bf16[1792,256]{1,0:T(8,128)(2,1)S(1)} %get-tuple-element.26.left, f32[4,1792,128]{2,1,0:T(8,128)S(1)} %get-tuple-element.27.drops, f32[7,8,128]{2,1,0:T(8,128)S(1)} %collective-permute-done.1.upper, f32[8,128]{1,0:T(8,128)S(1)} %get-tuple-element.23.zenith, ...), custom_call_target="tpu_custom_call" | custom-call | tf_op jit(solution)/shard_map/radiate/pallas_call | solution.py:386
  7.1 0.1 collective-permute-start.2
  7.2 0.0 collective-permute-done.other_state
  7.2 0.6 %state.1 = (f32[4,8,128]{2,1,0:T(8,128)S(1)}, f32[4,2,8,128]{3,2,1,0:T(8,128)S(1)}, f32[2,8,128]{2,1,0:T(8,128)S(1)}, f32[8,128]{1,0:T(8,128)S(1)}, f32[8,128]{1...) custom-call(f32[5,8,128]{2,1,0:T(8,128)S(1)} %get-tuple-element.21.own_state, ...), custom_call_target="tpu_custom_call" | custom-call | tf_op jit(solution)/shard_map/state/pallas_call | solution.py:391
  7.8 0.5 %collective-permute-done.2.other_heat = f32[4,8,128]{2,1,0:T(8,128)S(1)} collective-permute-done((f32[4,8,128]{2,1,0:T(8,128)S(1)}, f32[4,8,128]{2,1,0:T(8,128)S(1)}, u32[]{:S(2)}, u32[]{:S(2)}) %collective-permute-start.2) | collective-permute-done | bytes 16416 | tf_op jit(solution)/shard_map/ppermute | solution.py:342
  8.3 0.3 %edges.1 = f32[8,128]{1,0:T(8,128)S(1)} custom-call(f32[4,8,128]{2,1,0:T(8,128)S(1)} %radiate.1.own_heat, f32[4,8,128]{2,1,0:T(8,128)S(1)} %collective-permute-done.2.other_heat, f32[8,128]{1,0:T(8,128)S(1)} %get-tuple-element.38.second, f32[8,128]{1,0:T(8,128)S(1)} %get-tuple-element.36.kappa, f32[8,128]{1,0:T(8,128)S(1)} %get-tuple-element.39.fixed), custom_call_target="tpu_custom_call" | custom-call | tf_op jit(solution)/shard_map/edges/pallas_call | solution.py:397
  8.6 2.1 %collective-permute-start.3 = (f32[8,128]{1,0:T(8,128)S(1)}, f32[8,128]{1,0:T(8,128)S(1)}, u32[]{:S(2)}, u32[]{:S(2)}) collective-permute-start(f32[8,128]{1,0:T(8,128)S(1)} %edges.1), channel_id=1, source_target_pairs={{0,4},{4,8},{8,12},{12,0},{1,5},{5,9},{9,13},{13,1},{2,6},{6,10},{... | collective-permute-start | bytes 12296 | tf_op jit(solution)/shard_map/ppermute | solution.py:401
  10.7 2.1 %collective-permute-start.4 = (f32[8,128]{1,0:T(8,128)S(1)}, f32[8,128]{1,0:T(8,128)S(1)}, u32[]{:S(2)}, u32[]{:S(2)}) collective-permute-start(f32[8,128]{1,0:T(8,128)S(1)} %edges.1), channel_id=1, source_target_pairs={{4,0},{8,4},{12,8},{0,12},{5,1},{9,5},{13,9},{1,13},{6,2},{10,6},{... | collective-permute-start | bytes 12296 | tf_op jit(solution)/shard_map/ppermute | solution.py:402
  12.8 0.8 %base.1 = (f32[4,8,128]{2,1,0:T(8,128)}, f32[4,8,128]{2,1,0:T(8,128)S(1)}) custom-call(f32[5,8,128]{2,1,0:T(8,128)S(1)} %get-tuple-element.21.own_state, f32[5,8,128]{2,1,0:T(8,128)S(1)} %collective-permute-done.other_state, f32[4,8,128]{2,1,0:T(8,128)S(1)} %radiate.1.own_heat, f32[4,8,128]{2,1,0:T(8,128)S(1)} %collective-permute-done.2.other_heat, ...), custom_call_target="tpu_custom_call" | custom-call | tf_op jit(solution)/shard_map/base/pallas_call | solution.py:403
  13.6 0.7 %collective-permute-done.3.from_before = f32[8,128]{1,0:T(8,128)S(1)} collective-permute-done((f32[8,128]{1,0:T(8,128)S(1)}, f32[8,128]{1,0:T(8,128)S(1)}, u32[]{:S(2)}, u32[]{:S(2)}) %collective-permute-start.3) | collective-permute-done | bytes 4128 | tf_op jit(solution)/shard_map/ppermute | solution.py:401
  14.4 0.0 collective-permute-done.4.from_after
  14.4 0.9 %step.1 = f32[4,8,128]{2,1,0:T(8,128)} custom-call(f32[4,8,128]{2,1,0:T(8,128)S(1)} %get-tuple-element.34.base, f32[2,8,128]{2,1,0:T(8,128)S(1)} %get-tuple-element.35.span, f32[8,128]{1,0:T(8,128)S(1)} %get-tuple-element.36.kappa, f32[2,8,128]{2,1,0:T(8,128)S(1)} %get-tuple-element.37.mine, f32[8,128]{1,0:T(8,128)S(1)} %collective-permute-done.3.from_before, ...), custom_call_target="tpu_custom_call" | custom-call | tf_op jit(solution)/shard_map/step/pallas_call | solution.py:406
Async XLA Ops:
  1.6 4.9 %collective-permute-start.1 = (f32[7,8,128]{2,1,0:T(8,128)S(1)}, f32[7,8,128]{2,1,0:T(8,128)S(1)}, u32[]{:S(2)}, u32[]{:S(2)}) collective-permute-start(f32[7,8,128]{2,1,0:T(8,128)S(1)} %get-tuple-element.28), channel_id=1, source_target_pairs={{0,2},{2,0},{1,3},{3,1},{4,6},{6,4},{5,7},{7,5},{8,10},{10,8},{9,1... | collective-permute-start | bytes 86024 | tf_op jit(solution)/shard_map/ppermute | solution.py:368
  4.6 2.5 %collective-permute-start = (f32[5,8,128]{2,1,0:T(8,128)S(1)}, f32[5,8,128]{2,1,0:T(8,128)S(1)}, u32[]{:S(2)}, u32[]{:S(2)}) collective-permute-start(f32[5,8,128]{2,1,0:T(8,128)S(1)} %get-tuple-element.21.own_state), channel_id=1, source_target_pairs={{0,1},{1,0},{2,3},{3,2},{4,5},{5,4},{6,7},{7,6},{8,9},{9,8},{10,11... | collective-permute-start | bytes 61448 | tf_op jit(solution)/shard_map/ppermute | solution.py:342
  7.1 1.2 %collective-permute-start.2 = (f32[4,8,128]{2,1,0:T(8,128)S(1)}, f32[4,8,128]{2,1,0:T(8,128)S(1)}, u32[]{:S(2)}, u32[]{:S(2)}) collective-permute-start(f32[4,8,128]{2,1,0:T(8,128)S(1)} %radiate.1.own_heat), channel_id=1, source_target_pairs={{0,1},{1,0},{2,3},{3,2},{4,5},{5,4},{6,7},{7,6},{8,9},{9,8},{10,11... | collective-permute-start | bytes 49160 | tf_op jit(solution)/shard_map/ppermute | solution.py:342
  8.6 5.8 %collective-permute-start.3 = (f32[8,128]{1,0:T(8,128)S(1)}, f32[8,128]{1,0:T(8,128)S(1)}, u32[]{:S(2)}, u32[]{:S(2)}) collective-permute-start(f32[8,128]{1,0:T(8,128)S(1)} %edges.1), channel_id=1, source_target_pairs={{0,4},{4,8},{8,12},{12,0},{1,5},{5,9},{9,13},{13,1},{2,6},{6,10},{... | collective-permute-start | bytes 12296 | tf_op jit(solution)/shard_map/ppermute | solution.py:401
  10.7 3.7 %collective-permute-start.4 = (f32[8,128]{1,0:T(8,128)S(1)}, f32[8,128]{1,0:T(8,128)S(1)}, u32[]{:S(2)}, u32[]{:S(2)}) collective-permute-start(f32[8,128]{1,0:T(8,128)S(1)} %edges.1), channel_id=1, source_target_pairs={{4,0},{8,4},{12,8},{0,12},{5,1},{9,5},{13,9},{1,13},{6,2},{10,6},{... | collective-permute-start | bytes 12296 | tf_op jit(solution)/shard_map/ppermute | solution.py:402

commit v6 on v5

--- a/solution.py
+++ b/solution.py
@@ -1,3 +1,4 @@
+import functools
 import math
 
 import jax
@@ -126,12 +127,13 @@
 
 def fetch_kernel(*refs):
     air, diffusivity, absorber, thickness, zenith, lit, coef, weight = refs[:8]
-    amount, state, absorber_out, thickness_out, zenith_out, lit_out, coef_out, weight_out, sems = refs[8:]
+    amount, packet, absorber_out, thickness_out, zenith_out, lit_out, coef_out, weight_out = refs[8:16]
+    packed, sems = refs[16:]
     levels = air.shape[0]
     copies = [
         pltpu.make_async_copy(absorber, absorber_out, sems.at[0]),
-        pltpu.make_async_copy(air, state.at[pl.ds(0, levels)], sems.at[1]),
-        pltpu.make_async_copy(diffusivity, state.at[levels], sems.at[2]),
+        pltpu.make_async_copy(air, packet.at[pl.ds(0, levels)], sems.at[1]),
+        pltpu.make_async_copy(diffusivity, packet.at[levels], sems.at[2]),
         pltpu.make_async_copy(zenith, zenith_out, sems.at[3]),
         pltpu.make_async_copy(coef, coef_out, sems.at[4]),
         pltpu.make_async_copy(weight, weight_out, sems.at[5]),
@@ -142,11 +144,27 @@
         copy.start()
     for copy in copies:
         copy.wait()
-    for s in range(absorber_out.shape[0]):
+    species = absorber_out.shape[0]
+    lane = lax.broadcasted_iota(jnp.int32, packed.shape, 1)
+    zero = jnp.zeros(packed.shape, jnp.float32)
+    raw = levels + 1
+    totals = []
+    for s in range(species):
         total = absorber_out[s, 0]
+        sums = [None, total]
         for k in range(1, levels):
             total = total + absorber_out[s, k]
+            sums.append(total)
         amount[s] = total
+        totals.append(total)
+        packet[raw + s] = to_strips(lane, zero, sums)
+    packed[...] = to_strips(lane, zero, totals)
+    zen = zenith_out[...]
+    packet[raw + species] = to_strips(lane, zero - 1.0, [-log2e / zen] * (levels + 1))
+    lit_zenith = jnp.where(lit_out[...] == 1, zen, 0.0)
+    packet[raw + species + 1] = to_strips(
+        lane, zero, [lit_zenith / thickness_out[k] for k in range(levels)]
+    )
 
 
 def amount_rows(totals, scale, depth, ones):
@@ -205,7 +223,7 @@
             drops[k, pl.ds(start, chunk), :] = drop
 
 
-def radiate_kernel(left, drops, upper, zenith, lit, thickness, heat):
+def radiate_kernel(left, drops, upper, zenith, lit, thickness, after, heat):
     levels, rows, width = heat.shape
     depth = left.shape[1]
     species = upper.shape[0]
@@ -231,15 +249,40 @@
         heat[k] = factors[k] * (sums[k][0] + sums[k][1])
 
 
-def edge_kernel(own_heat, other_heat, second, kappa, fixed, edge):
-    levels, rows, width = own_heat.shape
+def sum_rows(value, rows):
+    parts = [value[i : i + rows] for i in range(0, value.shape[0], rows)]
+    sums = parts[:8]
+    for i in range(8, len(parts)):
+        sums[i % 8] = sums[i % 8] + parts[i]
+    while len(sums) > 1:
+        sums = [sum(sums[i : i + 2]) for i in range(0, len(sums), 2)]
+    return sums[0]
+
+
+def edge_kernel(levels, upper, upper_other, left, layers, factor, second, kappa, fixed, edge):
+    species = upper.shape[0]
+    rows, width = factor.shape
+    half = width // 2
     stencil = Stencil(rows, width)
-    heats = [own_heat[k] for k in range(levels)] + [None] * (8 - levels)
-    heats = heats + [other_heat[k] for k in range(levels)]
-    strips = to_strips(stencil.lane, jnp.zeros((rows, width), jnp.float32), heats)
-    r = second[...] + stencil.residual(strips, kappa[...])
-    joined = stencil.rows_joined(r, pltpu.roll(r, width // 2, 1))
-    node = stencil.lane % strip
+    lane = stencil.lane
+    below = lax.axis_index("lev") > 0
+    crossed = upper_other[...]
+    totals = []
+    for s in range(species):
+        other = pltpu.roll(crossed, (half - strip * s) % width, 1)
+        above = jnp.where(below & (lane < strip), pltpu.roll(upper[s], points, 1), 0.0)
+        above = jnp.where(below & (lane >= half) & (lane < half + strip), other, above)
+        total = layers[s] + above
+        for k in range(1, levels + 1):
+            total = total + pltpu.roll(above, strip * k, 1)
+        totals.append(total)
+    right = amount_rows(totals, layers[species], left.shape[1], 3)
+    passed = jnp.exp2(jnp.dot(left[...], right, preferred_element_type=jnp.float32))
+    passed = sum_rows(passed, rows)
+    heat = factor[...] * (passed - pltpu.roll(passed, width - strip, 1))
+    r = second[...] + stencil.residual(heat, kappa[...])
+    joined = stencil.rows_joined(r, pltpu.roll(r, half, 1))
+    node = lane % strip
     edge[...] = jnp.where((node == points - 1) | (node == points), joined, fixed[...])
 
 
@@ -248,11 +291,20 @@
     return [t for n in range(2) for t in [field[l, n] for l in range(field.shape[0])] + gap]
 
 
-def state_kernel(own_state, other_state, first_tend, second, span_out, second_strips, kappa_strips, fixed, mine):
-    levels = own_state.shape[0] - 1
+def state_kernel(
+    own_state, other_state, first_tend, second, span_out, second_strips, kappa_strips, fixed, mine, layers, factor
+):
+    species = layers.shape[0] - 1
+    levels = own_state.shape[0] - species - 3
     rows, width = own_state.shape[1:]
     stencil = Stencil(rows, width)
     lane = stencil.lane
+    for i in range(species + 1):
+        at = levels + 1 + i
+        other = pltpu.roll(other_state[at], width // 2, 1)
+        layers[i] = jnp.where(lane < width // 2, own_state[at], other)
+    at = levels + species + 2
+    factor[...] = own_state[at] + pltpu.roll(other_state[at], width // 2, 1)
     zero = jnp.zeros((rows, width), jnp.float32)
     air = jnp.stack([own_state[:levels], other_state[:levels]], axis=1)
     kappa = jnp.stack([own_state[levels], other_state[levels]], axis=0)
@@ -287,11 +339,10 @@
     mine[1] = stencil.weight_y * stencil.apply("d", 0, change)
 
 
-def base_kernel(own_state, other_state, own_heat, other_heat, first_tend, second, heat_out, base):
+def base_kernel(own_state, other_state, own_heat, other_heat, first_tend, second, base):
     levels, rows, width = own_heat.shape
     stencil = Stencil(rows, width)
     own = own_heat[...]
-    heat_out[...] = own
     heat = jnp.stack([own, other_heat[...]], axis=1)
     kappa = jnp.stack([own_state[levels], other_state[levels]], axis=0)
     r = second[...] + stencil.residual(heat, kappa)
@@ -303,11 +354,12 @@
     )
 
 
-def step_kernel(base, span, kappa, mine, from_before, from_after, out):
+def step_kernel(from_before, from_after, span, kappa, mine, base, heat, heat_out, out):
     levels, rows, width = base.shape
     half = width // 2
     stencil = Stencil(rows, width)
     lane = stencil.lane
+    heat_out[...] = heat[...]
     before, after = from_before[...], from_after[...]
     at_first = lane % strip == points
 
@@ -353,26 +405,34 @@
     args = (air_state, diffusivity, absorber, thickness, cos_zenith, sunlit, absorb_coef, weight)
     args = tuple(pltpu.with_memory_space_constraint(x, pltpu.HBM) for x in args)
     same = lambda x: jax.ShapeDtypeStruct(x.shape, x.dtype)
-    amount, own_state, absorber, thickness, cos_zenith, sunlit, absorb_coef, weight = pl.pallas_call(
+    plane = jax.ShapeDtypeStruct((rows, width), jnp.float32)
+    fetched = pl.pallas_call(
         fetch_kernel,
-        out_shape=(tile(absorber.shape[0]), tile(levels + 1)) + tuple(same(x) for x in args[2:]),
+        out_shape=(tile(absorber.shape[0]), tile(levels + absorber.shape[0] + 3)) + tuple(same(x) for x in args[2:])
+        + (plane,),
         in_specs=[pl.BlockSpec(memory_space=pltpu.HBM)] * len(args),
         scratch_shapes=[pltpu.SemaphoreType.DMA((len(args),))],
         compiler_params=pltpu.CompilerParams(vmem_limit_bytes=32 * 1024 * 1024),
         name="fetch",
     )(*args)
+    amount, packet, absorber, thickness, cos_zenith, sunlit, absorb_coef, weight, packed = fetched
+    species = absorber.shape[0]
     size = lax.axis_size("lev")
     lev = lax.axis_index("lev")
-    upper = None
+    upper = upper_other = None
     for step in range(1, size):
-        moved = lax.ppermute(amount, "lev", [(i, (i + step) % size) for i in range(size)])
+        straight = [(i, (i + step) % size) for i in range(size)]
+        crossed = [(2 * i + c, 2 * j + 1 - c) for i, j in straight for c in range(2)]
+        moved = lax.ppermute(amount, "lev", straight)
+        moved_other = lax.ppermute(packed, ("lev", "sub"), crossed)
         if size > 2:
             moved = jnp.where(lev >= step, moved, 0.0)
+            moved_other = jnp.where(lev >= step, moved_other, 0.0)
         upper = moved if upper is None else upper + moved
+        upper_other = moved_other if upper_other is None else upper_other + moved_other
     if upper is None:
-        upper = jnp.zeros_like(amount)
-    other_state = swap(own_state, "sub", [(0, 1)])
-    plane = jax.ShapeDtypeStruct((rows, width), jnp.float32)
+        upper, upper_other = jnp.zeros_like(amount), jnp.zeros_like(packed)
+    other_packet = swap(packet, "sub", [(0, 1)])
     left, drops = pl.pallas_call(
         layers_kernel,
         out_shape=(
@@ -383,29 +443,29 @@
         compiler_params=big,
         name="layers",
     )(absorber, cos_zenith, absorb_coef, weight)
-    own_heat = pl.pallas_call(
-        radiate_kernel, out_shape=tile(levels), compiler_params=big, name="radiate"
-    )(left, drops, upper, cos_zenith, sunlit, thickness)
-    other_heat = swap(own_heat, "sub", [(0, 1)])
     pair = jax.ShapeDtypeStruct((levels, 2, rows, width), jnp.float32)
-    first_tend, second, span, second_strips, kappa_strips, fixed, mine = pl.pallas_call(
+    first_tend, second, span, second_strips, kappa_strips, fixed, mine, strips, factor = pl.pallas_call(
         state_kernel,
-        out_shape=(tile(levels), pair, tile(2), plane, plane, plane, tile(2)),
+        out_shape=(tile(levels), pair, tile(2), plane, plane, plane, tile(2), tile(species + 1), plane),
         compiler_params=big,
         name="state",
-    )(own_state, other_state)
-    edge = pl.pallas_call(edge_kernel, out_shape=plane, compiler_params=big, name="edges")(
-        own_heat, other_heat, second_strips, kappa_strips, fixed
-    )
+    )(packet, other_packet)
+    edge = pl.pallas_call(
+        functools.partial(edge_kernel, levels), out_shape=plane, compiler_params=big, name="edges"
+    )(upper, upper_other, left, strips, factor, second_strips, kappa_strips, fixed)
     wide = lax.axis_size("wide")
     from_before = lax.ppermute(edge, "wide", [(i, (i + 1) % wide) for i in range(wide)])
     from_after = lax.ppermute(edge, "wide", [((i + 1) % wide, i) for i in range(wide)])
-    heat, base = pl.pallas_call(
-        base_kernel, out_shape=(tile(levels), tile(levels)), compiler_params=big, name="base"
-    )(own_state, other_state, own_heat, other_heat, first_tend, second)
-    new_state = pl.pallas_call(
-        step_kernel, out_shape=tile(levels), compiler_params=big, name="step"
-    )(base, span, kappa_strips, mine, from_before, from_after)
+    own_heat = pl.pallas_call(
+        radiate_kernel, out_shape=tile(levels), compiler_params=big, name="radiate"
+    )(left, drops, upper, cos_zenith, sunlit, thickness, edge)
+    other_heat = swap(own_heat, "sub", [(0, 1)])
+    base = pl.pallas_call(
+        base_kernel, out_shape=tile(levels), compiler_params=big, name="base"
+    )(packet, other_packet, own_heat, other_heat, first_tend, second)
+    heat, new_state = pl.pallas_call(
+        step_kernel, out_shape=(tile(levels), tile(levels)), compiler_params=big, name="step"
+    )(from_before, from_after, span, kappa_strips, mine, base, own_heat)
     return (heat, new_state)
 
 

time: 15.4 us -> 16 us (1.039)
  waiting for transfers between devices: 2.01 us -> 2.47 us
  Pallas kernels: 5.3 us -> 5.48 us
    ppermute x2, starting transfers between devices: 0.07 us -> 0.74 us  [swap(): return lax.ppermute(value, axis, route)]
    ppermute x1, starting transfers between devices: 2.1 us -> 1.58 us  [shards(): lax.ppermute(edge, 'wide', [(i, (i + 1) % wide) for i in range(wide)])]
    ppermute x2, waiting for transfers between devices: 0.53 us -> 0.01 us  [swap(): return lax.ppermute(value, axis, route)]
    ppermute x1, waiting for transfers between devices: 0.74 us -> 1.26 us  [shards(): lax.ppermute(edge, 'wide', [(i, (i + 1) % wide) for i in range(wide)])]
    ppermute x1 -> x2, waiting for transfers between devices: 0.74 us -> 1.21 us  [the longest x1 1.2 us: shards(): moved_other = lax.ppermute(packed, ('lev', 'sub'), crossed)]
    ppermute x1 -> x2, starting transfers between devices: 3 us -> 2.63 us  [the longest x1 2.56 us: shards(): moved = lax.ppermute(amount, 'lev', straight)]
    ppermute x1, starting transfers between devices: 2.07 us -> 2.24 us  [shards(): lax.ppermute(edge, 'wide', [((i + 1) % wide, i) for i in range(wide)])]
  transfers between devices with their start and end apart: 5 -> 6, of which waited for: 3 -> 2; matrix products, arithmetic and copies ran while one was open for 0% -> 0% of each run, Pallas kernels for 21% -> 13%
where the time goes in v6:
time: 16 us; the launch traced here: 15.8 us
  starting transfers between devices  7.2 us (45%)
  Pallas kernels  5.48 us (34%)
  waiting for transfers between devices  2.47 us (15%)
  between operations  0.68 us (4%)
    ppermute x1, starting transfers between devices, shards(): moved = lax.ppermute(amount, 'lev', straight)  2.56 us
    ppermute x1, starting transfers between devices, shards(): lax.ppermute(edge, 'wide', [((i + 1) % wide, i) for i in range(wide)])  2.24 us
    ppermute x1, starting transfers between devices, shards(): lax.ppermute(edge, 'wide', [(i, (i + 1) % wide) for i in range(wide)])  1.58 us
    ppermute x1, waiting for transfers between devices, shards(): lax.ppermute(edge, 'wide', [(i, (i + 1) % wide) for i in range(wide)])  1.26 us
    ppermute x1, waiting for transfers between devices, shards(): moved_other = lax.ppermute(packed, ('lev', 'sub'), crossed)  1.2 us
    pallas_call x1, Pallas kernels, shards(): pl.pallas_call(fetch_kernel, out_shape=(tile(absorber.shape[0]), tile(lev...  1.1 us
    pallas_call x1, Pallas kernels, shards(): pl.pallas_call(layers_kernel, out_shape=(jax.ShapeDtypeStruct((terms * ro...  1.09 us
    pallas_call x1, Pallas kernels, shards(): pl.pallas_call(functools.partial(edge_kernel, levels), out_shape=plane, c...  0.88 us
  transfers between devices with their start and end apart: 6, of which 2 were waited for; matrix products, arithmetic and copies ran while one was open for 0% of the time, Pallas kernels for 13%

profile of v6, /device:TPU:0, one launch (start us, length us, event | category | flops | bytes accessed | tf_op | source)
XLA Modules:
  0.0 15.8 jit_solution(5789798417483517081)
XLA Ops:
  0.6 1.1 %fetch.1 = (f32[7,8,128]{2,1,0:T(8,128)S(1)}, f32[14,8,128]{2,1,0:T(8,128)S(1)}, f32[7,4,8,128]{3,2,1,0:T(8,128)S(1)}, f32[4,8,128]{2,1,0:T(8,128)S(1)}, f32[8,1...) custom-call(f32[4,8,128]{2,1,0:T(8,128)} %refs_0_.1, ...), custom_call_target="tpu_custom_call" | custom-call | tf_op jit(solution)/shard_map/fetch/pallas_call | solution.py:409
  1.7 0.5 %collective-permute-start.2 = (f32[14,8,128]{2,1,0:T(8,128)S(1)}, f32[14,8,128]{2,1,0:T(8,128)S(1)}, u32[]{:S(2)}, u32[]{:S(2)}) collective-permute-start(f32[14,8,128]{2,1,0:T(8,128)S(1)} %get-tuple-element.29.own_state), channel_id=1, source_target_pairs={{0,1},{1,0},{2,3},{3,2},{4,5},{5,4},{6,7},{7,6},{8,9},{9,8},{10,11... | collective-permute-start | bytes 172040 | tf_op jit(solution)/shard_map/ppermute | solution.py:394
  2.3 2.6 %collective-permute-start = (f32[7,8,128]{2,1,0:T(8,128)S(1)}, f32[7,8,128]{2,1,0:T(8,128)S(1)}, u32[]{:S(2)}, u32[]{:S(2)}) collective-permute-start(f32[7,8,128]{2,1,0:T(8,128)S(1)} %get-tuple-element.22), channel_id=1, source_target_pairs={{0,2},{2,0},{1,3},{3,1},{4,6},{6,4},{5,7},{7,5},{8,10},{10,8},{9,1... | collective-permute-start | bytes 86024 | tf_op jit(solution)/shard_map/ppermute | solution.py:426
  4.8 0.1 collective-permute-start.1
  4.9 1.1 %layers.1 = (bf16[1792,256]{1,0:T(8,128)(2,1)S(1)}, f32[4,1792,128]{2,1,0:T(8,128)S(1)}) custom-call(f32[7,4,8,128]{3,2,1,0:T(8,128)S(1)} %get-tuple-element.24.absorber, f32[8,128]{1,0:T(8,128)S(1)} %get-tuple-element.25.zenith, f32[7,224]{1,0:T(8,128)S(1)} %get-tuple-element.26.coef, f32[1,224]{1,0:T(1,128)S(1)} %get-tuple-element.27.weight), custom_call_target="tpu_custom_call" | custom-call | tf_op jit(solution)/shard_map/layers/pallas_call | solution.py:436
  6.0 0.0 collective-permute-done.2.other_state
  6.0 0.6 %state.1 = (f32[4,8,128]{2,1,0:T(8,128)S(1)}, f32[4,2,8,128]{3,2,1,0:T(8,128)S(1)}, f32[2,8,128]{2,1,0:T(8,128)S(1)}, f32[8,128]{1,0:T(8,128)S(1)}, f32[8,128]{1...) custom-call(f32[14,8,128]{2,1,0:T(8,128)S(1)} %get-tuple-element.29., ...), custom_call_target="tpu_custom_call" | custom-call | tf_op jit(solution)/shard_map/state/pallas_call | solution.py:447
  6.7 1.2 %collective-permute-done.1.upper_other = f32[8,128]{1,0:T(8,128)S(1)} collective-permute-done((f32[8,128]{1,0:T(8,128)S(1)}, f32[8,128]{1,0:T(8,128)S(1)}, u32[]{:S(2)}, u32[]{:S(2)}) %collective-permute-start.1) | collective-permute-done | bytes 4128 | tf_op jit(solution)/shard_map/ppermute | solution.py:427
  7.9 0.0 collective-permute-done.upper
  7.9 0.9 %edges.1.after = f32[8,128]{1,0:T(8,128)S(1)} custom-call(f32[7,8,128]{2,1,0:T(8,128)S(1)} %collective-permute-done.upper, f32[8,128]{1,0:T(8,128)S(1)} %collective-permute-done.1.upper_other, bf16[1792,256]{1,0:T(8,128)(2,1)S(1)} %get-tuple-element.28.left, f32[8,8,128]{2,1,0:T(8,128)S(1)} %get-tuple-element.30.layers, ...), custom_call_target="tpu_custom_call" | custom-call | tf_op jit(solution)/shard_map/edges/pallas_call | solution.py:453
  8.7 0.6 %radiate.1.own_heat.heat = f32[4,8,128]{2,1,0:T(8,128)S(1)} custom-call(bf16[1792,256]{1,0:T(8,128)(2,1)S(1)} %get-tuple-element.28.left, f32[4,1792,128]{2,1,0:T(8,128)S(1)} %get-tuple-element.37.drops, f32[7,8,128]{2,1,0:T(8,128)S(1)} %collective-permute-done.upper, f32[8,128]{1,0:T(8,128)S(1)} %get-tuple-element.25.zenith, ...), custom_call_target="tpu_custom_call" | custom-call | tf_op jit(solution)/shard_map/radiate/pallas_call | solution.py:459
  9.3 0.2 %collective-permute-start.5 = (f32[4,8,128]{2,1,0:T(8,128)S(1)}, f32[4,8,128]{2,1,0:T(8,128)S(1)}, u32[]{:S(2)}, u32[]{:S(2)}) collective-permute-start(f32[4,8,128]{2,1,0:T(8,128)S(1)} %radiate.1.own_heat.heat), channel_id=1, source_target_pairs={{0,1},{1,0},{2,3},{3,2},{4,5},{5,4},{6,7},{7,6},{8,9},{9,8},{10,11... | collective-permute-start | bytes 49160 | tf_op jit(solution)/shard_map/ppermute | solution.py:394
  9.6 1.6 %collective-permute-start.3 = (f32[8,128]{1,0:T(8,128)S(1)}, f32[8,128]{1,0:T(8,128)S(1)}, u32[]{:S(2)}, u32[]{:S(2)}) collective-permute-start(f32[8,128]{1,0:T(8,128)S(1)} %edges.1.after), channel_id=1, source_target_pairs={{0,4},{4,8},{8,12},{12,0},{1,5},{5,9},{9,13},{13,1},{2,6},{6,10},{... | collective-permute-start | bytes 12296 | tf_op jit(solution)/shard_map/ppermute | solution.py:457
  11.1 2.2 %collective-permute-start.4 = (f32[8,128]{1,0:T(8,128)S(1)}, f32[8,128]{1,0:T(8,128)S(1)}, u32[]{:S(2)}, u32[]{:S(2)}) collective-permute-start(f32[8,128]{1,0:T(8,128)S(1)} %edges.1.after), channel_id=1, source_target_pairs={{4,0},{8,4},{12,8},{0,12},{5,1},{9,5},{13,9},{1,13},{6,2},{10,6},{... | collective-permute-start | bytes 12296 | tf_op jit(solution)/shard_map/ppermute | solution.py:458
  13.4 0.0 collective-permute-done.5.other_heat
  13.4 0.3 %base.1 = f32[4,8,128]{2,1,0:T(8,128)S(1)} custom-call(f32[14,8,128]{2,1,0:T(8,128)S(1)} %get-tuple-element.29.own_state, f32[14,8,128]{2,1,0:T(8,128)S(1)} %collective-permute-done.2.other_state, f32[4,8,128]{2,1,0:T(8,128)S(1)} %radiate.1.own_heat.heat, f32[4,8,128]{2,1,0:T(8,128)S(1)} %collective-permute-done.5.other_heat, ...), custom_call_target="tpu_custom_call" | custom-call | tf_op jit(solution)/shard_map/base/pallas_call | solution.py:463
  13.7 1.3 %collective-permute-done.3.from_before = f32[8,128]{1,0:T(8,128)S(1)} collective-permute-done((f32[8,128]{1,0:T(8,128)S(1)}, f32[8,128]{1,0:T(8,128)S(1)}, u32[]{:S(2)}, u32[]{:S(2)}) %collective-permute-start.3) | collective-permute-done | bytes 4128 | tf_op jit(solution)/shard_map/ppermute | solution.py:457
  15.0 0.0 collective-permute-done.4.from_after
  15.0 0.9 %step.1 = (f32[4,8,128]{2,1,0:T(8,128)}, f32[4,8,128]{2,1,0:T(8,128)}) custom-call(f32[8,128]{1,0:T(8,128)S(1)} %collective-permute-done.3.from_before, f32[8,128]{1,0:T(8,128)S(1)} %collective-permute-done.4.from_after, f32[2,8,128]{2,1,0:T(8,128)S(1)} %get-tuple-element.35.span, f32[8,128]{1,0:T(8,128)S(1)} %get-tuple-element.33.kappa, ...), custom_call_target="tpu_custom_call" | custom-call | tf_op jit(solution)/shard_map/step/pallas_call | solution.py:466
Async XLA Ops:
  1.7 4.3 %collective-permute-start.2 = (f32[14,8,128]{2,1,0:T(8,128)S(1)}, f32[14,8,128]{2,1,0:T(8,128)S(1)}, u32[]{:S(2)}, u32[]{:S(2)}) collective-permute-start(f32[14,8,128]{2,1,0:T(8,128)S(1)} %get-tuple-element.29.own_state), channel_id=1, source_target_pairs={{0,1},{1,0},{2,3},{3,2},{4,5},{5,4},{6,7},{7,6},{8,9},{9,8},{10,11... | collective-permute-start | bytes 172040 | tf_op jit(solution)/shard_map/ppermute | solution.py:394
  2.3 5.6 %collective-permute-start = (f32[7,8,128]{2,1,0:T(8,128)S(1)}, f32[7,8,128]{2,1,0:T(8,128)S(1)}, u32[]{:S(2)}, u32[]{:S(2)}) collective-permute-start(f32[7,8,128]{2,1,0:T(8,128)S(1)} %get-tuple-element.22), channel_id=1, source_target_pairs={{0,2},{2,0},{1,3},{3,1},{4,6},{6,4},{5,7},{7,5},{8,10},{10,8},{9,1... | collective-permute-start | bytes 86024 | tf_op jit(solution)/shard_map/ppermute | solution.py:426
  4.8 3.0 %collective-permute-start.1 = (f32[8,128]{1,0:T(8,128)S(1)}, f32[8,128]{1,0:T(8,128)S(1)}, u32[]{:S(2)}, u32[]{:S(2)}) collective-permute-start(f32[8,128]{1,0:T(8,128)S(1)} %get-tuple-element.23), channel_id=1, source_target_pairs={{0,3},{1,2},{2,1},{3,0},{4,7},{5,6},{6,5},{7,4},{8,11},{9,10},{10,... | collective-permute-start | bytes 12296 | tf_op jit(solution)/shard_map/ppermute | solution.py:427
  9.3 4.1 %collective-permute-start.5 = (f32[4,8,128]{2,1,0:T(8,128)S(1)}, f32[4,8,128]{2,1,0:T(8,128)S(1)}, u32[]{:S(2)}, u32[]{:S(2)}) collective-permute-start(f32[4,8,128]{2,1,0:T(8,128)S(1)} %radiate.1.own_heat.heat), channel_id=1, source_target_pairs={{0,1},{1,0},{2,3},{3,2},{4,5},{5,4},{6,7},{7,6},{8,9},{9,8},{10,11... | collective-permute-start | bytes 49160 | tf_op jit(solution)/shard_map/ppermute | solution.py:394
  9.6 5.4 %collective-permute-start.3 = (f32[8,128]{1,0:T(8,128)S(1)}, f32[8,128]{1,0:T(8,128)S(1)}, u32[]{:S(2)}, u32[]{:S(2)}) collective-permute-start(f32[8,128]{1,0:T(8,128)S(1)} %edges.1.after), channel_id=1, source_target_pairs={{0,4},{4,8},{8,12},{12,0},{1,5},{5,9},{9,13},{13,1},{2,6},{6,10},{... | collective-permute-start | bytes 12296 | tf_op jit(solution)/shard_map/ppermute | solution.py:457
  11.1 3.8 %collective-permute-start.4 = (f32[8,128]{1,0:T(8,128)S(1)}, f32[8,128]{1,0:T(8,128)S(1)}, u32[]{:S(2)}, u32[]{:S(2)}) collective-permute-start(f32[8,128]{1,0:T(8,128)S(1)} %edges.1.after), channel_id=1, source_target_pairs={{4,0},{8,4},{12,8},{0,12},{5,1},{9,5},{13,9},{1,13},{6,2},{10,6},{... | collective-permute-start | bytes 12296 | tf_op jit(solution)/shard_map/ppermute | solution.py:458

commit v7 on v5

--- a/solution.py
+++ b/solution.py
@@ -128,8 +128,12 @@
     air, diffusivity, absorber, thickness, zenith, lit, coef, weight = refs[:8]
     amount, state, absorber_out, thickness_out, zenith_out, lit_out, coef_out, weight_out, sems = refs[8:]
     levels = air.shape[0]
+    species = absorber.shape[0]
+    layers = [
+        pltpu.make_async_copy(absorber.at[s], absorber_out.at[s], sems.at[8 + s])
+        for s in range(species)
+    ]
     copies = [
-        pltpu.make_async_copy(absorber, absorber_out, sems.at[0]),
         pltpu.make_async_copy(air, state.at[pl.ds(0, levels)], sems.at[1]),
         pltpu.make_async_copy(diffusivity, state.at[levels], sems.at[2]),
         pltpu.make_async_copy(zenith, zenith_out, sems.at[3]),
@@ -138,15 +142,16 @@
         pltpu.make_async_copy(thickness, thickness_out, sems.at[6]),
         pltpu.make_async_copy(lit, lit_out, sems.at[7]),
     ]
-    for copy in copies:
+    for copy in layers + copies:
         copy.start()
-    for copy in copies:
-        copy.wait()
-    for s in range(absorber_out.shape[0]):
+    for s in range(species):
+        layers[s].wait()
         total = absorber_out[s, 0]
         for k in range(1, levels):
             total = total + absorber_out[s, k]
         amount[s] = total
+    for copy in copies:
+        copy.wait()
 
 
 def amount_rows(totals, scale, depth, ones):
@@ -357,7 +362,7 @@
         fetch_kernel,
         out_shape=(tile(absorber.shape[0]), tile(levels + 1)) + tuple(same(x) for x in args[2:]),
         in_specs=[pl.BlockSpec(memory_space=pltpu.HBM)] * len(args),
-        scratch_shapes=[pltpu.SemaphoreType.DMA((len(args),))],
+        scratch_shapes=[pltpu.SemaphoreType.DMA((len(args) + absorber.shape[0],))],
         compiler_params=pltpu.CompilerParams(vmem_limit_bytes=32 * 1024 * 1024),
         name="fetch",
     )(*args)

time: 15.4 us -> 15.5 us (level)
  no operation moved by 1% of the time
where the time goes in v7:
time: 15.5 us; the launch traced here: 15.3 us
  starting transfers between devices  7.26 us (47%)
  Pallas kernels  5.32 us (34%)
  waiting for transfers between devices  2.01 us (13%)
  between operations  0.68 us (4%)
    ppermute x1, starting transfers between devices, shards(): lax.ppermute(amount, 'lev', [(i, (i + step) % size) for i in range(size)])  3 us
    ppermute x1, starting transfers between devices, shards(): lax.ppermute(edge, 'wide', [(i, (i + 1) % wide) for i in range(wide)])  2.11 us
    ppermute x1, starting transfers between devices, shards(): lax.ppermute(edge, 'wide', [((i + 1) % wide, i) for i in range(wide)])  2.07 us
    pallas_call x1, Pallas kernels, shards(): pl.pallas_call(layers_kernel, out_shape=(jax.ShapeDtypeStruct((terms * ro...  1.1 us
    pallas_call x1, Pallas kernels, shards(): pl.pallas_call(fetch_kernel, out_shape=(tile(absorber.shape[0]), tile(lev...  1.01 us
    pallas_call x1, Pallas kernels, shards(): pl.pallas_call(step_kernel, out_shape=tile(levels), compiler_params=big,...  0.86 us
    pallas_call x1, Pallas kernels, shards(): pl.pallas_call(base_kernel, out_shape=(tile(levels), tile(levels)), compi...  0.84 us
    ppermute x1, waiting for transfers between devices, shards(): lax.ppermute(amount, 'lev', [(i, (i + step) % size) for i in range(size)])  0.74 us
  transfers between devices with their start and end apart: 5, of which 3 were waited for; matrix products, arithmetic and copies ran while one was open for 0% of the time, Pallas kernels for 21%

profile of v7, /device:TPU:0, one launch (start us, length us, event | category | flops | bytes accessed | tf_op | source)
XLA Modules:
  0.0 15.3 jit_solution(17990026049637187611)
XLA Ops:
  0.6 1.0 %fetch.1 = (f32[7,8,128]{2,1,0:T(8,128)S(1)}, f32[5,8,128]{2,1,0:T(8,128)S(1)}, f32[7,4,8,128]{3,2,1,0:T(8,128)S(1)}, f32[4,8,128]{2,1,0:T(8,128)S(1)}, f32[8,12...) custom-call(f32[4,8,128]{2,1,0:T(8,128)} %refs_0_.1, f32[8,128]{1,0:T(8,128)} %refs_1_.1, ...), custom_call_target="tpu_custom_call" | custom-call | tf_op jit(solution)/shard_map/fetch/pallas_call | solution.py:361
  1.6 3.0 %collective-permute-start.1 = (f32[7,8,128]{2,1,0:T(8,128)S(1)}, f32[7,8,128]{2,1,0:T(8,128)S(1)}, u32[]{:S(2)}, u32[]{:S(2)}) collective-permute-start(f32[7,8,128]{2,1,0:T(8,128)S(1)} %get-tuple-element.28), channel_id=1, source_target_pairs={{0,2},{2,0},{1,3},{3,1},{4,6},{6,4},{5,7},{7,5},{8,10},{10,8},{9,1... | collective-permute-start | bytes 86024 | tf_op jit(solution)/shard_map/ppermute | solution.py:373
  4.7 0.0 collective-permute-start
  4.7 1.1 %layers.1 = (bf16[1792,256]{1,0:T(8,128)(2,1)S(1)}, f32[4,1792,128]{2,1,0:T(8,128)S(1)}) custom-call(f32[7,4,8,128]{3,2,1,0:T(8,128)S(1)} %get-tuple-element.22.absorber, f32[8,128]{1,0:T(8,128)S(1)} %get-tuple-element.23.zenith, f32[7,224]{1,0:T(8,128)S(1)} %get-tuple-element.24.coef, f32[1,224]{1,0:T(1,128)S(1)} %get-tuple-element.25.weight), custom_call_target="tpu_custom_call" | custom-call | tf_op jit(solution)/shard_map/layers/pallas_call | solution.py:381
  5.8 0.7 %collective-permute-done.1.upper = f32[7,8,128]{2,1,0:T(8,128)S(1)} collective-permute-done((f32[7,8,128]{2,1,0:T(8,128)S(1)}, f32[7,8,128]{2,1,0:T(8,128)S(1)}, u32[]{:S(2)}, u32[]{:S(2)}) %collective-permute-start.1) | collective-permute-done | bytes 28704 | tf_op jit(solution)/shard_map/ppermute | solution.py:373
  6.5 0.6 %radiate.1.own_heat = f32[4,8,128]{2,1,0:T(8,128)S(1)} custom-call(bf16[1792,256]{1,0:T(8,128)(2,1)S(1)} %get-tuple-element.26.left, f32[4,1792,128]{2,1,0:T(8,128)S(1)} %get-tuple-element.27.drops, f32[7,8,128]{2,1,0:T(8,128)S(1)} %collective-permute-done.1.upper, f32[8,128]{1,0:T(8,128)S(1)} %get-tuple-element.23.zenith, ...), custom_call_target="tpu_custom_call" | custom-call | tf_op jit(solution)/shard_map/radiate/pallas_call | solution.py:391
  7.1 0.1 collective-permute-start.2
  7.2 0.0 collective-permute-done.other_state
  7.2 0.6 %state.1 = (f32[4,8,128]{2,1,0:T(8,128)S(1)}, f32[4,2,8,128]{3,2,1,0:T(8,128)S(1)}, f32[2,8,128]{2,1,0:T(8,128)S(1)}, f32[8,128]{1,0:T(8,128)S(1)}, f32[8,128]{1...) custom-call(f32[5,8,128]{2,1,0:T(8,128)S(1)} %get-tuple-element.21.own_state, ...), custom_call_target="tpu_custom_call" | custom-call | tf_op jit(solution)/shard_map/state/pallas_call | solution.py:396
  7.8 0.5 %collective-permute-done.2.other_heat = f32[4,8,128]{2,1,0:T(8,128)S(1)} collective-permute-done((f32[4,8,128]{2,1,0:T(8,128)S(1)}, f32[4,8,128]{2,1,0:T(8,128)S(1)}, u32[]{:S(2)}, u32[]{:S(2)}) %collective-permute-start.2) | collective-permute-done | bytes 16416 | tf_op jit(solution)/shard_map/ppermute | solution.py:347
  8.3 0.3 %edges.1 = f32[8,128]{1,0:T(8,128)S(1)} custom-call(f32[4,8,128]{2,1,0:T(8,128)S(1)} %radiate.1.own_heat, f32[4,8,128]{2,1,0:T(8,128)S(1)} %collective-permute-done.2.other_heat, f32[8,128]{1,0:T(8,128)S(1)} %get-tuple-element.38.second, f32[8,128]{1,0:T(8,128)S(1)} %get-tuple-element.36.kappa, f32[8,128]{1,0:T(8,128)S(1)} %get-tuple-element.39.fixed), custom_call_target="tpu_custom_call" | custom-call | tf_op jit(solution)/shard_map/edges/pallas_call | solution.py:402
  8.6 2.1 %collective-permute-start.3 = (f32[8,128]{1,0:T(8,128)S(1)}, f32[8,128]{1,0:T(8,128)S(1)}, u32[]{:S(2)}, u32[]{:S(2)}) collective-permute-start(f32[8,128]{1,0:T(8,128)S(1)} %edges.1), channel_id=1, source_target_pairs={{0,4},{4,8},{8,12},{12,0},{1,5},{5,9},{9,13},{13,1},{2,6},{6,10},{... | collective-permute-start | bytes 12296 | tf_op jit(solution)/shard_map/ppermute | solution.py:406
  10.7 2.1 %collective-permute-start.4 = (f32[8,128]{1,0:T(8,128)S(1)}, f32[8,128]{1,0:T(8,128)S(1)}, u32[]{:S(2)}, u32[]{:S(2)}) collective-permute-start(f32[8,128]{1,0:T(8,128)S(1)} %edges.1), channel_id=1, source_target_pairs={{4,0},{8,4},{12,8},{0,12},{5,1},{9,5},{13,9},{1,13},{6,2},{10,6},{... | collective-permute-start | bytes 12296 | tf_op jit(solution)/shard_map/ppermute | solution.py:407
  12.8 0.8 %base.1 = (f32[4,8,128]{2,1,0:T(8,128)}, f32[4,8,128]{2,1,0:T(8,128)S(1)}) custom-call(f32[5,8,128]{2,1,0:T(8,128)S(1)} %get-tuple-element.21.own_state, f32[5,8,128]{2,1,0:T(8,128)S(1)} %collective-permute-done.other_state, f32[4,8,128]{2,1,0:T(8,128)S(1)} %radiate.1.own_heat, f32[4,8,128]{2,1,0:T(8,128)S(1)} %collective-permute-done.2.other_heat, ...), custom_call_target="tpu_custom_call" | custom-call | tf_op jit(solution)/shard_map/base/pallas_call | solution.py:408
  13.7 0.7 %collective-permute-done.3.from_before = f32[8,128]{1,0:T(8,128)S(1)} collective-permute-done((f32[8,128]{1,0:T(8,128)S(1)}, f32[8,128]{1,0:T(8,128)S(1)}, u32[]{:S(2)}, u32[]{:S(2)}) %collective-permute-start.3) | collective-permute-done | bytes 4128 | tf_op jit(solution)/shard_map/ppermute | solution.py:406
  14.4 0.0 collective-permute-done.4.from_after
  14.4 0.9 %step.1 = f32[4,8,128]{2,1,0:T(8,128)} custom-call(f32[4,8,128]{2,1,0:T(8,128)S(1)} %get-tuple-element.34.base, f32[2,8,128]{2,1,0:T(8,128)S(1)} %get-tuple-element.35.span, f32[8,128]{1,0:T(8,128)S(1)} %get-tuple-element.36.kappa, f32[2,8,128]{2,1,0:T(8,128)S(1)} %get-tuple-element.37.mine, f32[8,128]{1,0:T(8,128)S(1)} %collective-permute-done.3.from_before, ...), custom_call_target="tpu_custom_call" | custom-call | tf_op jit(solution)/shard_map/step/pallas_call | solution.py:411
Async XLA Ops:
  1.6 4.9 %collective-permute-start.1 = (f32[7,8,128]{2,1,0:T(8,128)S(1)}, f32[7,8,128]{2,1,0:T(8,128)S(1)}, u32[]{:S(2)}, u32[]{:S(2)}) collective-permute-start(f32[7,8,128]{2,1,0:T(8,128)S(1)} %get-tuple-element.28), channel_id=1, source_target_pairs={{0,2},{2,0},{1,3},{3,1},{4,6},{6,4},{5,7},{7,5},{8,10},{10,8},{9,1... | collective-permute-start | bytes 86024 | tf_op jit(solution)/shard_map/ppermute | solution.py:373
  4.7 2.5 %collective-permute-start = (f32[5,8,128]{2,1,0:T(8,128)S(1)}, f32[5,8,128]{2,1,0:T(8,128)S(1)}, u32[]{:S(2)}, u32[]{:S(2)}) collective-permute-start(f32[5,8,128]{2,1,0:T(8,128)S(1)} %get-tuple-element.21.own_state), channel_id=1, source_target_pairs={{0,1},{1,0},{2,3},{3,2},{4,5},{5,4},{6,7},{7,6},{8,9},{9,8},{10,11... | collective-permute-start | bytes 61448 | tf_op jit(solution)/shard_map/ppermute | solution.py:347
  7.1 1.2 %collective-permute-start.2 = (f32[4,8,128]{2,1,0:T(8,128)S(1)}, f32[4,8,128]{2,1,0:T(8,128)S(1)}, u32[]{:S(2)}, u32[]{:S(2)}) collective-permute-start(f32[4,8,128]{2,1,0:T(8,128)S(1)} %radiate.1.own_heat), channel_id=1, source_target_pairs={{0,1},{1,0},{2,3},{3,2},{4,5},{5,4},{6,7},{7,6},{8,9},{9,8},{10,11... | collective-permute-start | bytes 49160 | tf_op jit(solution)/shard_map/ppermute | solution.py:347
  8.6 5.8 %collective-permute-start.3 = (f32[8,128]{1,0:T(8,128)S(1)}, f32[8,128]{1,0:T(8,128)S(1)}, u32[]{:S(2)}, u32[]{:S(2)}) collective-permute-start(f32[8,128]{1,0:T(8,128)S(1)} %edges.1), channel_id=1, source_target_pairs={{0,4},{4,8},{8,12},{12,0},{1,5},{5,9},{9,13},{13,1},{2,6},{6,10},{... | collective-permute-start | bytes 12296 | tf_op jit(solution)/shard_map/ppermute | solution.py:406
  10.7 3.7 %collective-permute-start.4 = (f32[8,128]{1,0:T(8,128)S(1)}, f32[8,128]{1,0:T(8,128)S(1)}, u32[]{:S(2)}, u32[]{:S(2)}) collective-permute-start(f32[8,128]{1,0:T(8,128)S(1)} %edges.1), channel_id=1, source_target_pairs={{4,0},{8,4},{12,8},{0,12},{5,1},{9,5},{13,9},{1,13},{6,2},{10,6},{... | collective-permute-start | bytes 12296 | tf_op jit(solution)/shard_map/ppermute | solution.py:407

commit v8 on v5

--- a/solution.py
+++ b/solution.py
@@ -216,19 +216,16 @@
     lit_zenith = jnp.where(lit[...] == 1, zen, 0.0)
     factors = [lit_zenith / thickness[k] for k in range(levels)]
     chunk = 448
-    zero = jnp.zeros((rows, width), jnp.float32)
-    sums = [[zero, zero] for _ in range(levels)]
+    sums = [jnp.zeros((rows, width), jnp.float32) for _ in range(levels)]
     for start in range(0, left.shape[0], chunk):
         above = jnp.exp2(
             jnp.dot(left[pl.ds(start, chunk), :], right, preferred_element_type=jnp.float32)
         )
-        for n, at in enumerate(range(0, chunk, rows)):
-            part = above[at : at + rows]
-            for k in range(levels):
-                drop = drops[k, pl.ds(start + at, rows), :]
-                sums[k][n % 2] = sums[k][n % 2] + part * drop
+        for k in range(levels):
+            absorbed = above * drops[k, pl.ds(start, chunk), :]
+            sums[k] = sums[k] + jnp.sum(absorbed.reshape(chunk // rows, rows, width), axis=0)
     for k in range(levels):
-        heat[k] = factors[k] * (sums[k][0] + sums[k][1])
+        heat[k] = factors[k] * sums[k]
 
 
 def edge_kernel(own_heat, other_heat, second, kappa, fixed, edge):

time: 15.4 us -> 15.4 us (level)
  transfers between devices with their start and end apart: 5 -> 5, of which waited for: 3 -> 3; matrix products, arithmetic and copies ran while one was open for 0% -> 0% of each run, Pallas kernels for 21% -> 20%
where the time goes in v8:
time: 15.4 us; the launch traced here: 15.2 us
  starting transfers between devices  7.25 us (47%)
  Pallas kernels  5.26 us (34%)
  waiting for transfers between devices  2.01 us (13%)
  between operations  0.68 us (4%)
    ppermute x1, starting transfers between devices, shards(): lax.ppermute(amount, 'lev', [(i, (i + step) % size) for i in range(size)])  3 us
    ppermute x1, starting transfers between devices, shards(): lax.ppermute(edge, 'wide', [(i, (i + 1) % wide) for i in range(wide)])  2.1 us
    ppermute x1, starting transfers between devices, shards(): lax.ppermute(edge, 'wide', [((i + 1) % wide, i) for i in range(wide)])  2.07 us
    pallas_call x1, Pallas kernels, shards(): pl.pallas_call(layers_kernel, out_shape=(jax.ShapeDtypeStruct((terms * ro...  1.1 us
    pallas_call x1, Pallas kernels, shards(): pl.pallas_call(fetch_kernel, out_shape=(tile(absorber.shape[0]), tile(lev...  0.99 us
    pallas_call x1, Pallas kernels, shards(): pl.pallas_call(step_kernel, out_shape=tile(levels), compiler_params=big,...  0.86 us
    pallas_call x1, Pallas kernels, shards(): pl.pallas_call(base_kernel, out_shape=(tile(levels), tile(levels)), compi...  0.84 us
    ppermute x1, waiting for transfers between devices, shards(): lax.ppermute(amount, 'lev', [(i, (i + step) % size) for i in range(size)])  0.74 us
  transfers between devices with their start and end apart: 5, of which 3 were waited for; matrix products, arithmetic and copies ran while one was open for 0% of the time, Pallas kernels for 20%

profile of v8, /device:TPU:0, one launch (start us, length us, event | category | flops | bytes accessed | tf_op | source)
XLA Modules:
  0.0 15.2 jit_solution(8632311257450332916)
XLA Ops:
  0.6 1.0 %fetch.1 = (f32[7,8,128]{2,1,0:T(8,128)S(1)}, f32[5,8,128]{2,1,0:T(8,128)S(1)}, f32[7,4,8,128]{3,2,1,0:T(8,128)S(1)}, f32[4,8,128]{2,1,0:T(8,128)S(1)}, f32[8,12...) custom-call(f32[4,8,128]{2,1,0:T(8,128)} %refs_0_.1, f32[8,128]{1,0:T(8,128)} %refs_1_.1, ...), custom_call_target="tpu_custom_call" | custom-call | tf_op jit(solution)/shard_map/fetch/pallas_call | solution.py:353
  1.6 3.0 %collective-permute-start.1 = (f32[7,8,128]{2,1,0:T(8,128)S(1)}, f32[7,8,128]{2,1,0:T(8,128)S(1)}, u32[]{:S(2)}, u32[]{:S(2)}) collective-permute-start(f32[7,8,128]{2,1,0:T(8,128)S(1)} %get-tuple-element.28), channel_id=1, source_target_pairs={{0,2},{2,0},{1,3},{3,1},{4,6},{6,4},{5,7},{7,5},{8,10},{10,8},{9,1... | collective-permute-start | bytes 86024 | tf_op jit(solution)/shard_map/ppermute | solution.py:365
  4.6 0.0 collective-permute-start
  4.6 1.1 %layers.1 = (bf16[1792,256]{1,0:T(8,128)(2,1)S(1)}, f32[4,1792,128]{2,1,0:T(8,128)S(1)}) custom-call(f32[7,4,8,128]{3,2,1,0:T(8,128)S(1)} %get-tuple-element.22.absorber, f32[8,128]{1,0:T(8,128)S(1)} %get-tuple-element.23.zenith, f32[7,224]{1,0:T(8,128)S(1)} %get-tuple-element.24.coef, f32[1,224]{1,0:T(1,128)S(1)} %get-tuple-element.25.weight), custom_call_target="tpu_custom_call" | custom-call | tf_op jit(solution)/shard_map/layers/pallas_call | solution.py:373
  5.7 0.7 %collective-permute-done.1.upper = f32[7,8,128]{2,1,0:T(8,128)S(1)} collective-permute-done((f32[7,8,128]{2,1,0:T(8,128)S(1)}, f32[7,8,128]{2,1,0:T(8,128)S(1)}, u32[]{:S(2)}, u32[]{:S(2)}) %collective-permute-start.1) | collective-permute-done | bytes 28704 | tf_op jit(solution)/shard_map/ppermute | solution.py:365
  6.5 0.5 %radiate.1.own_heat = f32[4,8,128]{2,1,0:T(8,128)S(1)} custom-call(bf16[1792,256]{1,0:T(8,128)(2,1)S(1)} %get-tuple-element.26.left, f32[4,1792,128]{2,1,0:T(8,128)S(1)} %get-tuple-element.27.drops, f32[7,8,128]{2,1,0:T(8,128)S(1)} %collective-permute-done.1.upper, f32[8,128]{1,0:T(8,128)S(1)} %get-tuple-element.23.zenith, ...), custom_call_target="tpu_custom_call" | custom-call | tf_op jit(solution)/shard_map/radiate/pallas_call | solution.py:383
  7.0 0.1 collective-permute-start.2
  7.1 0.0 collective-permute-done.other_state
  7.1 0.6 %state.1 = (f32[4,8,128]{2,1,0:T(8,128)S(1)}, f32[4,2,8,128]{3,2,1,0:T(8,128)S(1)}, f32[2,8,128]{2,1,0:T(8,128)S(1)}, f32[8,128]{1,0:T(8,128)S(1)}, f32[8,128]{1...) custom-call(f32[5,8,128]{2,1,0:T(8,128)S(1)} %get-tuple-element.21.own_state, ...), custom_call_target="tpu_custom_call" | custom-call | tf_op jit(solution)/shard_map/state/pallas_call | solution.py:388
  7.8 0.5 %collective-permute-done.2.other_heat = f32[4,8,128]{2,1,0:T(8,128)S(1)} collective-permute-done((f32[4,8,128]{2,1,0:T(8,128)S(1)}, f32[4,8,128]{2,1,0:T(8,128)S(1)}, u32[]{:S(2)}, u32[]{:S(2)}) %collective-permute-start.2) | collective-permute-done | bytes 16416 | tf_op jit(solution)/shard_map/ppermute | solution.py:339
  8.3 0.3 %edges.1 = f32[8,128]{1,0:T(8,128)S(1)} custom-call(f32[4,8,128]{2,1,0:T(8,128)S(1)} %radiate.1.own_heat, f32[4,8,128]{2,1,0:T(8,128)S(1)} %collective-permute-done.2.other_heat, f32[8,128]{1,0:T(8,128)S(1)} %get-tuple-element.38.second, f32[8,128]{1,0:T(8,128)S(1)} %get-tuple-element.36.kappa, f32[8,128]{1,0:T(8,128)S(1)} %get-tuple-element.39.fixed), custom_call_target="tpu_custom_call" | custom-call | tf_op jit(solution)/shard_map/edges/pallas_call | solution.py:394
  8.6 2.1 %collective-permute-start.3 = (f32[8,128]{1,0:T(8,128)S(1)}, f32[8,128]{1,0:T(8,128)S(1)}, u32[]{:S(2)}, u32[]{:S(2)}) collective-permute-start(f32[8,128]{1,0:T(8,128)S(1)} %edges.1), channel_id=1, source_target_pairs={{0,4},{4,8},{8,12},{12,0},{1,5},{5,9},{9,13},{13,1},{2,6},{6,10},{... | collective-permute-start | bytes 12296 | tf_op jit(solution)/shard_map/ppermute | solution.py:398
  10.7 2.1 %collective-permute-start.4 = (f32[8,128]{1,0:T(8,128)S(1)}, f32[8,128]{1,0:T(8,128)S(1)}, u32[]{:S(2)}, u32[]{:S(2)}) collective-permute-start(f32[8,128]{1,0:T(8,128)S(1)} %edges.1), channel_id=1, source_target_pairs={{4,0},{8,4},{12,8},{0,12},{5,1},{9,5},{13,9},{1,13},{6,2},{10,6},{... | collective-permute-start | bytes 12296 | tf_op jit(solution)/shard_map/ppermute | solution.py:399
  12.8 0.8 %base.1 = (f32[4,8,128]{2,1,0:T(8,128)}, f32[4,8,128]{2,1,0:T(8,128)S(1)}) custom-call(f32[5,8,128]{2,1,0:T(8,128)S(1)} %get-tuple-element.21.own_state, f32[5,8,128]{2,1,0:T(8,128)S(1)} %collective-permute-done.other_state, f32[4,8,128]{2,1,0:T(8,128)S(1)} %radiate.1.own_heat, f32[4,8,128]{2,1,0:T(8,128)S(1)} %collective-permute-done.2.other_heat, ...), custom_call_target="tpu_custom_call" | custom-call | tf_op jit(solution)/shard_map/base/pallas_call | solution.py:400
  13.6 0.7 %collective-permute-done.3.from_before = f32[8,128]{1,0:T(8,128)S(1)} collective-permute-done((f32[8,128]{1,0:T(8,128)S(1)}, f32[8,128]{1,0:T(8,128)S(1)}, u32[]{:S(2)}, u32[]{:S(2)}) %collective-permute-start.3) | collective-permute-done | bytes 4128 | tf_op jit(solution)/shard_map/ppermute | solution.py:398
  14.3 0.0 collective-permute-done.4.from_after
  14.3 0.9 %step.1 = f32[4,8,128]{2,1,0:T(8,128)} custom-call(f32[4,8,128]{2,1,0:T(8,128)S(1)} %get-tuple-element.34.base, f32[2,8,128]{2,1,0:T(8,128)S(1)} %get-tuple-element.35.span, f32[8,128]{1,0:T(8,128)S(1)} %get-tuple-element.36.kappa, f32[2,8,128]{2,1,0:T(8,128)S(1)} %get-tuple-element.37.mine, f32[8,128]{1,0:T(8,128)S(1)} %collective-permute-done.3.from_before, ...), custom_call_target="tpu_custom_call" | custom-call | tf_op jit(solution)/shard_map/step/pallas_call | solution.py:403
Async XLA Ops:
  1.6 4.9 %collective-permute-start.1 = (f32[7,8,128]{2,1,0:T(8,128)S(1)}, f32[7,8,128]{2,1,0:T(8,128)S(1)}, u32[]{:S(2)}, u32[]{:S(2)}) collective-permute-start(f32[7,8,128]{2,1,0:T(8,128)S(1)} %get-tuple-element.28), channel_id=1, source_target_pairs={{0,2},{2,0},{1,3},{3,1},{4,6},{6,4},{5,7},{7,5},{8,10},{10,8},{9,1... | collective-permute-start | bytes 86024 | tf_op jit(solution)/shard_map/ppermute | solution.py:365
  4.6 2.5 %collective-permute-start = (f32[5,8,128]{2,1,0:T(8,128)S(1)}, f32[5,8,128]{2,1,0:T(8,128)S(1)}, u32[]{:S(2)}, u32[]{:S(2)}) collective-permute-start(f32[5,8,128]{2,1,0:T(8,128)S(1)} %get-tuple-element.21.own_state), channel_id=1, source_target_pairs={{0,1},{1,0},{2,3},{3,2},{4,5},{5,4},{6,7},{7,6},{8,9},{9,8},{10,11... | collective-permute-start | bytes 61448 | tf_op jit(solution)/shard_map/ppermute | solution.py:339
  7.0 1.2 %collective-permute-start.2 = (f32[4,8,128]{2,1,0:T(8,128)S(1)}, f32[4,8,128]{2,1,0:T(8,128)S(1)}, u32[]{:S(2)}, u32[]{:S(2)}) collective-permute-start(f32[4,8,128]{2,1,0:T(8,128)S(1)} %radiate.1.own_heat), channel_id=1, source_target_pairs={{0,1},{1,0},{2,3},{3,2},{4,5},{5,4},{6,7},{7,6},{8,9},{9,8},{10,11... | collective-permute-start | bytes 49160 | tf_op jit(solution)/shard_map/ppermute | solution.py:339
  8.6 5.8 %collective-permute-start.3 = (f32[8,128]{1,0:T(8,128)S(1)}, f32[8,128]{1,0:T(8,128)S(1)}, u32[]{:S(2)}, u32[]{:S(2)}) collective-permute-start(f32[8,128]{1,0:T(8,128)S(1)} %edges.1), channel_id=1, source_target_pairs={{0,4},{4,8},{8,12},{12,0},{1,5},{5,9},{9,13},{13,1},{2,6},{6,10},{... | collective-permute-start | bytes 12296 | tf_op jit(solution)/shard_map/ppermute | solution.py:398
  10.7 3.7 %collective-permute-start.4 = (f32[8,128]{1,0:T(8,128)S(1)}, f32[8,128]{1,0:T(8,128)S(1)}, u32[]{:S(2)}, u32[]{:S(2)}) collective-permute-start(f32[8,128]{1,0:T(8,128)S(1)} %edges.1), channel_id=1, source_target_pairs={{4,0},{8,4},{12,8},{0,12},{5,1},{9,5},{13,9},{1,13},{6,2},{10,6},{... | collective-permute-start | bytes 12296 | tf_op jit(solution)/shard_map/ppermute | solution.py:399
